TPU v7x, 128 devices: a whole 4x4x4 slice. The times are simulated.
128 devices in a mesh: ctx: 32 (over z_hi, y, x), ws: 4 (over z_lo, core).
Axes of the slice: x: 4, y: 4, z: 4 (z_hi: 2, z_lo: 2; z = z_hi * 2 + z_lo), core: 2. Of those that a mesh axis runs over, the one named last changes fastest.
Arguments:
- hidden_in: bfloat16 [8192, 2048], P('ctx'), may hold values from -6 to 6
- grad_out: bfloat16 [8192, 2048], P('ctx'), may hold values from -6 to 6
- block_ids: int32 [64], replicated, may hold values from 0 to 63, as said below
- expert_ids: int32 [8192, 6], P('ctx'), may hold values from 0 to 63, all different within a row
- claim_order: int32 [8192], P('ctx'), may hold values from 0 to 255, as said below
- attn_gain: bfloat16 [2048], P(('ctx', 'ws')), may hold values from 0.5 to 1.5
- latent_gain: bfloat16 [512], P(('ctx', 'ws')), may hold values from 0.5 to 1.5
- ffn_gain: bfloat16 [2048], P(('ctx', 'ws')), may hold values from 0.5 to 1.5
- query_weight: bfloat16 [2048, 3072], P('ctx', 'ws'), may hold values from -0.125 to 0.125
- latent_down: bfloat16 [2048, 576], P('ws', 'ctx'), may hold values from -0.125 to 0.125
- latent_up: bfloat16 [512, 4096], P('ctx', 'ws'), may hold values from -0.25 to 0.25
- output_weight: bfloat16 [2048, 2048], P('ws', 'ctx'), may hold values from -1.5 to 1.5
- router_weight: bfloat16 [2048, 64], P('ws', 'ctx'), may hold values from -0.0625 to 0.0625
- expert_gate: bfloat16 [64, 2048, 1408], P('ctx', None, 'ws'), may hold values from -0.125 to 0.125
- expert_up: bfloat16 [64, 2048, 1408], P('ctx', None, 'ws'), may hold values from -0.125 to 0.125
- expert_down: bfloat16 [64, 1408, 2048], P('ctx', 'ws'), may hold values from -6 to 6
- shared_gate: bfloat16 [2048, 2816], P('ctx', 'ws'), may hold values from -0.125 to 0.125
- shared_up: bfloat16 [2048, 2816], P('ctx', 'ws'), may hold values from -0.125 to 0.125
- shared_down: bfloat16 [2816, 2048], P('ws', 'ctx'), may hold values from -0.109375 to 0.109375
Outputs:
- layer_out: bfloat16 [8192, 2048], P('ctx', 'ws')
- grad_in: float32 [8192, 2048], P('ctx', 'ws')
- grad_attn_gain: float32 [2048], P(('ctx', 'ws'))
- grad_latent_gain: float32 [512], P(('ctx', 'ws'))
- grad_ffn_gain: float32 [2048], P(('ctx', 'ws'))
- grad_query: float32 [2048, 3072], P('ctx', 'ws')
- grad_latent_down: float32 [2048, 576], P('ws', 'ctx')
- grad_latent_up: float32 [512, 4096], P('ctx', 'ws')
- grad_output_weight: float32 [2048, 2048], P('ws', 'ctx')
- grad_router: float32 [2048, 64], P('ws', 'ctx')
- grad_expert_gate: float32 [64, 2048, 1408], P('ctx', None, 'ws')
- grad_expert_up: float32 [64, 2048, 1408], P('ctx', None, 'ws')
- grad_expert_down: float32 [64, 1408, 2048], P('ctx', 'ws')
- grad_shared_gate: float32 [2048, 2816], P('ctx', 'ws')
- grad_shared_up: float32 [2048, 2816], P('ctx', 'ws')
- grad_shared_down: float32 [2816, 2048], P('ws', 'ctx')
Inputs may be any that keep to these rules, and one draw needn't show every extreme that they name: Stored block j of the stream is global block block_ids[j] = s * 16 + b, block b of sequence s; every block appears once. Stored blocks 2i and 2i + 1 are blocks b and 15 - b of one sequence, in either order. `expert_ids`: each row names 6 different experts. `claim_order`: within the 256 rows of each index of ctx, a permutation of 0 to 255.
All inputs are finite; a program needn't handle non-finite values.
Results may differ from a plain program's by a relative error of at most 0.028.
Values may be sent and summed in bfloat16 or wider, within the bound.
No kernel may reach another device: no remote copies, remote signals or barrier semaphores. Data moves between devices by JAX's collectives and lax.ppermute only.
A program may use at most 320 MiB of HBM per device.

v0:
```python
import jax
import jax.numpy as jnp
from jax import lax
from jax.sharding import PartitionSpec as P

NOPE = 128
ROPE = 64
VDIM = 128
RANK = 512
TOPK = 6
EXP_DEV = 2
BLOCK = 128
LENGTH = 2048


EPSILON = 1e-06
ROPE_BASE = 10000.0
HIGHEST = lax.Precision.HIGHEST


def rotate(values, positions, direction):
    half_width = values.shape[-1] // 2
    frequency = ROPE_BASE ** (-2.0 * jnp.arange(half_width, dtype=jnp.float32) / values.shape[-1])
    angles = positions.astype(jnp.float32)[:, None] * frequency[None, :]
    target_shape = (angles.shape[0],) + (1,) * (values.ndim - 2) + (half_width,)
    cosine = jnp.cos(angles).reshape(target_shape)
    sine_part = direction * jnp.sin(angles).reshape(target_shape)
    first_half = values[..., :half_width]
    second_half = values[..., half_width:]
    return jnp.concatenate(
        [
            first_half * cosine - second_half * sine_part,
            second_half * cosine + first_half * sine_part,
        ],
        axis=-1,
    )


def silu_slope(pre_act):
    sigmoid_val = jax.nn.sigmoid(pre_act)
    return sigmoid_val * (1.0 + pre_act * (1.0 - sigmoid_val))


def norm_back(upstream, source, inverse_root, gain_vec):
    scaled = upstream * gain_vec
    return inverse_root * scaled - source * inverse_root**3 * jnp.mean(
        scaled * source, axis=-1, keepdims=True
    )


def claim_slots(expert_ids, claim_order, experts, capacity):
    token_count = expert_ids.shape[0]
    picked_one = (expert_ids[:, :, None] == jnp.arange(experts)[None, None, :]).astype(jnp.float32)
    chosen = jnp.sum(picked_one, axis=1)
    ranking = (claim_order[None, :] == jnp.arange(token_count)[:, None]).astype(jnp.float32)
    ordered = jnp.dot(ranking, chosen, precision=HIGHEST)
    before = jnp.cumsum(ordered, axis=0) - ordered
    earlier = jnp.dot(ranking.T, before, precision=HIGHEST)
    slot_index = jnp.sum(picked_one * earlier[:, None, :], axis=2).astype(jnp.int32)
    kept_mask = slot_index < capacity
    target = jnp.where(kept_mask, expert_ids * capacity + slot_index, experts * capacity)
    return (picked_one, kept_mask.astype(jnp.float32), target.reshape(-1))


def to_experts(buffer):
    return lax.all_to_all(buffer, "ctx", split_axis=0, concat_axis=1, tiled=True)


def from_experts(buffer):
    return lax.all_to_all(buffer, "ctx", split_axis=1, concat_axis=0, tiled=True)


def hidden_sums(shared_part, routed_part):
    return (
        lax.psum_scatter(shared_part, "ws", scatter_dimension=1, tiled=True),
        lax.psum_scatter(routed_part, "ws", scatter_dimension=2, tiled=True),
    )


def ws_major(vector, ctx_count, ws_count):
    return vector.reshape(ctx_count, ws_count, -1).transpose(1, 0, 2).reshape(-1)


def owner_max(row_values, owner):
    first = jnp.max(jnp.where((owner == 0)[None, :, None], row_values, -1e30), axis=1)
    second = jnp.max(jnp.where((owner == 1)[None, :, None], row_values, -1e30), axis=1)
    return jnp.stack([first, second])


def owner_total(row_values, owner):
    first = jnp.sum(jnp.where((owner == 0)[None, :, None], row_values, 0.0), axis=1)
    second = jnp.sum(jnp.where((owner == 1)[None, :, None], row_values, 0.0), axis=1)
    return jnp.stack([first, second])


def owner_spread(per_owner, owner):
    return per_owner[owner].transpose(1, 0, 2)


def owner_rows(per_slot, owner):
    first = jnp.sum(jnp.where((owner == 0)[:, None, None, None], per_slot, 0.0), axis=0)
    second = jnp.sum(jnp.where((owner == 1)[:, None, None, None], per_slot, 0.0), axis=0)
    return jnp.concatenate([first, second], axis=0)


def on_device(
    hidden_in,
    grad_out,
    block_ids,
    expert_ids,
    claim_order,
    attn_gain,
    latent_gain,
    ffn_gain,
    query_weight,
    latent_down,
    latent_up,
    output_weight,
    router_weight,
    expert_gate,
    expert_up,
    expert_down,
    shared_gate,
    shared_up,
    shared_down,
):
    ctx_count = lax.axis_size("ctx")
    ws_count = lax.axis_size("ws")
    ctx_index = lax.axis_index("ctx")
    ws_index = lax.axis_index("ws")
    token_count, model_width = hidden_in.shape
    quarter = model_width // ws_count
    column_start = ws_index * quarter
    experts = EXP_DEV * ctx_count
    capacity = 5 * token_count * TOPK // (4 * experts)
    slot_total = experts * capacity
    down_ws, router_ws, gain_one_ws, gain_kv_ws, gain_two_ws = (
        lax.all_gather(latent_down, "ws", axis=0, tiled=True),
        lax.all_gather(router_weight, "ws", axis=0, tiled=True),
        lax.all_gather(attn_gain, "ws", axis=0, tiled=True),
        lax.all_gather(latent_gain, "ws", axis=0, tiled=True),
        lax.all_gather(ffn_gain, "ws", axis=0, tiled=True),
    )
    (
        query_full,
        up_full,
        output_full,
        shared_gate_full,
        shared_up_full,
        shared_down_full,
        down_full,
        router_full,
        gain_one_full,
        gain_kv_full,
        gain_two_full,
    ) = (
        lax.all_gather(query_weight, "ctx", axis=0, tiled=True),
        lax.all_gather(latent_up, "ctx", axis=0, tiled=True),
        lax.all_gather(output_weight, "ctx", axis=1, tiled=True),
        lax.all_gather(shared_gate, "ctx", axis=0, tiled=True),
        lax.all_gather(shared_up, "ctx", axis=0, tiled=True),
        lax.all_gather(shared_down, "ctx", axis=1, tiled=True),
        lax.all_gather(down_ws, "ctx", axis=1, tiled=True),
        lax.all_gather(router_ws, "ctx", axis=1, tiled=True),
        lax.all_gather(gain_one_ws, "ctx", axis=0, tiled=True),
        lax.all_gather(gain_kv_ws, "ctx", axis=0, tiled=True),
        lax.all_gather(gain_two_ws, "ctx", axis=0, tiled=True),
    )
    gain_one = gain_one_full.astype(jnp.float32)
    gain_kv = gain_kv_full.astype(jnp.float32)
    gain_two = gain_two_full.astype(jnp.float32)
    heads_local = query_full.shape[1] // (NOPE + ROPE)
    blocks_dev = token_count // BLOCK
    seq_blocks = LENGTH // BLOCK
    local_ids = lax.dynamic_slice_in_dim(block_ids, ctx_index * blocks_dev, blocks_dev)
    positions = ((local_ids % seq_blocks)[:, None] * BLOCK + jnp.arange(BLOCK)[None, :]).reshape(-1)
    inputs = hidden_in.astype(jnp.float32)
    root_one = lax.rsqrt(jnp.mean(inputs * inputs, axis=-1, keepdims=True) + EPSILON)
    normed_one = (inputs * root_one * gain_one).astype(jnp.bfloat16)
    query_all = jnp.dot(normed_one, query_full, preferred_element_type=jnp.float32).reshape(
        token_count, heads_local, NOPE + ROPE
    )
    query_nope = query_all[..., :NOPE].astype(jnp.bfloat16)
    query_rope = rotate(query_all[..., NOPE:], positions, 1.0).astype(jnp.bfloat16)
    compressed = jnp.dot(normed_one, down_full, preferred_element_type=jnp.float32)
    latent_pre = compressed[:, :RANK]
    root_kv = lax.rsqrt(jnp.mean(latent_pre * latent_pre, axis=-1, keepdims=True) + EPSILON)
    latent_norm = (latent_pre * root_kv * gain_kv).astype(jnp.bfloat16)
    key_rope = rotate(compressed[:, RANK:], positions, 1.0).astype(jnp.bfloat16)
    latent_local = jnp.concatenate([latent_norm, key_rope], axis=1)
    latent_all = lax.all_gather(latent_local, "ctx", axis=0, tiled=True)
    up_heads = up_full.reshape(RANK, heads_local, NOPE + VDIM)
    key_up = up_heads[..., :NOPE]
    value_up = up_heads[..., NOPE:]
    query_latent = jnp.einsum(
        "thn,rhn->thr", query_nope, key_up, preferred_element_type=jnp.float32
    ).astype(jnp.bfloat16)
    total_blocks = latent_all.shape[0] // BLOCK
    latent_blocks = latent_all.reshape(total_blocks, BLOCK, RANK + ROPE)
    pair_rows = 2 * BLOCK
    score_scale = (NOPE + ROPE) ** (-0.5)
    slot_range = jnp.arange(seq_blocks + 1)

    def pair_keys(pair_index):
        sequence = local_ids[2 * pair_index] // seq_blocks
        first_count = local_ids[2 * pair_index] % seq_blocks + 1
        owner = (slot_range >= first_count).astype(jnp.int32)
        key_place = jnp.where(owner == 0, slot_range, slot_range - first_count)
        wanted = sequence * seq_blocks + key_place
        matches = block_ids[None, :] == wanted[:, None]
        stream_index = jnp.sum(jnp.where(matches, jnp.arange(total_blocks)[None, :], 0), axis=1)
        key_rows = latent_blocks[stream_index]
        return (stream_index, key_rows, owner)

    def pair_pick(values, owner):
        return values.reshape((2, BLOCK) + values.shape[1:])[owner]

    def pair_scores(qlat_slots, qrope_slots, key_rows):
        raw_scores = jnp.einsum(
            "jqhr,jkr->hjqk", qlat_slots, key_rows[..., :RANK], preferred_element_type=jnp.float32
        )
        raw_scores = raw_scores + jnp.einsum(
            "jqhp,jkp->hjqk", qrope_slots, key_rows[..., RANK:], preferred_element_type=jnp.float32
        )
        return raw_scores * score_scale

    pair_index = 0
    stream_index, key_rows, owner = pair_keys(pair_index)
    qlat_slots = pair_pick(query_latent, owner)
    qrope_slots = pair_pick(query_rope, owner)
    scores = pair_scores(qlat_slots, qrope_slots, key_rows)
    top_owner = owner_max(jnp.max(scores, axis=-1), owner)
    weights = jnp.exp(scores - owner_spread(top_owner, owner)[..., None])
    total_owner = owner_total(jnp.sum(weights, axis=-1), owner)
    probabilities = (weights / owner_spread(total_owner, owner)[..., None]).astype(jnp.bfloat16)
    log_owner = top_owner + jnp.log(total_owner)
    log_parts = log_owner.transpose(1, 0, 2).reshape(heads_local, pair_rows)
    value_slots = jnp.einsum(
        "hjqk,jkr->jqhr", probabilities, key_rows[..., :RANK], preferred_element_type=jnp.float32
    )
    value_parts = owner_rows(value_slots, owner).astype(jnp.bfloat16)
    head_out = jnp.einsum(
        "thr,rhv->thv", value_parts, value_up, preferred_element_type=jnp.float32
    ).astype(jnp.bfloat16)
    head_flat = head_out.reshape(token_count, heads_local * VDIM)
    attn_part = jnp.dot(head_flat, output_full, preferred_element_type=jnp.float32)
    attn_total = lax.psum(attn_part, "ws")
    after_attn = inputs + attn_total
    root_two = lax.rsqrt(jnp.mean(after_attn * after_attn, axis=-1, keepdims=True) + EPSILON)
    normed_two = (after_attn * root_two * gain_two).astype(jnp.bfloat16)
    logits = jnp.dot(normed_two, router_full, preferred_element_type=jnp.float32)
    probs_router = jax.nn.softmax(logits, axis=-1)
    picked_one, kept_mask, target = claim_slots(expert_ids, claim_order, experts, capacity)
    gate_value = jnp.sum(probs_router[:, None, :] * picked_one, axis=2)
    combine = gate_value * kept_mask
    send_rows = (
        jnp.zeros((slot_total + 1, model_width), jnp.bfloat16)
        .at[target]
        .set(jnp.repeat(normed_two, TOPK, axis=0))
    )
    slots_in = to_experts(send_rows[:slot_total].reshape(experts, capacity, model_width))
    gate_sh = jnp.dot(normed_two, shared_gate_full, preferred_element_type=jnp.float32)
    up_sh = jnp.dot(normed_two, shared_up_full, preferred_element_type=jnp.float32)
    hidden_sh = (jax.nn.silu(gate_sh) * up_sh).astype(jnp.bfloat16)
    shared_part = jnp.dot(hidden_sh, shared_down_full, preferred_element_type=jnp.float32)
    gate_ex = jnp.einsum("esd,edf->esf", slots_in, expert_gate, preferred_element_type=jnp.float32)
    up_ex = jnp.einsum("esd,edf->esf", slots_in, expert_up, preferred_element_type=jnp.float32)
    hidden_ex = (jax.nn.silu(gate_ex) * up_ex).astype(jnp.bfloat16)
    routed_part = jnp.einsum(
        "esf,efd->esd", hidden_ex, expert_down, preferred_element_type=jnp.float32
    )
    shared_quarter, routed_quarter = hidden_sums(shared_part, routed_part)
    returned = from_experts(routed_quarter.astype(jnp.bfloat16)).reshape(slot_total, quarter)
    returned = jnp.concatenate([returned, jnp.zeros((1, quarter), jnp.bfloat16)], axis=0)
    picked_rows = returned[target].reshape(token_count, TOPK, quarter).astype(jnp.float32)
    routed_out = jnp.sum(combine[:, :, None] * picked_rows, axis=1)
    after_quarter = lax.dynamic_slice_in_dim(after_attn, column_start, quarter, 1)
    layer_out = (after_quarter + shared_quarter + routed_out).astype(jnp.bfloat16)
    upstream = grad_out.astype(jnp.float32)
    upstream_quarter = lax.dynamic_slice_in_dim(upstream, column_start, quarter, 1)
    grad_rows_send = (
        (combine[:, :, None] * upstream[:, None, :])
        .astype(jnp.bfloat16)
        .reshape(token_count * TOPK, model_width)
    )
    grad_send = (
        jnp.zeros((slot_total + 1, model_width), jnp.bfloat16).at[target].set(grad_rows_send)
    )
    grad_slots = to_experts(grad_send[:slot_total].reshape(experts, capacity, model_width))
    gate_part = jnp.sum(picked_rows * upstream_quarter[:, None, :], axis=2)
    grad_hidden_sh = jnp.dot(grad_out, shared_down_full.T, preferred_element_type=jnp.float32)
    grad_gate_sh = (grad_hidden_sh * up_sh * silu_slope(gate_sh)).astype(jnp.bfloat16)
    grad_up_sh = (grad_hidden_sh * jax.nn.silu(gate_sh)).astype(jnp.bfloat16)
    grad_shared_down = jnp.dot(hidden_sh.T, grad_out, preferred_element_type=jnp.float32)
    grad_shared_gate = jnp.dot(normed_two.T, grad_gate_sh, preferred_element_type=jnp.float32)
    grad_shared_up = jnp.dot(normed_two.T, grad_up_sh, preferred_element_type=jnp.float32)
    shared_in_part = jnp.dot(grad_gate_sh, shared_gate_full.T, preferred_element_type=jnp.float32)
    shared_in_part = shared_in_part + jnp.dot(
        grad_up_sh, shared_up_full.T, preferred_element_type=jnp.float32
    )
    grad_expert_down = jnp.einsum(
        "esf,esd->efd", hidden_ex, grad_slots, preferred_element_type=jnp.float32
    )
    grad_hidden_ex = jnp.einsum(
        "esd,efd->esf", grad_slots, expert_down, preferred_element_type=jnp.float32
    )
    grad_gate_ex = (grad_hidden_ex * up_ex * silu_slope(gate_ex)).astype(jnp.bfloat16)
    grad_up_ex = (grad_hidden_ex * jax.nn.silu(gate_ex)).astype(jnp.bfloat16)
    grad_expert_gate = jnp.einsum(
        "esd,esf->edf", slots_in, grad_gate_ex, preferred_element_type=jnp.float32
    )
    grad_expert_up = jnp.einsum(
        "esd,esf->edf", slots_in, grad_up_ex, preferred_element_type=jnp.float32
    )
    slot_in_part = jnp.einsum(
        "esf,edf->esd", grad_gate_ex, expert_gate, preferred_element_type=jnp.float32
    )
    slot_in_part = slot_in_part + jnp.einsum(
        "esf,edf->esd", grad_up_ex, expert_up, preferred_element_type=jnp.float32
    )
    shared_in_quarter, slot_in_quarter = hidden_sums(shared_in_part, slot_in_part)
    slot_back = from_experts(slot_in_quarter.astype(jnp.bfloat16)).reshape(slot_total, quarter)
    slot_back = jnp.concatenate([slot_back, jnp.zeros((1, quarter), jnp.bfloat16)], axis=0)
    routed_in_quarter = jnp.sum(
        slot_back[target].reshape(token_count, TOPK, quarter).astype(jnp.float32), axis=1
    )
    normed_quarter = shared_in_quarter + routed_in_quarter
    normed_gathered, gate_parts = (
        lax.all_gather(normed_quarter, "ws", axis=1, tiled=True),
        lax.all_gather(gate_part, "ws", axis=1, tiled=True),
    )
    gate_grad = jnp.sum(gate_parts.reshape(token_count, ws_count, TOPK), axis=1) * kept_mask
    prob_grad = jnp.sum(gate_grad[:, :, None] * picked_one, axis=1)
    logit_grad = (
        probs_router * (prob_grad - jnp.sum(probs_router * prob_grad, axis=-1, keepdims=True))
    ).astype(jnp.bfloat16)
    normed_two_grad = normed_gathered + jnp.dot(
        logit_grad, router_full.T, preferred_element_type=jnp.float32
    )
    router_grad_full = jnp.dot(normed_two.T, logit_grad, preferred_element_type=jnp.float32)
    router_quarter = lax.dynamic_slice_in_dim(router_grad_full, column_start, quarter, 0)
    after_grad = upstream + norm_back(normed_two_grad, after_attn, root_two, gain_two)
    gain_two_full_grad = jnp.sum(normed_two_grad * after_attn * root_two, axis=0)
    gain_two_pick = lax.dynamic_index_in_dim(
        gain_two_full_grad.reshape(ctx_count, ws_count, -1), ws_index, 1, keepdims=False
    ).reshape(-1)
    attn_grad = after_grad.astype(jnp.bfloat16)
    grad_output_part = jnp.dot(head_flat.T, attn_grad, preferred_element_type=jnp.float32)
    head_grad = (
        jnp.dot(attn_grad, output_full.T, preferred_element_type=jnp.float32)
        .astype(jnp.bfloat16)
        .reshape(token_count, heads_local, VDIM)
    )
    grad_value_up = jnp.einsum(
        "thr,thv->rhv", value_parts, head_grad, preferred_element_type=jnp.float32
    )
    latent_grad = jnp.einsum(
        "thv,rhv->thr", head_grad, value_up, preferred_element_type=jnp.float32
    ).astype(jnp.bfloat16)
    key_grads = jnp.zeros((total_blocks, BLOCK, RANK + ROPE), jnp.float32)
    pair_index = 0
    stream_index, key_rows, owner = pair_keys(pair_index)
    qlat_slots = pair_pick(query_latent, owner)
    qrope_slots = pair_pick(query_rope, owner)
    grad_slots_lat = pair_pick(latent_grad, owner)
    scores = pair_scores(qlat_slots, qrope_slots, key_rows)
    log_owner = log_parts.reshape(heads_local, 2, BLOCK).transpose(1, 0, 2)
    probs_pair = jnp.exp(scores - owner_spread(log_owner, owner)[..., None])
    prob_back = jnp.einsum(
        "jqhr,jkr->hjqk", grad_slots_lat, key_rows[..., :RANK], preferred_element_type=jnp.float32
    )
    inner_owner = owner_total(jnp.sum(probs_pair * prob_back, axis=-1), owner)
    score_grad = (probs_pair * (prob_back - owner_spread(inner_owner, owner)[..., None])).astype(
        jnp.bfloat16
    )
    qlat_slot_grad = jnp.einsum(
        "hjqk,jkr->jqhr", score_grad, key_rows[..., :RANK], preferred_element_type=jnp.float32
    )
    qrope_slot_grad = jnp.einsum(
        "hjqk,jkp->jqhp", score_grad, key_rows[..., RANK:], preferred_element_type=jnp.float32
    )
    qlat_parts = owner_rows(qlat_slot_grad, owner) * score_scale
    qrope_parts = owner_rows(qrope_slot_grad, owner) * score_scale
    nope_grad = (
        jnp.einsum("hjqk,jqhr->jkr", score_grad, qlat_slots, preferred_element_type=jnp.float32)
        * score_scale
    )
    nope_grad = nope_grad + jnp.einsum(
        "hjqk,jqhr->jkr",
        probs_pair.astype(jnp.bfloat16),
        grad_slots_lat,
        preferred_element_type=jnp.float32,
    )
    rope_grad = (
        jnp.einsum("hjqk,jqhp->jkp", score_grad, qrope_slots, preferred_element_type=jnp.float32)
        * score_scale
    )
    pair_grad = jnp.concatenate([nope_grad, rope_grad], axis=2)
    key_grads = key_grads.at[stream_index].add(pair_grad)
    latent_sum = lax.psum_scatter(
        key_grads.reshape(total_blocks * BLOCK, RANK + ROPE),
        ("ctx", "ws"),
        scatter_dimension=0,
        tiled=True,
    )
    qlat_grad = qlat_parts.astype(jnp.bfloat16)
    nope_query_grad = jnp.einsum(
        "thr,rhn->thn", qlat_grad, key_up, preferred_element_type=jnp.float32
    )
    grad_key_up = jnp.einsum(
        "thn,thr->rhn", query_nope, qlat_grad, preferred_element_type=jnp.float32
    )
    rope_query_grad = rotate(qrope_parts, positions, -1.0)
    query_grad = (
        jnp.concatenate([nope_query_grad, rope_query_grad], axis=-1)
        .astype(jnp.bfloat16)
        .reshape(token_count, heads_local * (NOPE + ROPE))
    )
    grad_query_part = jnp.dot(normed_one.T, query_grad, preferred_element_type=jnp.float32)
    normed_one_grad = jnp.dot(query_grad, query_full.T, preferred_element_type=jnp.float32)
    grad_up_part = jnp.concatenate([grad_key_up, grad_value_up], axis=-1).reshape(
        RANK, heads_local * (NOPE + VDIM)
    )
    sub_rows = token_count // ws_count
    sub_start = ws_index * sub_rows
    pre_rows = lax.dynamic_slice_in_dim(latent_pre, sub_start, sub_rows, 0)
    root_rows = lax.dynamic_slice_in_dim(root_kv, sub_start, sub_rows, 0)
    place_rows = lax.dynamic_slice_in_dim(positions, sub_start, sub_rows, 0)
    normed_rows = lax.dynamic_slice_in_dim(normed_one, sub_start, sub_rows, 0)
    latent_norm_grad = latent_sum[:, :RANK]
    latent_pre_grad = norm_back(latent_norm_grad, pre_rows, root_rows, gain_kv)
    gain_kv_part = jnp.sum(latent_norm_grad * pre_rows * root_rows, axis=0)
    rope_pre_grad = rotate(latent_sum[:, RANK:], place_rows, -1.0)
    compressed_grad = jnp.concatenate([latent_pre_grad, rope_pre_grad], axis=1).astype(jnp.bfloat16)
    grad_down_part = jnp.dot(normed_rows.T, compressed_grad, preferred_element_type=jnp.float32)
    rows_back = jnp.dot(compressed_grad, down_full.T, preferred_element_type=jnp.float32)
    current_rows = lax.dynamic_slice_in_dim(normed_one_grad, sub_start, sub_rows, 0)
    normed_one_grad = lax.dynamic_update_slice_in_dim(
        normed_one_grad, current_rows + rows_back, sub_start, 0
    )
    input_part = norm_back(normed_one_grad, inputs, root_one, gain_one)
    gain_one_part = jnp.sum(normed_one_grad * inputs * root_one, axis=0)
    input_quarter, down_quarter, gain_one_quarter, gain_kv_quarter = (
        lax.psum_scatter(input_part, "ws", scatter_dimension=1, tiled=True),
        lax.psum_scatter(grad_down_part, "ws", scatter_dimension=0, tiled=True),
        lax.psum_scatter(
            ws_major(gain_one_part, ctx_count, ws_count), "ws", scatter_dimension=0, tiled=True
        ),
        lax.psum_scatter(
            ws_major(gain_kv_part, ctx_count, ws_count), "ws", scatter_dimension=0, tiled=True
        ),
    )
    grad_in = lax.dynamic_slice_in_dim(after_grad, column_start, quarter, 1) + input_quarter
    (
        query_sum,
        down_sum,
        up_sum,
        output_sum,
        router_sum,
        shared_gate_sum,
        shared_up_sum,
        shared_down_sum,
        gain_one_sum,
        gain_kv_sum,
        gain_two_sum,
    ) = (
        lax.psum_scatter(grad_query_part, "ctx", scatter_dimension=0, tiled=True),
        lax.psum_scatter(down_quarter, "ctx", scatter_dimension=1, tiled=True),
        lax.psum_scatter(grad_up_part, "ctx", scatter_dimension=0, tiled=True),
        lax.psum_scatter(grad_output_part, "ctx", scatter_dimension=1, tiled=True),
        lax.psum_scatter(router_quarter, "ctx", scatter_dimension=1, tiled=True),
        lax.psum_scatter(grad_shared_gate, "ctx", scatter_dimension=0, tiled=True),
        lax.psum_scatter(grad_shared_up, "ctx", scatter_dimension=0, tiled=True),
        lax.psum_scatter(grad_shared_down, "ctx", scatter_dimension=1, tiled=True),
        lax.psum_scatter(gain_one_quarter, "ctx", scatter_dimension=0, tiled=True),
        lax.psum_scatter(gain_kv_quarter, "ctx", scatter_dimension=0, tiled=True),
        lax.psum_scatter(gain_two_pick, "ctx", scatter_dimension=0, tiled=True),
    )
    return (
        layer_out,
        grad_in,
        gain_one_sum,
        gain_kv_sum,
        gain_two_sum,
        query_sum,
        down_sum,
        up_sum,
        output_sum,
        router_sum,
        grad_expert_gate,
        grad_expert_up,
        grad_expert_down,
        shared_gate_sum,
        shared_up_sum,
        shared_down_sum,
    )


def solution(mesh):
    placed = (
        P("ctx", None),
        P("ctx", None),
        P(),
        P("ctx", None),
        P("ctx"),
        P(("ctx", "ws")),
        P(("ctx", "ws")),
        P(("ctx", "ws")),
        P("ctx", "ws"),
        P("ws", "ctx"),
        P("ctx", "ws"),
        P("ws", "ctx"),
        P("ws", "ctx"),
        P("ctx", None, "ws"),
        P("ctx", None, "ws"),
        P("ctx", "ws", None),
        P("ctx", "ws"),
        P("ctx", "ws"),
        P("ws", "ctx"),
    )
    return jax.shard_map(
        on_device,
        mesh=mesh,
        in_specs=placed,
        out_specs=(
            P("ctx", "ws"),
            P("ctx", "ws"),
            P(("ctx", "ws")),
            P(("ctx", "ws")),
            P(("ctx", "ws")),
            P("ctx", "ws"),
            P("ws", "ctx"),
            P("ctx", "ws"),
            P("ws", "ctx"),
            P("ws", "ctx"),
            P("ctx", None, "ws"),
            P("ctx", None, "ws"),
            P("ctx", "ws", None),
            P("ctx", "ws"),
            P("ctx", "ws"),
            P("ws", "ctx"),
        ),
        check_vma=False,
    )
```

profile of v0, /device:TPU:0, one launch (start us, length us, event | category | flops | bytes accessed | tf_op | source)
XLA Modules:
  0.0 3928.5 jit_solution(1947178227556078948)
XLA Ops:
  29.9 99.8 %all-reduce.18 = (bf16[2048]{0:T(1024)(128)(2,1)S(1)}, bf16[512]{0:T(512)(128)(2,1)S(1)}, bf16[2048]{0:T(1024)(128)(2,1)S(1)}) all-reduce(bf16[2048]{0:T(1024)(128)(2,1)S(1)} %dynamic-update-slice.1, bf16[512]{0:T(512)(128)(2,1)S(1)} %dynamic-update-slice.3, ...), channel_id=1, replica_groups=mesh['ctx'=32,'ws'=4] {'ctx'}, use_global_device_ids=true, to_apply=%add.3 | all-reduce | flops 4608 | bytes 18432
  146.7 14.8 all-gather.17.cloned.1.call-done
  163.7 74.9 %all-gather.15.cloned.1.call-done = bf16[2048,768]{1,0:T(8,128)(2,1)} async-done(((bf16[64,768]{1,0:T(8,128)(2,1)}), bf16[2048,768]{1,0:T(8,128)(2,1)}) %all-gather.15.cloned.1.call-update) | async-done | bytes 3145744 | tf_op jit(solution)/shard_map/all_gather | solution.py:157
  251.9 128.9 %all-gather.13.cloned.1.call-done = bf16[8192,576]{0,1:T(8,128)(2,1)} async-done(((bf16[256,576]{0,1:T(8,128)(2,1)}), bf16[8192,576]{0,1:T(8,128)(2,1)}) %all-gather.13.cloned.1.call-update) | async-done | bytes 9437200 | tf_op jit(solution)/shard_map/all_gather | solution.py:191
  428.4 24.3 all-gather.19.cloned.1.call-done
  464.1 92.0 %all-gather.1 = bf16[32,2,2048]{2,1,0:T(2,128)(2,1)S(1)} all-gather(bf16[1,2,2048]{2,1,0:T(2,128)(2,1)S(1)} %bitcast.323), channel_id=1, replica_groups=mesh['ctx'=32,'ws'=4] {'ctx'}, dimensions={0}, use_global_device_ids=true | all-gather | bytes 270336 | tf_op jit(solution)/shard_map/all_gather | solution.py:164
  580.5 15.0 scatter_custom_fusion
  627.7 15.7 mul.564
  643.7 15.9 scatter_custom_fusion.1
  677.0 46.6 %all-to-all-done = bf16[64,30,2048]{2,1,0:T(8,128)(2,1)} async-done(((bf16[64,30,2048]{2,1,0:T(8,128)(2,1)}), bf16[64,30,2048]{2,1,0:T(8,128)(2,1)}, u32[]{:S(2)}, u32[]{:S(2)}) %all-to-all-start) | async-done | bytes 7864352 | tf_op jit(solution)/shard_map/all_to_all | solution.py:66
  733.6 15.4 copy.332
  749.0 85.6 %all-to-all-done.2 = bf16[64,30,2048]{2,1,0:T(8,128)(2,1)} async-done(((bf16[64,30,2048]{2,1,0:T(8,128)(2,1)}), bf16[64,30,2048]{2,1,0:T(8,128)(2,1)}, u32[]{:S(2)}, u32[]{:S(2)}) %all-to-all-start.2) | async-done | bytes 7864352 | tf_op jit(solution)/shard_map/all_to_all | solution.py:66
  834.6 15.7 copy.334
  919.9 73.2 %all-gather.25.cloned.1.call-done = bf16[704,2048]{0,1:T(8,128)(2,1)} async-done(((bf16[704,64]{0,1:T(8,128)(2,1)}), bf16[704,2048]{0,1:T(8,128)(2,1)}) %all-gather.25.cloned.1.call-update) | async-done | bytes 2883600 | tf_op jit(solution)/shard_map/all_gather | solution.py:162
  1011.9 119.0 %reduce-scatter.24.cloned.1.call-done = f32[2,960,512]{2,1,0:T(8,128)} async-done(((f32[2,960,2048]{2,1,0:T(8,128)}), f32[2,960,512]{2,1,0:T(8,128)}) %reduce-scatter.24.cloned.1.call-update) | async-done | bytes 3932176 | tf_op jit(solution)/shard_map/reduce_scatter | solution.py:76
  1146.2 27.9 all-to-all-done.3
  1195.5 130.7 %reduce-scatter.20.cloned.1.call-done = f32[2,960,512]{2,1,0:T(8,128)} async-done(((f32[2,960,2048]{2,1,0:T(8,128)}), f32[2,960,512]{2,1,0:T(8,128)}) %reduce-scatter.20.cloned.1.call-update) | async-done | bytes 3932176 | tf_op jit(solution)/shard_map/reduce_scatter | solution.py:76
  1345.0 24.7 all-to-all-done.1
  1460.1 14.0 scatter_fusion
  1474.1 20.5 copy.339
  1500.1 664.5 %reduce-scatter.42.cloned.1.call-done = f32[64,576]{1,0:T(8,128)} async-done(((f32[8192,576]{1,0:T(8,128)}), f32[64,576]{1,0:T(8,128)}) %reduce-scatter.42.cloned.1.call-update) | async-done | bytes 147472
  2231.2 15.1 fusion.1
  2246.2 15.0 fusion.9
  2271.7 98.8 %fusion = f32[512,24]{0,1:T(8,128)S(1)} fusion(f32[512,576]{0,1:T(8,128)} %reduce-scatter.30.cloned.1.call-done), kind=kCustom, calls=%all-reduce-scatter | all-reduce-scatter fusion | flops 393217 | bytes 1229312
  2374.4 194.9 %all-reduce.25.cloned.1.call-done = f32[512,64]{0,1:T(8,128)} async-done(((f32[512,64]{0,1:T(8,128)}), f32[512,64]{0,1:T(8,128)}) %all-reduce.25.cloned.1.call-update) | async-done | bytes 131088
  2581.6 94.9 %all-reduce.16 = (f32[512]{0:T(512)S(1)}, f32[128]{0:T(128)S(1)}, f32[512]{0:T(512)S(1)}) all-reduce(f32[512]{0:T(512)S(1)} %dynamic-slice.11, f32[128]{0:T(128)S(1)} %dynamic-slice.15, f32[512]{0:T(512)S(1)} %reshape.445), channel_id=9, replica_groups=mesh['ctx'=32,'ws'=4] {'ctx'}, use_global_device_ids=true, to_apply=%region_47.48.clone | all-reduce | flops 1152 | bytes 9216
  2701.0 138.5 %reduce-scatter.38.cloned.1.call-done = f32[64,704]{1,0:T(8,128)} async-done(((f32[2048,704]{1,0:T(8,128)}), f32[64,704]{1,0:T(8,128)}) %reduce-scatter.38.cloned.1.call-update) | async-done | bytes 180240 | tf_op jit(solution)/shard_map/reduce_scatter | solution.py:473
  2839.5 235.7 %reduce-scatter.36.cloned.1.call-done = f32[64,704]{1,0:T(8,128)} async-done(((f32[2048,704]{1,0:T(8,128)}), f32[64,704]{1,0:T(8,128)}) %reduce-scatter.36.cloned.1.call-update) | async-done | bytes 180240 | tf_op jit(solution)/shard_map/reduce_scatter | solution.py:472
  3075.2 235.9 %reduce-scatter.40.cloned.1.call-done = f32[704,64]{0,1:T(8,128)} async-done(((f32[704,2048]{0,1:T(8,128)}), f32[704,64]{0,1:T(8,128)}) %reduce-scatter.40.cloned.1.call-update) | async-done | bytes 180240 | tf_op jit(solution)/shard_map/reduce_scatter | solution.py:474
  3311.1 187.4 %reduce-scatter.32.cloned.1.call-done = f32[16,1024]{1,0:T(8,128)} async-done(((f32[512,1024]{1,0:T(8,128)}), f32[16,1024]{1,0:T(8,128)}) %reduce-scatter.32.cloned.1.call-update) | async-done | bytes 65552 | tf_op jit(solution)/shard_map/reduce_scatter | solution.py:469
  3498.5 190.3 %reduce-scatter.34.cloned.1.call-done = f32[512,64]{0,1:T(8,128)} async-done(((f32[512,2048]{0,1:T(8,128)}), f32[512,64]{0,1:T(8,128)}) %reduce-scatter.34.cloned.1.call-update) | async-done | bytes 131088 | tf_op jit(solution)/shard_map/reduce_scatter | solution.py:470
  3688.8 232.4 %reduce-scatter.28.cloned.1.call-done = f32[64,768]{1,0:T(8,128)} async-done(((f32[2048,768]{1,0:T(8,128)}), f32[64,768]{1,0:T(8,128)}) %reduce-scatter.28.cloned.1.call-update) | async-done | bytes 196624 | tf_op jit(solution)/shard_map/reduce_scatter | solution.py:467
  (484 shorter events, 547.2 us)
Async XLA Ops:
  7.2 128.6 %all-gather.29.cloned.1.call-start = ((), (), s32[]{:S(2)}) async-start(), calls=%async_computation.38 | async-start | bytes 3244032 | tf_op jit(solution)/shard_map/all_gather | solution.py:163
  14.8 146.7 %all-gather.17.cloned.1.call-start = ((), (), s32[]{:S(2)}) async-start(), calls=%async_computation.19 | async-start | bytes 1081344 | tf_op jit(solution)/shard_map/all_gather | solution.py:158
  15.5 223.1 %all-gather.15.cloned.1.call-start = ((), (), s32[]{:S(2)}) async-start(), calls=%async_computation.18 | async-start | bytes 3244032 | tf_op jit(solution)/shard_map/all_gather | solution.py:157
  16.3 364.5 %all-gather.13.cloned.1.call-start = ((), (), s32[]{:S(2)}) async-start(), calls=%async_computation.17 | async-start | bytes 9732096 | tf_op jit(solution)/shard_map/all_gather | solution.py:191
  145.6 307.2 %all-gather.19.cloned.1.call-start = ((), (), s32[]{:S(2)}) async-start(), calls=%async_computation.20 | async-start | bytes 2162688 | tf_op jit(solution)/shard_map/all_gather | solution.py:159
  146.2 411.1 %all-reduce.23.cloned.1.call-start = ((), (), s32[]{:S(2)}) async-start(), calls=%async_computation.21 | async-start | bytes 4194304 | tf_op jit(solution)/shard_map/psum | solution.py:247
  612.9 110.7 %all-to-all-start = ((bf16[64,30,2048]{2,1,0:T(8,128)(2,1)}), bf16[64,30,2048]{2,1,0:T(8,128)(2,1)}, u32[]{:S(2)}, u32[]{:S(2)}) async-start(bf16[64,30,2048]{2,1,0:T(8,128)(2,1)} %reshape.432), calls=%async_computation.1 | async-start | bytes 16777216 | tf_op jit(solution)/shard_map/all_to_all | solution.py:66
  617.8 281.4 %all-gather.23.cloned.1.call-start = ((), (), s32[]{:S(2)}) async-start(), calls=%async_computation.23 | async-start | bytes 3244032 | tf_op jit(solution)/shard_map/all_gather | solution.py:161
  723.6 111.0 %all-to-all-start.2 = ((bf16[64,30,2048]{2,1,0:T(8,128)(2,1)}), bf16[64,30,2048]{2,1,0:T(8,128)(2,1)}, u32[]{:S(2)}, u32[]{:S(2)}) async-start(bf16[64,30,2048]{2,1,0:T(8,128)(2,1)} %reshape.434), calls=%async_computation.5 | async-start | bytes 16777216 | tf_op jit(solution)/shard_map/all_to_all | solution.py:66
  732.0 183.4 %all-gather.21.cloned.1.call-start = ((), (), s32[]{:S(2)}) async-start(), calls=%async_computation.22 | async-start | bytes 3244032 | tf_op jit(solution)/shard_map/all_gather | solution.py:160
  732.8 260.3 %all-gather.25.cloned.1.call-start = ((), (), s32[]{:S(2)}) async-start(), calls=%async_computation.24 | async-start | bytes 3244032 | tf_op jit(solution)/shard_map/all_gather | solution.py:162
  733.5 397.3 %reduce-scatter.24.cloned.1.call-start = ((), (), s32[]{:S(2)}) async-start(), calls=%async_computation.28 | async-start | bytes 19660800 | tf_op jit(solution)/shard_map/reduce_scatter | solution.py:76
  899.0 294.6 %reduce-scatter.22.cloned.1.call-start = ((), (), s32[]{:S(2)}) async-start(), calls=%async_computation.27 | async-start | bytes 2621440 | tf_op jit(solution)/shard_map/reduce_scatter | solution.py:75
  1002.5 323.7 %reduce-scatter.20.cloned.1.call-start = ((), (), s32[]{:S(2)}) async-start(), calls=%async_computation.26 | async-start | bytes 19660800 | tf_op jit(solution)/shard_map/reduce_scatter | solution.py:76
  1136.5 37.6 all-to-all-start.3
  1146.0 248.7 %all-gather.27.cloned.1.call-start = ((), (), s32[]{:S(2)}) async-start(), calls=%async_computation.29 | async-start | bytes 2621440 | tf_op jit(solution)/shard_map/all_gather | solution.py:329
  1331.9 37.8 all-to-all-start.1
  1341.6 823.1 %reduce-scatter.42.cloned.1.call-start = ((), (), s32[]{:S(2)}) async-start(), calls=%async_computation.39 | async-start | bytes 21135360
  1494.6 774.9 %reduce-scatter.18.cloned.1.call-start = ((), (), s32[]{:S(2)}) async-start(), calls=%async_computation.25 | async-start | bytes 2621440 | tf_op jit(solution)/shard_map/reduce_scatter | solution.py:75
  1499.9 771.8 %reduce-scatter.30.cloned.1.call-start = ((), (), s32[]{:S(2)}) async-start(), calls=%async_computation.32 | async-start | bytes 5898240 | tf_op jit(solution)/shard_map/reduce_scatter | solution.py:445
  2171.5 397.9 %all-reduce.25.cloned.1.call-start = ((), (), s32[]{:S(2)}) async-start(), calls=%async_computation.40 | async-start | bytes 262144
  2173.7 518.6 %reduce-scatter.26.cloned.1.call-start = ((), (), s32[]{:S(2)}) async-start(), calls=%async_computation.30 | async-start | bytes 2621440 | tf_op jit(solution)/shard_map/reduce_scatter | solution.py:444
  2196.7 642.9 %reduce-scatter.38.cloned.1.call-start = ((), (), s32[]{:S(2)}) async-start(), calls=%async_computation.36 | async-start | bytes 6488064 | tf_op jit(solution)/shard_map/reduce_scatter | solution.py:473
  2201.4 873.8 %reduce-scatter.36.cloned.1.call-start = ((), (), s32[]{:S(2)}) async-start(), calls=%async_computation.35 | async-start | bytes 6488064 | tf_op jit(solution)/shard_map/reduce_scatter | solution.py:472
  2206.1 1105.0 %reduce-scatter.40.cloned.1.call-start = ((), (), s32[]{:S(2)}) async-start(), calls=%async_computation.37 | async-start | bytes 6488064 | tf_op jit(solution)/shard_map/reduce_scatter | solution.py:474
  2211.0 1287.5 %reduce-scatter.32.cloned.1.call-start = ((), (), s32[]{:S(2)}) async-start(), calls=%async_computation.33 | async-start | bytes 2162688 | tf_op jit(solution)/shard_map/reduce_scatter | solution.py:469
  2219.4 1469.4 %reduce-scatter.34.cloned.1.call-start = ((), (), s32[]{:S(2)}) async-start(), calls=%async_computation.34 | async-start | bytes 4325376 | tf_op jit(solution)/shard_map/reduce_scatter | solution.py:470
  2222.2 1699.1 %reduce-scatter.28.cloned.1.call-start = ((), (), s32[]{:S(2)}) async-start(), calls=%async_computation.31 | async-start | bytes 6488064 | tf_op jit(solution)/shard_map/reduce_scatter | solution.py:467
  2370.5 311.7 %collective-permute-start.6 = (f32[512,24]{0,1:T(8,128)S(1)}, f32[512,24]{0,1:T(8,128)S(1)}, u32[]{:S(2)}, u32[]{:S(2)}) collective-permute-start(f32[512,24]{0,1:T(8,128)S(1)} %fusion), channel_id=1, source_target_pairs={{0,28},{4,32},{8,36},{12,40},{16,44},{20,48},{24,52},{28,56},{32,6... | collective-permute-start | bytes 147464
  2371.8 313.0 %collective-permute-start.5 = (f32[512,24]{0,1:T(8,128)S(1)}, f32[512,24]{0,1:T(8,128)S(1)}, u32[]{:S(2)}, u32[]{:S(2)}) collective-permute-start(f32[512,24]{0,1:T(8,128)S(1)} %fusion), channel_id=1, source_target_pairs={{0,24},{4,28},{8,32},{12,36},{16,40},{20,44},{24,48},{28,52},{32,5... | collective-permute-start | bytes 147464
  2373.1 307.8 %collective-permute-start.7 = (f32[512,18]{0,1:T(8,128)S(1)}, f32[512,18]{0,1:T(8,128)S(1)}, u32[]{:S(2)}, u32[]{:S(2)}) collective-permute-start(f32[512,18]{0,1:T(8,128)S(1)} %slice.137), channel_id=1, source_target_pairs={{0,32},{4,36},{8,40},{12,44},{16,48},{20,52},{24,56},{28,60},{32,6... | collective-permute-start | bytes 110600
  2678.3 16.0 collective-permute-start.4
  (100 other events, 6190.3 us)
Sparse Core Ops, SparseCore 0:
  14.9 79.8 all-gather.28
  97.7 63.6 all-gather.16
  164.5 74.0 all-gather.14
  241.8 138.8 all-gather.12
  383.7 69.0 all-gather.18
  457.2 54.9 all-reduce.22
  622.2 212.3 all-gather.22
  838.1 77.3 all-gather.20
  919.0 74.0 all-gather.24
  995.5 135.2 reduce-scatter.23
  1134.0 50.3 reduce-scatter.21
  1186.7 139.5 reduce-scatter.19
  1327.9 51.0 all-gather.26
  1494.7 669.8 reduce-scatter.41
  2166.9 22.7 reduce-scatter.17
  2192.2 50.6 reduce-scatter.29
  2245.9 323.3 all-reduce.24
  2571.6 27.7 reduce-scatter.25
  2605.9 233.5 reduce-scatter.37
  2845.9 229.2 reduce-scatter.35
  3081.8 229.2 reduce-scatter.39
  3314.2 184.3 reduce-scatter.31
  3501.5 187.2 reduce-scatter.33
  3694.4 226.8 reduce-scatter.27
where the time goes:
time: 3940 us; the launch traced here: 3930 us
  waiting for transfers between devices  2850 us (72%)
  blocking collectives  420 us (11%)
  local copies, waits for them, and re-layouts  280 us (7%)
  matrix products  222 us (6%)
  other arithmetic  85.4 us (2%)
  starting transfers between devices  51.9 us (1%)
    unnamed x34, waiting for transfers between devices  864 us
    unnamed x5, blocking collectives  310 us
    reduce_scatter x2, waiting for transfers between devices, hidden_sums(): lax.psum_scatter(routed_part, 'ws', scatter_dimension=2, tiled=True)  250 us
    reduce_scatter x1, waiting for transfers between devices, on_device(): lax.psum_scatter(grad_shared_down, 'ctx', scatter_dimension=1, tiled=True)  236 us
    reduce_scatter x1, waiting for transfers between devices, on_device(): lax.psum_scatter(grad_shared_gate, 'ctx', scatter_dimension=0, tiled=True)  236 us
    reduce_scatter x1, waiting for transfers between devices, on_device(): lax.psum_scatter(grad_query_part, 'ctx', scatter_dimension=0, tiled=True)  232 us
    reduce_scatter x1, waiting for transfers between devices, on_device(): lax.psum_scatter(grad_output_part, 'ctx', scatter_dimension=1, tiled=True)  190 us
    reduce_scatter x1, waiting for transfers between devices, on_device(): lax.psum_scatter(grad_up_part, 'ctx', scatter_dimension=0, tiled=True)  187 us
  transfers between devices with their start and end apart: 36, of which 20 were waited for; matrix products, arithmetic and copies ran while one was open for 13% of the time, Pallas kernels for 0%

commit v1 on v0

v1 whole, which is shorter than its diff:
```python
import jax
import jax.numpy as jnp
from jax import lax
from jax.experimental import pallas as pl
from jax.experimental.pallas import tpu as pltpu
from jax.sharding import Mesh
from jax.sharding import PartitionSpec as P

WIDTH = 2048
NOPE = 128
ROPE = 64
VDIM = 128
RANK = 512
KEYS = RANK + ROPE
HEADS = 4
EXPERTS = 64
EXP_DEV = 2
CAP = 30
SLOTS = 32
BLOCK = 128
SEQ_BLOCKS = 16
SEQ_PAIRS = 8
TOK = 256
QUARTER = 512
HALF = 1024
FF_SH = 704
N_CTX = 32
CHUNK = 512
EPSILON = 1e-06
ROPE_BASE = 10000.0
SCALE = (NOPE + ROPE) ** (-0.5)
CTX = ("zh", "y", "x")
MIB = 1 << 20

bf16 = jnp.bfloat16
f32 = jnp.float32


def dot(a, b, contract):
    return lax.dot_general(a, b, ((contract[0], contract[1]), ((), ())), preferred_element_type=f32)


def nn(a, b):
    return dot(a, b, ((1,), (0,)))


def nt(a, b):
    return dot(a, b, ((1,), (1,)))


def tn(a, b):
    return dot(a, b, ((0,), (0,)))


def rotate(values, positions, direction):
    half_width = values.shape[-1] // 2
    frequency = ROPE_BASE ** (-2.0 * jnp.arange(half_width, dtype=f32) / values.shape[-1])
    angles = positions.astype(f32)[:, None] * frequency[None, :]
    target_shape = (angles.shape[0],) + (1,) * (values.ndim - 2) + (half_width,)
    cosine = jnp.cos(angles).reshape(target_shape)
    sine_part = direction * jnp.sin(angles).reshape(target_shape)
    first_half = values[..., :half_width]
    second_half = values[..., half_width:]
    return jnp.concatenate(
        [
            first_half * cosine - second_half * sine_part,
            second_half * cosine + first_half * sine_part,
        ],
        axis=-1,
    )


def silu_slope(pre_act):
    sigmoid_val = jax.nn.sigmoid(pre_act)
    return sigmoid_val * (1.0 + pre_act * (1.0 - sigmoid_val))


def norm_back(upstream, source, inverse_root, gain_vec):
    scaled = upstream * gain_vec
    return inverse_root * scaled - source * inverse_root**3 * jnp.mean(
        scaled * source, axis=-1, keepdims=True
    )


def shift(value, axis, size, step):
    return lax.ppermute(value, axis, [(i, (i + step) % size) for i in range(size)])


def swap(value, axis):
    return shift(value, axis, 2, 1)


def pick(value, index, dim):
    return lax.dynamic_index_in_dim(value, index, dim, keepdims=False)


def gather_two(value, axis, dim):
    other = swap(value, axis)
    first = lax.axis_index(axis) == 0
    return jnp.stack(
        [jnp.where(first, value, other), jnp.where(first, other, value)], axis=dim
    )


def gather_four(value, axis, dim):
    here = lax.axis_index(axis)
    pieces = [value] + [shift(value, axis, 4, k) for k in (1, 2, 3)]
    shape = value.shape[:dim] + (4,) + value.shape[dim:]
    result = jnp.zeros(shape, value.dtype)
    for k, piece in enumerate(pieces):
        result = lax.dynamic_update_slice_in_dim(
            result, jnp.expand_dims(piece, dim), (here - k) % 4, dim
        )
    return result


def gather_ctx(value, x_last):
    pair = gather_two(value, "zh", 0)
    if x_last:
        return gather_four(gather_four(pair, "y", 1), "x", 2).reshape((N_CTX,) + value.shape)
    return gather_four(gather_four(pair, "x", 1), "y", 1).reshape((N_CTX,) + value.shape)


def scatter_four(value, axis, dim, kind):
    here = lax.axis_index(axis)
    arrived = [
        shift(pick(value, (here + k) % 4, dim), axis, 4, k).astype(f32) for k in (1, 2, 3)
    ]
    return (pick(value, here, dim).astype(f32) + arrived[0] + arrived[1] + arrived[2]).astype(kind)


def scatter_ctx(value, x_first):
    grid = value.reshape((2, 4, 4) + value.shape[1:])
    if x_first:
        grid = scatter_four(scatter_four(grid, "x", 2, bf16), "y", 1, bf16)
    else:
        grid = scatter_four(scatter_four(grid, "y", 1, bf16), "x", 1, bf16)
    here = lax.axis_index("zh")
    arrived = swap(pick(grid, 1 - here, 0), "zh")
    return pick(grid, here, 0).astype(f32) + arrived.astype(f32)


def exchange_ctx(value):
    return lax.all_to_all(value, CTX, 0, 0, tiled=True)


def half_of(value, core, dim=1):
    return jnp.concatenate(
        [
            lax.dynamic_slice_in_dim(value, core * QUARTER, QUARTER, dim),
            lax.dynamic_slice_in_dim(value, HALF + core * QUARTER, QUARTER, dim),
        ],
        axis=dim,
    )


def whole_of(own, other, core):
    first = jnp.where(core == 0, own, other)
    second = jnp.where(core == 0, other, own)
    return jnp.concatenate(
        [first[:, :QUARTER], second[:, :QUARTER], first[:, QUARTER:], second[:, QUARTER:]], axis=1
    )


def core_half(partial, core):
    arrived = swap(half_of(partial, 1 - core).astype(bf16), "core")
    return half_of(partial, core) + arrived.astype(f32)


def zl_sum(half):
    mine = half.astype(bf16)
    return mine.astype(f32) + swap(mine, "zl").astype(f32)


def zl_quarter(half, zl):
    arrived = swap(
        lax.dynamic_slice_in_dim(half, (1 - zl) * QUARTER, QUARTER, 1).astype(bf16), "zl"
    )
    return lax.dynamic_slice_in_dim(half, zl * QUARTER, QUARTER, 1) + arrived.astype(f32)


def attend_kernel(place_ref, q_ref, k_ref, out_ref, log_ref, top_ref, sum_ref, acc_ref):
    owner, chunk = pl.program_id(0), pl.program_id(1)
    place = place_ref[owner]

    @pl.when(chunk == 0)
    def _():
        top_ref[...] = jnp.full(top_ref.shape, -1e30, f32)
        sum_ref[...] = jnp.zeros(sum_ref.shape, f32)
        acc_ref[...] = jnp.zeros(acc_ref.shape, f32)

    @pl.when(chunk * (CHUNK // BLOCK) <= place)
    def _():
        q = q_ref[...].reshape(HEADS * BLOCK, KEYS)
        k = k_ref[pl.ds(chunk * CHUNK, CHUNK), :]
        scores = nt(q, k) * SCALE
        column = lax.broadcasted_iota(jnp.int32, scores.shape, 1) + chunk * CHUNK
        scores = jnp.where(column < (place + 1) * BLOCK, scores, -1e30)
        top_old = top_ref[...][:, :1]
        top = jnp.maximum(top_old, jnp.max(scores, axis=1, keepdims=True))
        weights = jnp.exp(scores - top)
        fade = jnp.exp(top_old - top)
        total = sum_ref[...][:, :1] * fade + jnp.sum(weights, axis=1, keepdims=True)
        acc_ref[...] = acc_ref[...] * fade + nn(weights.astype(bf16), k[:, :RANK])
        top_ref[...] = jnp.broadcast_to(top, top_ref.shape)
        sum_ref[...] = jnp.broadcast_to(total, sum_ref.shape)

    @pl.when(chunk == pl.num_programs(1) - 1)
    def _():
        total = sum_ref[...][:, :1]
        out_ref[...] = (acc_ref[...] / total).reshape(out_ref.shape)
        log_ref[...] = (top_ref[...] + jnp.log(sum_ref[...])).reshape(log_ref.shape)


def attend(places, query, keys):
    rows = HEADS * BLOCK
    return pl.pallas_call(
        attend_kernel,
        grid_spec=pltpu.PrefetchScalarGridSpec(
            num_scalar_prefetch=1,
            grid=(2, SEQ_BLOCKS * BLOCK // CHUNK),
            in_specs=[
                pl.BlockSpec((HEADS, 1, BLOCK, KEYS), lambda o, c, p: (0, o, 0, 0)),
                pl.BlockSpec((SEQ_BLOCKS * BLOCK, KEYS), lambda o, c, p: (0, 0)),
            ],
            out_specs=[
                pl.BlockSpec((HEADS, 1, BLOCK, RANK), lambda o, c, p: (0, o, 0, 0)),
                pl.BlockSpec((HEADS, 1, BLOCK, BLOCK), lambda o, c, p: (0, o, 0, 0)),
            ],
            scratch_shapes=[
                pltpu.VMEM((rows, 128), f32),
                pltpu.VMEM((rows, 128), f32),
                pltpu.VMEM((rows, RANK), f32),
            ],
        ),
        out_shape=[
            jax.ShapeDtypeStruct((HEADS, 2, BLOCK, RANK), f32),
            jax.ShapeDtypeStruct((HEADS, 2, BLOCK, BLOCK), f32),
        ],
        compiler_params=pltpu.CompilerParams(vmem_limit_bytes=48 * MIB),
        cost_estimate=pl.CostEstimate(
            flops=2 * 2 * rows * 1280 * (KEYS + RANK), bytes_accessed=8 * MIB, transcendentals=0
        ),
        name="attend",
    )(places, query, keys)


def attend_back_kernel(
    place_ref, q_ref, k_ref, out_ref, log_ref, grad_ref, dq_ref, dk_ref, inner_ref
):
    owner, chunk = pl.program_id(0), pl.program_id(1)
    place = place_ref[owner]
    rows = HEADS * BLOCK

    @pl.when((owner == 0) & (chunk == 0))
    def _():
        dk_ref[...] = jnp.zeros(dk_ref.shape, f32)

    @pl.when(chunk == 0)
    def _():
        dq_ref[...] = jnp.zeros(dq_ref.shape, f32)
        inner = jnp.sum(
            grad_ref[...].reshape(rows, RANK).astype(f32) * out_ref[...].reshape(rows, RANK),
            axis=1,
            keepdims=True,
        )
        inner_ref[...] = jnp.broadcast_to(inner, inner_ref.shape)

    @pl.when(chunk * (CHUNK // BLOCK) <= place)
    def _():
        q = q_ref[...].reshape(rows, KEYS)
        grad = grad_ref[...].reshape(rows, RANK)
        part = pl.ds(chunk * CHUNK, CHUNK)
        k = k_ref[part, :]
        scores = nt(q, k) * SCALE
        column = lax.broadcasted_iota(jnp.int32, scores.shape, 1) + chunk * CHUNK
        log_total = log_ref[...].reshape(rows, BLOCK)[:, :1]
        probs = jnp.where(column < (place + 1) * BLOCK, jnp.exp(scores - log_total), 0.0)
        prob_back = nt(grad, k[:, :RANK])
        score_grad = (probs * (prob_back - inner_ref[...][:, :1])).astype(bf16)
        dq_ref[...] += (nn(score_grad, k) * SCALE).reshape(dq_ref.shape)
        dk_ref[part, :] += tn(score_grad, q) * SCALE
        dk_ref[part, :RANK] += tn(probs.astype(bf16), grad)


def attend_back(places, query, keys, value, log_total, grad):
    rows = HEADS * BLOCK

    def per_owner(width):
        return pl.BlockSpec((HEADS, 1, BLOCK, width), lambda o, c, p: (0, o, 0, 0))

    whole = pl.BlockSpec((SEQ_BLOCKS * BLOCK, KEYS), lambda o, c, p: (0, 0))
    return pl.pallas_call(
        attend_back_kernel,
        grid_spec=pltpu.PrefetchScalarGridSpec(
            num_scalar_prefetch=1,
            grid=(2, SEQ_BLOCKS * BLOCK // CHUNK),
            in_specs=[
                per_owner(KEYS),
                whole,
                per_owner(RANK),
                per_owner(BLOCK),
                per_owner(RANK),
            ],
            out_specs=[per_owner(KEYS), whole],
            scratch_shapes=[pltpu.VMEM((rows, 128), f32)],
        ),
        out_shape=[
            jax.ShapeDtypeStruct((HEADS, 2, BLOCK, KEYS), f32),
            jax.ShapeDtypeStruct((SEQ_BLOCKS * BLOCK, KEYS), f32),
        ],
        compiler_params=pltpu.CompilerParams(vmem_limit_bytes=48 * MIB),
        cost_estimate=pl.CostEstimate(
            flops=2 * 2 * rows * 1280 * 5 * KEYS, bytes_accessed=14 * MIB, transcendentals=0
        ),
        name="attend_back",
    )(places, query, keys, value, log_total, grad)


def on_device(
    hidden_in,
    grad_out,
    block_ids,
    expert_ids,
    claim_order,
    attn_gain,
    latent_gain,
    ffn_gain,
    query_weight,
    latent_down,
    latent_up,
    output_weight,
    router_weight,
    expert_gate,
    expert_up,
    expert_down,
    shared_gate,
    shared_up,
    shared_down,
):
    ctx = lax.axis_index(CTX)
    zl = lax.axis_index("zl")
    core = lax.axis_index("core")
    ws = zl * 2 + core
    column_start = ws * QUARTER

    gains = jnp.concatenate([attn_gain, latent_gain, ffn_gain])
    small = jnp.concatenate(
        [
            latent_down.T,
            router_weight.T,
            jnp.pad(gains, (0, QUARTER - gains.shape[0]))[None],
            jnp.zeros((3, QUARTER), bf16),
        ],
        axis=0,
    )
    small_all = gather_ctx(small, True)
    down_t = small_all[:, :18].reshape(KEYS, QUARTER)
    side = gather_two(gather_two(small_all[:, 18:21], "zl", 0), "core", 1).reshape(
        4, N_CTX, 3, QUARTER
    )
    router_t = side[:, :, :2].transpose(1, 2, 0, 3).reshape(EXPERTS, WIDTH)
    gain_one = side[:, :, 2, :16].transpose(1, 0, 2).reshape(-1).astype(f32)
    gain_kv = side[:, :, 2, 16:20].transpose(1, 0, 2).reshape(-1).astype(f32)
    gain_two = side[:, :, 2, 20:36].transpose(1, 0, 2).reshape(-1).astype(f32)

    up_mine = latent_up.reshape(16, HEADS, NOPE + VDIM).transpose(1, 0, 2).reshape(64, NOPE + VDIM)
    out_up = jnp.concatenate([output_weight.T, up_mine], axis=1)
    query_full = gather_ctx(query_weight, True).reshape(WIDTH, HEADS * (NOPE + ROPE))
    out_up_all = gather_ctx(out_up, False)
    output_t = out_up_all[..., :QUARTER].reshape(WIDTH, QUARTER)
    up_heads = (
        out_up_all[..., QUARTER:]
        .reshape(N_CTX, HEADS, 16, NOPE + VDIM)
        .transpose(1, 0, 2, 3)
        .reshape(HEADS, RANK, NOPE + VDIM)
    )
    key_up = up_heads[..., :NOPE]
    value_up = up_heads[..., NOPE:]

    local_ids = lax.dynamic_slice_in_dim(block_ids, ctx * 2, 2)
    places = local_ids % SEQ_BLOCKS
    sequence = local_ids[0] // SEQ_BLOCKS
    positions = (places[:, None] * BLOCK + jnp.arange(BLOCK)[None, :]).reshape(-1)
    pair_ids = block_ids.reshape(N_CTX, 2)
    in_seq = (pair_ids[:, 0] // SEQ_BLOCKS) == sequence
    rank = jnp.cumsum(in_seq.astype(jnp.int32)) - 1
    is_pair = in_seq[None, :] & (rank[None, :] == jnp.arange(SEQ_PAIRS)[:, None])
    pairs = jnp.sum(jnp.where(is_pair, jnp.arange(N_CTX)[None, :], 0), axis=1)
    pair_places = pair_ids[pairs] % SEQ_BLOCKS
    place_of = pair_places.T.reshape(-1)
    slot_of = jnp.sum(
        jnp.where(
            place_of[None, :] == jnp.arange(SEQ_BLOCKS)[:, None],
            jnp.arange(SEQ_BLOCKS)[None, :],
            0,
        ),
        axis=1,
    )

    inputs = hidden_in.astype(f32)
    root_one = lax.rsqrt(jnp.mean(inputs * inputs, axis=-1, keepdims=True) + EPSILON)
    normed_one = (inputs * root_one * gain_one).astype(bf16)
    normed_quarter = lax.dynamic_slice_in_dim(normed_one, column_start, QUARTER, 1)
    compressed_part = nt(normed_quarter, down_t).reshape(2, 2, 64, KEYS)
    compressed_half = pick(compressed_part, core, 1) + swap(
        pick(compressed_part, 1 - core, 1), "core"
    )
    compressed = pick(compressed_half, zl, 0) + swap(pick(compressed_half, 1 - zl, 0), "zl")
    row_start = ws * 64
    my_positions = lax.dynamic_slice_in_dim(positions, row_start, 64)
    latent_pre = compressed[:, :RANK]
    root_kv = lax.rsqrt(jnp.mean(latent_pre * latent_pre, axis=-1, keepdims=True) + EPSILON)
    latent_rows = jnp.concatenate(
        [
            (latent_pre * root_kv * gain_kv).astype(bf16),
            rotate(compressed[:, RANK:], my_positions, 1.0).astype(bf16),
        ],
        axis=1,
    )
    latent_ctx = gather_ctx(latent_rows, True)
    latent_mine = latent_ctx[pairs]
    latent_seq = gather_two(gather_two(latent_mine, "zl", 0), "core", 2).reshape(
        SEQ_BLOCKS, BLOCK, KEYS
    )
    keys = latent_seq[slot_of].reshape(SEQ_BLOCKS * BLOCK, KEYS)

    query_all = nn(normed_one, query_full).reshape(TOK, HEADS, NOPE + ROPE)
    query_nope = query_all[..., :NOPE].astype(bf16)
    query_rope = rotate(query_all[..., NOPE:], positions, 1.0).astype(bf16)
    query_latent = jnp.einsum(
        "thn,hrn->htr", query_nope, key_up, preferred_element_type=f32
    ).astype(bf16)
    query = jnp.concatenate([query_latent, query_rope.transpose(1, 0, 2)], axis=2)
    query = query.reshape(HEADS, 2, BLOCK, KEYS)
    value, log_total = attend(places, query, keys)
    value_parts = value.reshape(HEADS, TOK, RANK).astype(bf16)
    head_out = jnp.einsum("htr,hrv->thv", value_parts, value_up, preferred_element_type=f32)
    head_flat = head_out.astype(bf16).reshape(TOK, HEADS * VDIM)
    attn_part = nt(head_flat, output_t)
    attn_half = zl_sum(core_half(attn_part, core))
    after_half = half_of(inputs, core) + attn_half
    after_attn = whole_of(after_half, swap(after_half, "core"), core)
    root_two = lax.rsqrt(jnp.mean(after_attn * after_attn, axis=-1, keepdims=True) + EPSILON)
    normed_two = (after_attn * root_two * gain_two).astype(bf16)

    gate_up_mine, shared_down_mine, _ = lax.optimization_barrier(
        (jnp.concatenate([shared_gate, shared_up], axis=1), shared_down.T, keys)
    )
    gate_up = gather_ctx(gate_up_mine, True).reshape(WIDTH, 2 * FF_SH)
    shared_down_t = gather_ctx(shared_down_mine, False).reshape(WIDTH, FF_SH)

    chosen = jnp.sum(
        (expert_ids[:, :, None] == jnp.arange(EXPERTS)[None, None, :]).astype(f32), axis=1
    )
    before = (claim_order[None, :] < claim_order[:, None]).astype(bf16)
    earlier = nn(before, chosen.astype(bf16))
    slot_by = jnp.where(chosen > 0, earlier, float(CAP))
    slot_by = jnp.where(slot_by < CAP, slot_by, 99.0).T.reshape(N_CTX, EXP_DEV, TOK)
    slot_by = slot_by.transpose(1, 0, 2)
    places_hot = (
        slot_by[:, :, None, :] == jnp.arange(SLOTS, dtype=f32)[None, None, :, None]
    ).astype(bf16)
    flat_hot = places_hot.reshape(EXP_DEV, N_CTX * SLOTS, TOK)

    grad_half, _ = lax.optimization_barrier((half_of(grad_out, core), keys))
    grad_rows = []
    for e in range(EXP_DEV):
        sent = nn(flat_hot[e], grad_half).astype(bf16).reshape(N_CTX, SLOTS, HALF)
        own = exchange_ctx(sent).reshape(N_CTX * SLOTS, HALF)
        grad_rows.append(whole_of(own, swap(own, "core"), core))

    logits = nt(normed_two, router_t)
    probs_router = jax.nn.softmax(logits, axis=-1)
    probs_by = probs_router.T.reshape(N_CTX, EXP_DEV, TOK).transpose(1, 0, 2)
    gate_slots = jnp.sum(places_hot.astype(f32) * probs_by[:, :, None, :], axis=3)

    normed_half = half_of(normed_two, core)
    rows_in, gate_in = [], []
    for e in range(EXP_DEV):
        sent = nn(flat_hot[e], normed_half).astype(bf16).reshape(N_CTX, SLOTS, HALF)
        gate_row = jnp.pad(gate_slots[e].astype(bf16), ((0, 0), (0, HALF - SLOTS)))
        sent = lax.dynamic_update_slice_in_dim(sent, gate_row[:, None, :], CAP, 1)
        own = exchange_ctx(sent)
        gate_in.append(own[:, CAP, :SLOTS].astype(f32).reshape(N_CTX * SLOTS, 1))
        own = own.reshape(N_CTX * SLOTS, HALF)
        rows_in.append(whole_of(own, swap(own, "core"), core))

    gate_up_pre = nn(normed_two, gate_up)
    gate_sh, up_sh = gate_up_pre[:, :FF_SH], gate_up_pre[:, FF_SH:]
    hidden_sh = (jax.nn.silu(gate_sh) * up_sh).astype(bf16)
    grad_hidden_sh = nn(grad_out, shared_down_t)
    grad_gate_up = jnp.concatenate(
        [
            (grad_hidden_sh * up_sh * silu_slope(gate_sh)).astype(bf16),
            (grad_hidden_sh * jax.nn.silu(gate_sh)).astype(bf16),
        ],
        axis=1,
    )
    shared_in_half = core_half(nt(grad_gate_up, gate_up), core)
    shared_part = nt(hidden_sh, shared_down_t)
    shared_half = core_half(shared_part, core)
    grad_gate_up_part = tn(normed_two, grad_gate_up).astype(bf16)
    grad_shared_down_part = tn(grad_out, hidden_sh).astype(bf16)

    grads_gate, grads_up, grads_down = [], [], []
    rows_back, outs_back = [], []
    later = []
    for e in range(EXP_DEV):
        rows, grads = rows_in[e], grad_rows[e]
        gate_ex = nn(rows, expert_gate[e])
        up_ex = nn(rows, expert_up[e])
        hidden_ex = (jax.nn.silu(gate_ex) * up_ex).astype(bf16)
        plain = nt(grads, expert_down[e])
        gate_dot = jnp.sum(hidden_ex.astype(f32) * plain, axis=1)
        grad_hidden = plain * gate_in[e]
        grad_gate_ex = (grad_hidden * up_ex * silu_slope(gate_ex)).astype(bf16)
        grad_up_ex = (grad_hidden * jax.nn.silu(gate_ex)).astype(bf16)
        halves = []
        for which in (1 - core, core):
            halves.append(
                nt(grad_gate_ex, half_of(expert_gate[e], which, 0))
                + nt(grad_up_ex, half_of(expert_up[e], which, 0))
            )
        summed = halves[1] + swap(halves[0].astype(bf16), "core").astype(f32)
        gate_dot = (gate_dot + swap(gate_dot, "core")).astype(bf16).reshape(N_CTX, SLOTS)
        sent = summed.astype(bf16).reshape(N_CTX, SLOTS, HALF)
        gate_row = jnp.pad(gate_dot, ((0, 0), (0, HALF - SLOTS)))
        sent = lax.dynamic_update_slice_in_dim(sent, gate_row[:, None, :], CAP, 1)
        rows_back.append(exchange_ctx(sent))
        later.append((rows, grads, hidden_ex, grad_gate_ex, grad_up_ex))
    for e in range(EXP_DEV):
        rows, grads, hidden_ex, grad_gate_ex, grad_up_ex = later[e]
        halves = [nn(hidden_ex, half_of(expert_down[e], which, 1)) for which in (1 - core, core)]
        summed = halves[1] + swap(halves[0].astype(bf16), "core").astype(f32)
        outs_back.append(exchange_ctx(summed.astype(bf16).reshape(N_CTX, SLOTS, HALF)))
        scaled_hidden = (hidden_ex.astype(f32) * gate_in[e]).astype(bf16)
        grads_down.append(tn(scaled_hidden, grads))
        grads_gate.append(tn(rows, grad_gate_ex))
        grads_up.append(tn(rows, grad_up_ex))
    grad_expert_gate = jnp.stack(grads_gate)
    grad_expert_up = jnp.stack(grads_up)
    grad_expert_down = jnp.stack(grads_down)

    routed_in_half = shared_in_half
    prob_grad = []
    for e in range(EXP_DEV):
        routed_in_half = routed_in_half + tn(
            flat_hot[e], rows_back[e].reshape(N_CTX * SLOTS, HALF)
        )
        dots = rows_back[e][:, CAP, :SLOTS].astype(f32)
        prob_grad.append(jnp.sum(places_hot[e].astype(f32) * dots[:, :, None], axis=1))
    prob_grad = jnp.stack(prob_grad, axis=1).reshape(EXPERTS, TOK).T
    prob_grad = prob_grad + swap(prob_grad, "zl")
    normed_half_grad = zl_sum(routed_in_half)
    normed_two_grad = whole_of(normed_half_grad, swap(normed_half_grad, "core"), core)
    logit_grad = (
        probs_router * (prob_grad - jnp.sum(probs_router * prob_grad, axis=-1, keepdims=True))
    ).astype(bf16)
    normed_two_grad = normed_two_grad + nn(logit_grad, router_t)
    normed_two_quarter = lax.dynamic_slice_in_dim(normed_two, column_start, QUARTER, 1)
    router_part = tn(logit_grad, normed_two_quarter).reshape(N_CTX, EXP_DEV, QUARTER)
    upstream = grad_out.astype(f32)
    after_grad = upstream + norm_back(normed_two_grad, after_attn, root_two, gain_two)
    gain_two_part = jnp.sum(normed_two_grad * after_attn * root_two, axis=0)
    gain_two_mine = pick(gain_two_part.reshape(N_CTX, 4, 16), ws, 1)

    attn_grad = after_grad.astype(bf16)
    head_grad = nn(attn_grad, output_t).astype(bf16).reshape(TOK, HEADS, VDIM)
    latent_grad = jnp.einsum(
        "thv,hrv->htr", head_grad, value_up, preferred_element_type=f32
    ).astype(bf16)
    grad_query_lat, grad_keys = attend_back(
        places,
        query,
        keys,
        value,
        log_total,
        latent_grad.reshape(HEADS, 2, BLOCK, RANK),
    )
    grad_query_lat = grad_query_lat.reshape(HEADS, TOK, KEYS)

    grad_keys = grad_keys.astype(bf16).reshape(SEQ_BLOCKS, 2, 64, KEYS)
    keys_half = pick(grad_keys, core, 1).astype(f32) + swap(
        pick(grad_keys, 1 - core, 1), "core"
    ).astype(f32)
    keys_half = keys_half.astype(bf16)[place_of].reshape(2, SEQ_PAIRS, 64, KEYS)
    keys_mine = pick(keys_half, zl, 0).astype(f32) + swap(pick(keys_half, 1 - zl, 0), "zl").astype(
        f32
    )
    keys_sent = jnp.where(
        in_seq[:, None, None], keys_mine.astype(bf16)[jnp.clip(rank, 0, SEQ_PAIRS - 1)], 0
    )
    latent_sum = jnp.sum(exchange_ctx(keys_sent).astype(f32), axis=0)

    query_lat_grad = grad_query_lat[..., :RANK].astype(bf16)
    nope_grad = jnp.einsum("htr,hrn->thn", query_lat_grad, key_up, preferred_element_type=f32)
    rope_grad = rotate(grad_query_lat[..., RANK:].transpose(1, 0, 2), positions, -1.0)
    query_grad = (
        jnp.concatenate([nope_grad, rope_grad], axis=-1)
        .astype(bf16)
        .reshape(TOK, HEADS * (NOPE + ROPE))
    )
    grad_query_part = tn(normed_one, query_grad).astype(bf16)
    normed_one_part = nt(query_grad, query_full)
    grad_key_up = jnp.einsum(
        "thn,htr->hrn", query_nope, query_lat_grad, preferred_element_type=f32
    )
    grad_value_up = jnp.einsum("htr,thv->hrv", value_parts, head_grad, preferred_element_type=f32)
    grad_up_part = (
        jnp.concatenate([grad_key_up, grad_value_up], axis=-1)
        .astype(bf16)
        .reshape(HEADS, N_CTX, 16, NOPE + VDIM)
        .transpose(1, 0, 2, 3)
        .reshape(N_CTX, 64, NOPE + VDIM)
    )
    grad_output_part = tn(attn_grad, head_flat).astype(bf16).reshape(N_CTX, 64, QUARTER)

    latent_norm_grad = latent_sum[:, :RANK]
    latent_pre_grad = norm_back(latent_norm_grad, latent_pre, root_kv, gain_kv)
    gain_kv_part = jnp.sum(latent_norm_grad * latent_pre * root_kv, axis=0)
    rope_pre_grad = rotate(latent_sum[:, RANK:], my_positions, -1.0)
    compressed_grad = jnp.concatenate([latent_pre_grad, rope_pre_grad], axis=1).astype(bf16)
    compressed_grad = gather_two(gather_two(compressed_grad, "core", 0), "zl", 0).reshape(TOK, KEYS)
    grad_down_part = tn(compressed_grad, normed_quarter).reshape(N_CTX, 18, QUARTER)
    rows_grad = nn(compressed_grad, down_t)
    mine = lax.dynamic_slice_in_dim(normed_one_part, column_start, QUARTER, 1)
    normed_one_part = lax.dynamic_update_slice_in_dim(
        normed_one_part, mine + rows_grad, column_start, 1
    )
    input_part = norm_back(normed_one_part, inputs, root_one, gain_one)
    gain_one_part = jnp.sum(normed_one_part * inputs * root_one, axis=0)
    input_quarter = zl_quarter(core_half(input_part, core), zl)
    grad_in = lax.dynamic_slice_in_dim(after_grad, column_start, QUARTER, 1) + input_quarter
    gain_parts = jnp.concatenate(
        [gain_one_part.reshape(N_CTX, 2, 2, 16), gain_kv_part.reshape(N_CTX, 2, 2, 4)], axis=-1
    )
    gain_core = pick(gain_parts, core, 2) + swap(pick(gain_parts, 1 - core, 2), "core")
    gain_mine = pick(gain_core, zl, 1) + swap(pick(gain_core, 1 - zl, 1), "zl")

    routed_half = shared_half
    for e in range(EXP_DEV):
        weighted = (flat_hot[e].astype(f32) * gate_slots[e].reshape(N_CTX * SLOTS, 1)).astype(bf16)
        routed_half = routed_half + tn(weighted, outs_back[e].reshape(N_CTX * SLOTS, HALF))
    layer_out = (
        lax.dynamic_slice_in_dim(after_attn, column_start, QUARTER, 1)
        + zl_quarter(routed_half, zl)
    ).astype(bf16)

    gate_up_sum = scatter_ctx(grad_gate_up_part.reshape(N_CTX, 64, 2 * FF_SH), True)
    shared_down_sum = scatter_ctx(grad_shared_down_part.reshape(N_CTX, 64, FF_SH), False)
    query_sum = scatter_ctx(grad_query_part.reshape(N_CTX, 64, HEADS * (NOPE + ROPE)), True)
    out_up_sum = scatter_ctx(jnp.concatenate([grad_output_part, grad_up_part], axis=2), False)
    gain_row = jnp.concatenate([gain_mine, gain_two_mine], axis=1)
    gain_row = jnp.pad(gain_row, ((0, 0), (0, QUARTER - 36)))[:, None, :]
    small_parts = jnp.concatenate(
        [
            grad_down_part.astype(bf16),
            router_part.astype(bf16),
            gain_row.astype(bf16),
            jnp.zeros((N_CTX, 3, QUARTER), bf16),
        ],
        axis=1,
    )
    small_sum = scatter_ctx(small_parts, True)
    up_sum = (
        out_up_sum[:, QUARTER:]
        .reshape(HEADS, 16, NOPE + VDIM)
        .transpose(1, 0, 2)
        .reshape(16, HEADS * (NOPE + VDIM))
    )
    return (
        layer_out,
        grad_in,
        small_sum[20, :16],
        small_sum[20, 16:20],
        small_sum[20, 20:36],
        query_sum,
        small_sum[:18].T,
        up_sum,
        out_up_sum[:, :QUARTER].T,
        small_sum[18:20].T,
        grad_expert_gate,
        grad_expert_up,
        grad_expert_down,
        gate_up_sum[:, :FF_SH],
        gate_up_sum[:, FF_SH:],
        shared_down_sum.T,
    )


def solution(mesh):
    grid = Mesh(mesh.devices.reshape(2, 4, 4, 2, 2), CTX + ("zl", "core"))
    ctx, ws, both = CTX, ("zl", "core"), CTX + ("zl", "core")
    placed = (
        P(ctx, None),
        P(ctx, None),
        P(),
        P(ctx, None),
        P(ctx),
        P(both),
        P(both),
        P(both),
        P(ctx, ws),
        P(ws, ctx),
        P(ctx, ws),
        P(ws, ctx),
        P(ws, ctx),
        P(ctx, None, ws),
        P(ctx, None, ws),
        P(ctx, ws, None),
        P(ctx, ws),
        P(ctx, ws),
        P(ws, ctx),
    )
    return jax.shard_map(
        on_device,
        mesh=grid,
        in_specs=placed,
        out_specs=(
            P(ctx, ws),
            P(ctx, ws),
            P(both),
            P(both),
            P(both),
            P(ctx, ws),
            P(ws, ctx),
            P(ctx, ws),
            P(ws, ctx),
            P(ws, ctx),
            P(ctx, None, ws),
            P(ctx, None, ws),
            P(ctx, ws, None),
            P(ctx, ws),
            P(ctx, ws),
            P(ws, ctx),
        ),
        check_vma=False,
    )
```

time: 3940 us -> 1080 us (0.27)
  waiting for transfers between devices: 2850 us -> 371 us
  blocking collectives: 420 us -> 0 us
  starting transfers between devices: 51.9 us -> 206 us
  matrix products: 222 us -> 141 us
  local copies, waits for them, and re-layouts: 280 us -> 202 us
    reduce_scatter x12 -> x0, waiting for transfers between devices: 1470 us -> none  [the longest x2 250 us: hidden_sums(): lax.psum_scatter(routed_part, 'ws', scatter_dimension=2, tiled=True)]
    unnamed x34 -> x0, waiting for transfers between devices: 864 us -> none
    all_gather x9 -> x0, waiting for transfers between devices: 328 us -> none  [the longest x1 129 us: on_device(): latent_all = lax.all_gather(latent_local, 'ctx', axis=0, tiled=True)]
    ppermute x0 -> x110, waiting for transfers between devices: none -> 312 us  [shift(): lax.ppermute(value, axis, [(i, (i + step) % size) for i in range(size)])]
    unnamed x5 -> x0, blocking collectives: 310 us -> none
    ppermute x0 -> x110, starting transfers between devices: none -> 141 us  [shift(): lax.ppermute(value, axis, [(i, (i + step) % size) for i in range(size)])]
    all_to_all x4 -> x9, waiting for transfers between devices: 185 us -> 59 us  [exchange_ctx(): return lax.all_to_all(value, CTX, 0, 0, tiled=True)]
    all_gather x4 -> x0, blocking collectives: 110 us -> none  [the longest x1 92 us: on_device(): lax.all_gather(router_ws, 'ctx', axis=1, tiled=True)]
  transfers between devices with their start and end apart: 36 -> 119, of which waited for: 20 -> 44; matrix products, arithmetic and copies ran while one was open for 13% -> 37% of each run, Pallas kernels for 0% -> 2%
where the time goes in v1:
time: 1080 us; the launch traced here: 1060 us
  waiting for transfers between devices  371 us (34%)
  starting transfers between devices  206 us (19%)
  local copies, waits for them, and re-layouts  202 us (19%)
  matrix products  141 us (13%)
  other arithmetic  110 us (10%)
  Pallas kernels  30.5 us (3%)
    ppermute x110, waiting for transfers between devices, shift(): lax.ppermute(value, axis, [(i, (i + step) % size) for i in range(size)])  312 us
    ppermute x110, starting transfers between devices, shift(): lax.ppermute(value, axis, [(i, (i + step) % size) for i in range(size)])  141 us
    dot_general x51, matrix products, dot(): lax.dot_general(a, b, ((contract[0], contract[1]), ((), ())), preferred_e...  135 us
    all_to_all x9, starting transfers between devices, exchange_ctx(): return lax.all_to_all(value, CTX, 0, 0, tiled=True)  65.1 us
    all_to_all x9, waiting for transfers between devices, exchange_ctx(): return lax.all_to_all(value, CTX, 0, 0, tiled=True)  59 us
    dynamic_update_slice x43, local copies, waits for them, and re-layouts, gather_four(): lax.dynamic_update_slice_in_dim(result, jnp.expand_dims(piece, dim), (her...  47.8 us
    unnamed x409, local copies, waits for them, and re-layouts  28.5 us
  transfers between devices with their start and end apart: 119, of which 44 were waited for; matrix products, arithmetic and copies ran while one was open for 37% of the time, Pallas kernels for 2%

profile of v1, /device:TPU:0, one launch (start us, length us, event | category | flops | bytes accessed | tf_op | source)
XLA Modules:
  0.0 1064.1 jit_solution(10058085310157659446)
XLA Ops:
  112.4 7.5 collective-permute-done.24
  167.5 16.2 %collective-permute-done.29 = bf16[2,4,64,576]{3,2,1,0:T(8,128)(2,1)S(1)} collective-permute-done((bf16[2,4,64,576]{3,2,1,0:T(8,128)(2,1)}, bf16[2,4,64,576]{3,2,1,0:T(8,128)(2,1)S(1)}, u32[]{:S(2)}, u32[]{:S(2)}) %collective-permute-start.29) | collective-permute-done | bytes 589856 | tf_op jit(solution)/shard_map/ppermute | solution.py:86
  198.8 8.9 collective-permute-done.32
  232.0 13.6 %attend.1 = (f32[4,2,128,512]{3,2,1,0:T(8,128)S(1)}, f32[4,2,128,128]{3,2,1,0:T(8,128)S(1)}) custom-call(s32[2]{0:T(128)S(1)} %get-tuple-element.45.place_ref, bf16[4,2,128,576]{3,2,1,0:T(8,128)(2,1)S(1)} %bitcast.718, bf16[2048,576]{1,0:T(8,128)(2,1)} %bitcast.764), custom_call_target="tpu_custom_call" | custom-call | flops 2852126720 | bytes 8388608 | tf_op jit(solution)/shard_map/attend/pallas_call | solution.py:217
  253.8 6.9 collective-permute-done.44
  287.8 14.1 %collective-permute-done.40 = bf16[2,64,1408]{2,1,0:T(8,128)(2,1)S(1)} collective-permute-done((bf16[2,64,1408]{2,1,0:T(8,128)(2,1)S(1)}, bf16[2,64,1408]{2,1,0:T(8,128)(2,1)S(1)}, u32[]{:S(2)}, u32[]{:S(2)}) %collective-permute-start.40) | collective-permute-done | bytes 360480 | tf_op jit(solution)/shard_map/ppermute | solution.py:86
  304.9 13.7 %collective-permute-done.49 = bf16[2,4,64,704]{3,2,1,0:T(8,128)(2,1)S(1)} collective-permute-done((bf16[2,4,64,704]{3,2,1,0:T(8,128)(2,1)S(1)}, bf16[2,4,64,704]{3,2,1,0:T(8,128)(2,1)S(1)}, u32[]{:S(2)}, u32[]{:S(2)}) %collective-permute-start.49) | collective-permute-done | bytes 720928 | tf_op jit(solution)/shard_map/ppermute | solution.py:86
  321.5 12.5 %collective-permute-done.41 = bf16[2,4,64,1408]{3,2,1,0:T(8,128)(2,1)S(1)} collective-permute-done((bf16[2,4,64,1408]{3,2,1,0:T(8,128)(2,1)S(1)}, bf16[2,4,64,1408]{3,2,1,0:T(8,128)(2,1)S(1)}, u32[]{:S(2)}, u32[]{:S(2)}) %collective-permute-start.41) | collective-permute-done | bytes 1441824 | tf_op jit(solution)/shard_map/ppermute | solution.py:86
  334.3 19.9 %collective-permute-done.42 = bf16[2,4,64,1408]{3,2,1,0:T(8,128)(2,1)S(1)} collective-permute-done((bf16[2,4,64,1408]{3,2,1,0:T(8,128)(2,1)S(1)}, bf16[2,4,64,1408]{3,2,1,0:T(8,128)(2,1)S(1)}, u32[]{:S(2)}, u32[]{:S(2)}) %collective-permute-start.42) | collective-permute-done | bytes 1441824 | tf_op jit(solution)/shard_map/ppermute | solution.py:86
  354.3 12.9 %collective-permute-done.43 = bf16[2,4,64,1408]{3,2,1,0:T(8,128)(2,1)S(1)} collective-permute-done((bf16[2,4,64,1408]{3,2,1,0:T(8,128)(2,1)S(1)}, bf16[2,4,64,1408]{3,2,1,0:T(8,128)(2,1)S(1)}, u32[]{:S(2)}, u32[]{:S(2)}) %collective-permute-start.43) | collective-permute-done | bytes 1441824 | tf_op jit(solution)/shard_map/ppermute | solution.py:86
  381.0 6.0 all-to-all-start
  408.9 36.7 %all-to-all-done = bf16[32,32,1024]{2,1,0:T(8,128)(2,1)} async-done(((bf16[32,32,1024]{2,1,0:T(8,128)(2,1)}), bf16[32,32,1024]{2,1,0:T(8,128)(2,1)}, u32[]{:S(2)}, u32[]{:S(2)}) %all-to-all-start) | async-done | bytes 2097184 | tf_op jit(solution)/shard_map/all_to_all | solution.py:144
  476.5 23.8 %collective-permute-done.105 = bf16[2,4,64,704]{3,2,1,0:T(8,128)(2,1)S(1)} collective-permute-done((bf16[2,4,64,704]{3,2,1,0:T(8,128)(2,1)S(1)}, bf16[2,4,64,704]{3,2,1,0:T(8,128)(2,1)S(1)}, u32[]{:S(2)}, u32[]{:S(2)}) %collective-permute-start.105) | collective-permute-done | bytes 720928 | tf_op jit(solution)/shard_map/ppermute | solution.py:86
  507.2 11.7 %all-to-all-start.2 = ((bf16[32,32,1024]{2,1,0:T(8,128)(2,1)}), bf16[32,32,1024]{2,1,0:T(8,128)(2,1)}, u32[]{:S(2)}, u32[]{:S(2)}) async-start(bf16[32,32,1024]{2,1,0:T(8,128)(2,1)} %dynamic_update_slice.208), calls=%async_computation.2 | async-start | bytes 4194304 | tf_op jit(solution)/shard_map/all_to_all | solution.py:144
  522.3 15.1 %collective-permute-done.103 = bf16[2,4,64,704]{3,2,1,0:T(8,128)(2,1)} collective-permute-done((bf16[2,4,64,704]{3,2,1,0:T(8,128)(2,1)}, bf16[2,4,64,704]{3,2,1,0:T(8,128)(2,1)}, u32[]{:S(2)}, u32[]{:S(2)}) %collective-permute-start.103) | collective-permute-done | bytes 720928 | tf_op jit(solution)/shard_map/ppermute | solution.py:86
  540.2 6.0 collective-permute-start.107
  554.8 9.7 all-to-all-start.6
  571.5 20.8 %collective-permute-done.109 = bf16[64,704]{1,0:T(8,128)(2,1)S(1)} collective-permute-done((bf16[64,704]{1,0:T(8,128)(2,1)S(1)}, bf16[64,704]{1,0:T(8,128)(2,1)S(1)}, u32[]{:S(2)}, u32[]{:S(2)}) %collective-permute-start.109) | collective-permute-done | bytes 90144 | tf_op jit(solution)/shard_map/ppermute | solution.py:86
  657.8 6.9 all-to-all-start.1
  687.9 6.4 all-to-all-done.1
  699.8 6.1 pad_maximum_fusion
  733.9 6.1 pad_maximum_fusion.1
  753.2 10.1 all-to-all-done.7
  768.4 6.0 pad_maximum_fusion.2
  779.4 6.8 collective-permute-start.64
  791.2 18.6 %collective-permute-done.64 = bf16[256,1024]{1,0:T(8,128)(2,1)} collective-permute-done((bf16[256,1024]{1,0:T(8,128)(2,1)S(1)}, bf16[256,1024]{1,0:T(8,128)(2,1)}, u32[]{:S(2)}, u32[]{:S(2)}) %collective-permute-start.64) | collective-permute-done | bytes 524320 | tf_op jit(solution)/shard_map/ppermute | solution.py:86
  828.2 16.9 %attend_back.1 = (f32[4,2,128,576]{3,2,1,0:T(8,128)}, f32[2048,576]{1,0:T(8,128)}) custom-call(s32[2]{0:T(128)S(1)} %get-tuple-element.45.place_ref, bf16[4,2,128,576]{3,2,1,0:T(8,128)(2,1)S(1)} %bitcast.719, bf16[2048,576]{1,0:T(8,128)(2,1)} %bitcast.765, f32[4,2,128,512]{3,2,1,0:T(8,128)S(1)} %copy-done.1, ...), custom_call_target="tpu_custom_call" | custom-call | flops 7549747200 | bytes 14680064 | tf_op jit(solution)/shard_map/attend_back/pallas_call | solution.py:293
  876.3 10.2 collective-permute-done.68
  894.1 9.3 all-to-all-start.8
  923.1 27.9 %collective-permute-done.91 = bf16[2,4,64,768]{3,2,0,1:T(8,128)(2,1)S(1)} collective-permute-done((bf16[2,4,64,768]{3,2,0,1:T(8,128)(2,1)S(1)}, bf16[2,4,64,768]{3,2,0,1:T(8,128)(2,1)S(1)}, u32[]{:S(2)}, u32[]{:S(2)}) %collective-permute-start.91) | collective-permute-done | bytes 786464 | tf_op jit(solution)/shard_map/ppermute | solution.py:86
  953.3 18.7 %collective-permute-done.89 = bf16[2,4,64,768]{3,2,0,1:T(8,128)(2,1)S(1)} collective-permute-done((bf16[2,4,64,768]{3,2,0,1:T(8,128)(2,1)S(1)}, bf16[2,4,64,768]{3,2,0,1:T(8,128)(2,1)S(1)}, u32[]{:S(2)}, u32[]{:S(2)}) %collective-permute-start.89) | collective-permute-done | bytes 786464 | tf_op jit(solution)/shard_map/ppermute | solution.py:86
  995.0 7.7 collective-permute-done.70
  (1025 shorter events, 645.5 us)
Async XLA Ops:
  6.4 54.6 %collective-permute-start.16 = (bf16[64,768]{1,0:T(8,128)(2,1)}, bf16[64,768]{1,0:T(8,128)(2,1)}, u32[]{:S(2)}, u32[]{:S(2)}) collective-permute-start(bf16[64,768]{1,0:T(8,128)(2,1)} %param.27), channel_id=1, source_target_pairs={{0,64},{64,0},{1,65},{65,1},{2,66},{66,2},{3,67},{67,3},{4,68},{68... | collective-permute-start | bytes 294920 | tf_op jit(solution)/shard_map/ppermute | solution.py:86
  8.8 55.9 %collective-permute-start = (bf16[64,768]{1,0:T(8,128)(2,1)}, bf16[64,768]{1,0:T(8,128)(2,1)}, u32[]{:S(2)}, u32[]{:S(2)}) collective-permute-start(bf16[64,768]{1,0:T(8,128)(2,1)} %pad_maximum_fusion.39), channel_id=1, source_target_pairs={{0,64},{64,0},{1,65},{65,1},{2,66},{66,2},{3,67},{67,3},{4,68},{68... | collective-permute-start | bytes 294920 | tf_op jit(solution)/shard_map/ppermute | solution.py:86
  94.4 61.8 %collective-permute-start.20 = (bf16[2,4,64,768]{3,2,1,0:T(8,128)(2,1)}, bf16[2,4,64,768]{3,2,1,0:T(8,128)(2,1)}, u32[]{:S(2)}, u32[]{:S(2)}) collective-permute-start(bf16[2,4,64,768]{3,2,1,0:T(8,128)(2,1)} %bitcast_dynamic-update-slice_fusion.28), channel_id=1, source_target_pairs={{0,4},{4,8},{8,12},{12,0},{1,5},{5,9},{9,13},{13,1},{2,6},{6,10},{... | collective-permute-start | bytes 2359304 | tf_op jit(solution)/shard_map/ppermute | solution.py:86
  95.3 64.6 %collective-permute-start.21 = (bf16[2,4,64,768]{3,2,1,0:T(8,128)(2,1)}, bf16[2,4,64,768]{3,2,1,0:T(8,128)(2,1)}, u32[]{:S(2)}, u32[]{:S(2)}) collective-permute-start(bf16[2,4,64,768]{3,2,1,0:T(8,128)(2,1)} %bitcast_dynamic-update-slice_fusion.28), channel_id=1, source_target_pairs={{0,8},{4,12},{8,0},{12,4},{1,9},{5,13},{9,1},{13,5},{2,10},{6,14},... | collective-permute-start | bytes 2359304 | tf_op jit(solution)/shard_map/ppermute | solution.py:86
  143.9 49.9 %collective-permute-start.22 = (bf16[2,4,64,768]{3,2,1,0:T(8,128)(2,1)}, bf16[2,4,64,768]{3,2,1,0:T(8,128)(2,1)}, u32[]{:S(2)}, u32[]{:S(2)}) collective-permute-start(bf16[2,4,64,768]{3,2,1,0:T(8,128)(2,1)} %bitcast_dynamic-update-slice_fusion.28), channel_id=1, source_target_pairs={{0,12},{4,0},{8,4},{12,8},{1,13},{5,1},{9,5},{13,9},{2,14},{6,2},{... | collective-permute-start | bytes 2359304 | tf_op jit(solution)/shard_map/ppermute | solution.py:86
  147.9 48.0 %collective-permute-start.4 = (bf16[2,4,64,768]{3,2,1,0:T(8,128)(2,1)}, bf16[2,4,64,768]{3,2,1,0:T(8,128)(2,1)}, u32[]{:S(2)}, u32[]{:S(2)}) collective-permute-start(bf16[2,4,64,768]{3,2,1,0:T(8,128)(2,1)} %bitcast_dynamic-update-slice_fusion.35), channel_id=1, source_target_pairs={{0,16},{16,32},{32,48},{48,0},{1,17},{17,33},{33,49},{49,1},{2,18}... | collective-permute-start | bytes 2359304 | tf_op jit(solution)/shard_map/ppermute | solution.py:86
  279.4 41.6 %collective-permute-start.50 = (bf16[2,4,64,704]{3,2,1,0:T(8,128)(2,1)S(1)}, bf16[2,4,64,704]{3,2,1,0:T(8,128)(2,1)S(1)}, u32[]{:S(2)}, u32[]{:S(2)}) collective-permute-start(bf16[2,4,64,704]{3,2,1,0:T(8,128)(2,1)S(1)} %bitcast_dynamic-update-slice_fusion.24), channel_id=1, source_target_pairs={{0,48},{16,0},{32,16},{48,32},{1,49},{17,1},{33,17},{49,33},{2,50}... | collective-permute-start | bytes 2162696 | tf_op jit(solution)/shard_map/ppermute | solution.py:86
  303.5 50.6 %collective-permute-start.42 = (bf16[2,4,64,1408]{3,2,1,0:T(8,128)(2,1)S(1)}, bf16[2,4,64,1408]{3,2,1,0:T(8,128)(2,1)S(1)}, u32[]{:S(2)}, u32[]{:S(2)}) collective-permute-start(bf16[2,4,64,1408]{3,2,1,0:T(8,128)(2,1)S(1)} %bitcast_dynamic-update-slice_fusion.23), channel_id=1, source_target_pairs={{0,8},{4,12},{8,0},{12,4},{1,9},{5,13},{9,1},{13,5},{2,10},{6,14},... | collective-permute-start | bytes 4325384 | tf_op jit(solution)/shard_map/ppermute | solution.py:86
  318.6 48.7 %collective-permute-start.43 = (bf16[2,4,64,1408]{3,2,1,0:T(8,128)(2,1)S(1)}, bf16[2,4,64,1408]{3,2,1,0:T(8,128)(2,1)S(1)}, u32[]{:S(2)}, u32[]{:S(2)}) collective-permute-start(bf16[2,4,64,1408]{3,2,1,0:T(8,128)(2,1)S(1)} %bitcast_dynamic-update-slice_fusion.23), channel_id=1, source_target_pairs={{0,12},{4,0},{8,4},{12,8},{1,13},{5,1},{9,5},{13,9},{2,14},{6,2},{... | collective-permute-start | bytes 4325384 | tf_op jit(solution)/shard_map/ppermute | solution.py:86
  321.4 46.1 %collective-permute-start.36 = (f32[256,1024]{1,0:T(8,128)S(1)}, f32[256,1024]{1,0:T(8,128)S(1)}, u32[]{:S(2)}, u32[]{:S(2)}) collective-permute-start(f32[256,1024]{1,0:T(8,128)S(1)} %maximum_add_fusion.1), channel_id=1, source_target_pairs={{0,1},{1,0},{2,3},{3,2},{4,5},{5,4},{6,7},{7,6},{8,9},{9,8},{10,11... | collective-permute-start | bytes 3145736 | tf_op jit(solution)/shard_map/ppermute | solution.py:86
  381.0 64.6 %all-to-all-start = ((bf16[32,32,1024]{2,1,0:T(8,128)(2,1)}), bf16[32,32,1024]{2,1,0:T(8,128)(2,1)}, u32[]{:S(2)}, u32[]{:S(2)}) async-start(bf16[32,32,1024]{2,1,0:T(8,128)(2,1)} %dynamic_update_slice.207), calls=%async_computation | async-start | bytes 4194304 | tf_op jit(solution)/shard_map/all_to_all | solution.py:144
  399.4 146.8 %collective-permute-start.98 = (bf16[2,4,64,1408]{3,2,0,1:T(8,128)(2,1)}, bf16[2,4,64,1408]{3,2,0,1:T(8,128)(2,1)}, u32[]{:S(2)}, u32[]{:S(2)}) collective-permute-start(bf16[2,4,64,1408]{3,2,0,1:T(8,128)(2,1)} %bitcast.707), channel_id=1, source_target_pairs={{0,12},{4,0},{8,4},{12,8},{1,13},{5,1},{9,5},{13,9},{2,14},{6,2},{... | collective-permute-start | bytes 4325384 | tf_op jit(solution)/shard_map/ppermute | solution.py:86
  403.8 143.9 %collective-permute-start.97 = (bf16[2,4,64,1408]{3,2,0,1:T(8,128)(2,1)}, bf16[2,4,64,1408]{3,2,0,1:T(8,128)(2,1)}, u32[]{:S(2)}, u32[]{:S(2)}) collective-permute-start(bf16[2,4,64,1408]{3,2,0,1:T(8,128)(2,1)} %bitcast.708), channel_id=1, source_target_pairs={{0,8},{4,12},{8,0},{12,4},{1,9},{5,13},{9,1},{13,5},{2,10},{6,14},... | collective-permute-start | bytes 4325384 | tf_op jit(solution)/shard_map/ppermute | solution.py:86
  405.9 141.7 %collective-permute-start.96 = (bf16[2,4,64,1408]{3,2,0,1:T(8,128)(2,1)}, bf16[2,4,64,1408]{3,2,0,1:T(8,128)(2,1)}, u32[]{:S(2)}, u32[]{:S(2)}) collective-permute-start(bf16[2,4,64,1408]{3,2,0,1:T(8,128)(2,1)} %bitcast.709), channel_id=1, source_target_pairs={{0,4},{4,8},{8,12},{12,0},{1,5},{5,9},{9,13},{13,1},{2,6},{6,10},{... | collective-permute-start | bytes 4325384 | tf_op jit(solution)/shard_map/ppermute | solution.py:86
  445.6 61.6 %all-to-all-start.4 = ((bf16[32,32,1024]{2,1,0:T(8,128)(2,1)}), bf16[32,32,1024]{2,1,0:T(8,128)(2,1)}, u32[]{:S(2)}, u32[]{:S(2)}) async-start(bf16[32,32,1024]{2,1,0:T(8,128)(2,1)} %bitcast.746), calls=%async_computation.4 | async-start | bytes 4194304 | tf_op jit(solution)/shard_map/all_to_all | solution.py:144
  473.4 49.0 %collective-permute-start.104 = (bf16[2,4,64,704]{3,2,1,0:T(8,128)(2,1)}, bf16[2,4,64,704]{3,2,1,0:T(8,128)(2,1)}, u32[]{:S(2)}, u32[]{:S(2)}) collective-permute-start(bf16[2,4,64,704]{3,2,1,0:T(8,128)(2,1)} %get-tuple-element.63), channel_id=1, source_target_pairs={{0,32},{16,48},{32,0},{48,16},{1,33},{17,49},{33,1},{49,17},{2,34}... | collective-permute-start | bytes 2162696 | tf_op jit(solution)/shard_map/ppermute | solution.py:86
  507.2 47.6 %all-to-all-start.2 = ((bf16[32,32,1024]{2,1,0:T(8,128)(2,1)}), bf16[32,32,1024]{2,1,0:T(8,128)(2,1)}, u32[]{:S(2)}, u32[]{:S(2)}) async-start(bf16[32,32,1024]{2,1,0:T(8,128)(2,1)} %dynamic_update_slice.208), calls=%async_computation.2 | async-start | bytes 4194304 | tf_op jit(solution)/shard_map/all_to_all | solution.py:144
  554.8 257.3 %collective-permute-start.51 = (bf16[256,1024]{1,0:T(8,128)(2,1)}, bf16[256,1024]{1,0:T(8,128)(2,1)}, u32[]{:S(2)}, u32[]{:S(2)}) collective-permute-start(bf16[256,1024]{1,0:T(8,128)(2,1)} %pad_maximum_fusion.19), channel_id=1, source_target_pairs={{0,1},{1,0},{2,3},{3,2},{4,5},{5,4},{6,7},{7,6},{8,9},{9,8},{10,11... | collective-permute-start | bytes 1572872 | tf_op jit(solution)/shard_map/ppermute | solution.py:86
  554.8 45.4 %all-to-all-start.6 = ((bf16[32,32,1024]{2,1,0:T(8,128)(2,1)}), bf16[32,32,1024]{2,1,0:T(8,128)(2,1)}, u32[]{:S(2)}, u32[]{:S(2)}) async-start(bf16[32,32,1024]{2,1,0:T(8,128)(2,1)} %bitcast.745), calls=%async_computation.6 | async-start | bytes 4194304 | tf_op jit(solution)/shard_map/all_to_all | solution.py:144
  566.0 210.8 %collective-permute-start.57 = (bf16[256,1024]{1,0:T(8,128)(2,1)}, bf16[256,1024]{1,0:T(8,128)(2,1)}, u32[]{:S(2)}, u32[]{:S(2)}) collective-permute-start(bf16[256,1024]{1,0:T(8,128)(2,1)} %pad_maximum_fusion.21), channel_id=1, source_target_pairs={{0,1},{1,0},{2,3},{3,2},{4,5},{5,4},{6,7},{7,6},{8,9},{9,8},{10,11... | collective-permute-start | bytes 1572872 | tf_op jit(solution)/shard_map/ppermute | solution.py:86
  638.2 110.7 %collective-permute-start.55 = (bf16[1024,1024]{1,0:T(8,128)(2,1)}, bf16[1024,1024]{1,0:T(8,128)(2,1)}, u32[]{:S(2)}, u32[]{:S(2)}) collective-permute-start(bf16[1024,1024]{1,0:T(8,128)(2,1)} %convolution_convert_fusion.4), channel_id=1, source_target_pairs={{0,1},{1,0},{2,3},{3,2},{4,5},{5,4},{6,7},{7,6},{8,9},{9,8},{10,11... | collective-permute-start | bytes 6291464 | tf_op jit(solution)/shard_map/ppermute | solution.py:86
  763.3 48.8 %all-to-all-start.3 = ((bf16[32,32,1024]{2,1,0:T(8,128)(2,1)}), bf16[32,32,1024]{2,1,0:T(8,128)(2,1)}, u32[]{:S(2)}, u32[]{:S(2)}) async-start(bf16[32,32,1024]{2,1,0:T(8,128)(2,1)} %bitcast.772), calls=%async_computation.3 | async-start | bytes 4194304 | tf_op jit(solution)/shard_map/all_to_all | solution.py:144
  816.1 46.5 %collective-permute-start.56 = (bf16[256,512]{1,0:T(8,128)(2,1)S(1)}, bf16[256,512]{1,0:T(8,128)(2,1)S(1)}, u32[]{:S(2)}, u32[]{:S(2)}) collective-permute-start(bf16[256,512]{1,0:T(8,128)(2,1)S(1)} %dynamic-slice_convert_fusion.5), channel_id=1, source_target_pairs={{0,2},{2,0},{1,3},{3,1},{4,6},{6,4},{5,7},{7,5},{8,10},{10,8},{9,1... | collective-permute-start | bytes 786440 | tf_op jit(solution)/shard_map/ppermute | solution.py:86
  855.8 56.0 %collective-permute-start.84 = (bf16[2,4,64,768]{3,2,0,1:T(8,128)(2,1)}, bf16[2,4,64,768]{3,2,0,1:T(8,128)(2,1)}, u32[]{:S(2)}, u32[]{:S(2)}) collective-permute-start(bf16[2,4,64,768]{3,2,0,1:T(8,128)(2,1)} %bitcast.713), channel_id=1, source_target_pairs={{0,12},{4,0},{8,4},{12,8},{1,13},{5,1},{9,5},{13,9},{2,14},{6,2},{... | collective-permute-start | bytes 2359304 | tf_op jit(solution)/shard_map/ppermute | solution.py:86
  859.4 57.7 %collective-permute-start.83 = (bf16[2,4,64,768]{3,2,0,1:T(8,128)(2,1)}, bf16[2,4,64,768]{3,2,0,1:T(8,128)(2,1)}, u32[]{:S(2)}, u32[]{:S(2)}) collective-permute-start(bf16[2,4,64,768]{3,2,0,1:T(8,128)(2,1)} %bitcast.714), channel_id=1, source_target_pairs={{0,8},{4,12},{8,0},{12,4},{1,9},{5,13},{9,1},{13,5},{2,10},{6,14},... | collective-permute-start | bytes 2359304 | tf_op jit(solution)/shard_map/ppermute | solution.py:86
  861.9 55.2 %collective-permute-start.82 = (bf16[2,4,64,768]{3,2,0,1:T(8,128)(2,1)}, bf16[2,4,64,768]{3,2,0,1:T(8,128)(2,1)}, u32[]{:S(2)}, u32[]{:S(2)}) collective-permute-start(bf16[2,4,64,768]{3,2,0,1:T(8,128)(2,1)} %bitcast.715), channel_id=1, source_target_pairs={{0,4},{4,8},{8,12},{12,0},{1,5},{5,9},{9,13},{13,1},{2,6},{6,10},{... | collective-permute-start | bytes 2359304 | tf_op jit(solution)/shard_map/ppermute | solution.py:86
  894.1 94.4 %all-to-all-start.8 = ((bf16[32,64,576]{2,1,0:T(8,128)(2,1)}), bf16[32,64,576]{2,1,0:T(8,128)(2,1)}, u32[]{:S(2)}, u32[]{:S(2)}) async-start(bf16[32,64,576]{2,1,0:T(8,128)(2,1)} %broadcast_select_fusion), calls=%async_computation.8 | async-start | bytes 5242880 | tf_op jit(solution)/shard_map/all_to_all | solution.py:144
  905.5 45.6 %collective-permute-start.91 = (bf16[2,4,64,768]{3,2,0,1:T(8,128)(2,1)S(1)}, bf16[2,4,64,768]{3,2,0,1:T(8,128)(2,1)S(1)}, u32[]{:S(2)}, u32[]{:S(2)}) collective-permute-start(bf16[2,4,64,768]{3,2,0,1:T(8,128)(2,1)S(1)} %bitcast.787), channel_id=1, source_target_pairs={{0,48},{16,0},{32,16},{48,32},{1,49},{17,1},{33,17},{49,33},{2,50}... | collective-permute-start | bytes 2359304 | tf_op jit(solution)/shard_map/ppermute | solution.py:86
  909.7 43.6 %collective-permute-start.90 = (bf16[2,4,64,768]{3,2,0,1:T(8,128)(2,1)S(1)}, bf16[2,4,64,768]{3,2,0,1:T(8,128)(2,1)S(1)}, u32[]{:S(2)}, u32[]{:S(2)}) collective-permute-start(bf16[2,4,64,768]{3,2,0,1:T(8,128)(2,1)S(1)} %bitcast.785), channel_id=1, source_target_pairs={{0,32},{16,48},{32,0},{48,16},{1,33},{17,49},{33,1},{49,17},{2,34}... | collective-permute-start | bytes 2359304 | tf_op jit(solution)/shard_map/ppermute | solution.py:86
  911.8 60.2 %collective-permute-start.89 = (bf16[2,4,64,768]{3,2,0,1:T(8,128)(2,1)S(1)}, bf16[2,4,64,768]{3,2,0,1:T(8,128)(2,1)S(1)}, u32[]{:S(2)}, u32[]{:S(2)}) collective-permute-start(bf16[2,4,64,768]{3,2,0,1:T(8,128)(2,1)S(1)} %bitcast.786), channel_id=1, source_target_pairs={{0,16},{16,32},{32,48},{48,0},{1,17},{17,33},{33,49},{49,1},{2,18}... | collective-permute-start | bytes 2359304 | tf_op jit(solution)/shard_map/ppermute | solution.py:86
  919.2 56.5 %collective-permute-start.87 = (bf16[2,64,768]{2,1,0:T(8,128)(2,1)S(1)}, bf16[2,64,768]{2,1,0:T(8,128)(2,1)S(1)}, u32[]{:S(2)}, u32[]{:S(2)}) collective-permute-start(bf16[2,64,768]{2,1,0:T(8,128)(2,1)S(1)} %get-tuple-element.179), channel_id=1, source_target_pairs={{0,48},{16,0},{32,16},{48,32},{1,49},{17,1},{33,17},{49,33},{2,50}... | collective-permute-start | bytes 589832 | tf_op jit(solution)/shard_map/ppermute | solution.py:86
  921.7 55.0 %collective-permute-start.86 = (bf16[2,64,768]{2,1,0:T(8,128)(2,1)S(1)}, bf16[2,64,768]{2,1,0:T(8,128)(2,1)S(1)}, u32[]{:S(2)}, u32[]{:S(2)}) collective-permute-start(bf16[2,64,768]{2,1,0:T(8,128)(2,1)S(1)} %get-tuple-element.180), channel_id=1, source_target_pairs={{0,32},{16,48},{32,0},{48,16},{1,33},{17,49},{33,1},{49,17},{2,34}... | collective-permute-start | bytes 589832 | tf_op jit(solution)/shard_map/ppermute | solution.py:86
  (287 other events, 3516.2 us)

commit v2 on v1

v2 whole, which is shorter than its diff:
```python
import jax
import jax.numpy as jnp
from jax import lax
from jax.experimental import pallas as pl
from jax.experimental.pallas import tpu as pltpu
from jax.sharding import Mesh
from jax.sharding import PartitionSpec as P

WIDTH = 2048
NOPE = 128
ROPE = 64
VDIM = 128
RANK = 512
KEYS = RANK + ROPE
HEADS = 4
EXPERTS = 64
EXP_DEV = 2
CAP = 30
TOPK = 6
SLOTS = 32
BLOCK = 128
SEQ_BLOCKS = 16
SEQ_PAIRS = 8
TOK = 256
QUARTER = 512
HALF = 1024
FF_SH = 704
N_CTX = 32
CHUNK = 512
EPSILON = 1e-06
ROPE_BASE = 10000.0
SCALE = (NOPE + ROPE) ** (-0.5)
CTX = ("zh", "y", "x")
MIB = 1 << 20

bf16 = jnp.bfloat16
f32 = jnp.float32


def dot(a, b, contract):
    return lax.dot_general(a, b, ((contract[0], contract[1]), ((), ())), preferred_element_type=f32)


def nn(a, b):
    return dot(a, b, ((1,), (0,)))


def nt(a, b):
    return dot(a, b, ((1,), (1,)))


def tn(a, b):
    return dot(a, b, ((0,), (0,)))


def rotate(values, positions, direction):
    half_width = values.shape[-1] // 2
    frequency = ROPE_BASE ** (-2.0 * jnp.arange(half_width, dtype=f32) / values.shape[-1])
    angles = positions.astype(f32)[:, None] * frequency[None, :]
    target_shape = (angles.shape[0],) + (1,) * (values.ndim - 2) + (half_width,)
    cosine = jnp.cos(angles).reshape(target_shape)
    sine_part = direction * jnp.sin(angles).reshape(target_shape)
    first_half = values[..., :half_width]
    second_half = values[..., half_width:]
    return jnp.concatenate(
        [
            first_half * cosine - second_half * sine_part,
            second_half * cosine + first_half * sine_part,
        ],
        axis=-1,
    )


def silu_slope(pre_act):
    sigmoid_val = jax.nn.sigmoid(pre_act)
    return sigmoid_val * (1.0 + pre_act * (1.0 - sigmoid_val))


def norm_back(upstream, source, inverse_root, gain_vec):
    scaled = upstream * gain_vec
    return inverse_root * scaled - source * inverse_root**3 * jnp.mean(
        scaled * source, axis=-1, keepdims=True
    )


def shift(value, axis, size, step):
    return lax.ppermute(value, axis, [(i, (i + step) % size) for i in range(size)])


def swap(value, axis):
    return shift(value, axis, 2, 1)


def pick(value, index, dim):
    return lax.dynamic_index_in_dim(value, index, dim, keepdims=False)


def gather_two(value, axis, dim):
    other = swap(value, axis)
    first = lax.axis_index(axis) == 0
    return jnp.stack(
        [jnp.where(first, value, other), jnp.where(first, other, value)], axis=dim
    )


def gather_ctx(value, name):
    with jax.named_scope(name):
        gathered = lax.all_gather(value, CTX, axis=0, tiled=False)
        return gathered.reshape((2, 16) + value.shape)


def scatter_yx(value, name):
    with jax.named_scope(name):
        pair = lax.psum_scatter(value, ("y", "x"), scatter_dimension=0, tiled=True)
        return pair.reshape(2, -1, pair.shape[1])


def scatter_zh(pair, name):
    with jax.named_scope(name):
        here = lax.axis_index("zh")
        arrived = swap(pick(pair, 1 - here, 0), "zh")
        return pick(pair, here, 0).astype(f32) + arrived.astype(f32)


def after(value, earlier):
    return lax.optimization_barrier((value, earlier))[0]


def exchange_ctx(value, name, earlier=None):
    with jax.named_scope(name):
        if earlier is not None:
            value = after(value, earlier)
        return lax.all_to_all(value, CTX, 0, 0, tiled=True)


def share_ctx(value, name):
    return exchange_ctx(jnp.broadcast_to(value[None], (N_CTX,) + value.shape), name)


def half_of(value, core, dim=1):
    return jnp.concatenate(
        [
            lax.dynamic_slice_in_dim(value, core * QUARTER, QUARTER, dim),
            lax.dynamic_slice_in_dim(value, HALF + core * QUARTER, QUARTER, dim),
        ],
        axis=dim,
    )


def whole_of(own, other, core):
    first = jnp.where(core == 0, own, other)
    second = jnp.where(core == 0, other, own)
    return jnp.concatenate(
        [first[:, :QUARTER], second[:, :QUARTER], first[:, QUARTER:], second[:, QUARTER:]], axis=1
    )


def core_half(partial, core):
    arrived = swap(half_of(partial, 1 - core).astype(bf16), "core")
    return half_of(partial, core) + arrived.astype(f32)


def zl_sum(half):
    mine = half.astype(bf16)
    return mine.astype(f32) + swap(mine, "zl").astype(f32)


def zl_quarter(half, zl):
    arrived = swap(
        lax.dynamic_slice_in_dim(half, (1 - zl) * QUARTER, QUARTER, 1).astype(bf16), "zl"
    )
    return lax.dynamic_slice_in_dim(half, zl * QUARTER, QUARTER, 1) + arrived.astype(f32)


def call(body, outs, name, flops, scratch=(), limit=56):
    def run(scalars, *arrays):
        spec = pl.BlockSpec(memory_space=pltpu.VMEM)
        moved = sum(a.size * a.dtype.itemsize for a in arrays)
        moved += sum(o.size * o.dtype.itemsize for o in outs)
        return pl.pallas_call(
            body,
            in_specs=[pl.BlockSpec(memory_space=pltpu.SMEM)] + [spec] * len(arrays),
            out_specs=[spec] * len(outs),
            out_shape=outs,
            scratch_shapes=scratch,
            compiler_params=pltpu.CompilerParams(vmem_limit_bytes=limit * MIB),
            cost_estimate=pl.CostEstimate(
                flops=int(flops), bytes_accessed=int(moved), transcendentals=0
            ),
            name=name,
        )(scalars, *arrays)

    return run


def out(shape, kind):
    return jax.ShapeDtypeStruct(shape, kind)


def quarter_at(zl, core):
    return pl.ds(pl.multiple_of(zl * HALF + core * QUARTER, QUARTER), QUARTER)


def whole_value(own, other, core):
    first = jnp.where(core == 0, own, other)
    second = jnp.where(core == 0, other, own)
    return jnp.concatenate(
        [first[:, :QUARTER], second[:, :QUARTER], first[:, QUARTER:], second[:, QUARTER:]], axis=1
    )


def one_hot(slots):
    number = lax.broadcasted_iota(jnp.int32, (N_CTX, SLOTS, TOK), 1).astype(f32)
    hot = jnp.where(slots[:, None, :] == number, 1.0, 0.0)
    return hot.reshape(N_CTX * SLOTS, TOK)


def cotangents_kernel(core_ref, ids_ref, row_ref, col_ref, grad_ref, slot_ref, sent_ref):
    core = core_ref[0]
    row = lax.broadcasted_iota(jnp.int32, (EXPERTS, TOK), 0)
    expert = (row & (N_CTX - 1)) * 2 + (row >> 5)
    chosen = jnp.zeros((EXPERTS, TOK), f32)
    for k in range(TOPK):
        chosen = chosen + jnp.where(ids_ref[k : k + 1, :] == expert, 1.0, 0.0)
    before = jnp.where(col_ref[...] < row_ref[...], 1.0, 0.0).astype(bf16)
    earlier = nn(chosen.astype(bf16), before)
    slots = jnp.where((chosen > 0.5) & (earlier < CAP - 0.5), earlier, 99.0)
    slot_ref[...] = slots
    grad = jnp.concatenate([grad_ref[:, quarter_at(0, core)], grad_ref[:, quarter_at(1, core)]], 1)
    for e in range(EXP_DEV):
        hot = one_hot(slots[e * N_CTX : (e + 1) * N_CTX]).astype(bf16)
        sent_ref[:, e] = nn(hot, grad).astype(bf16).reshape(N_CTX, SLOTS, HALF)


def middle_kernel(
    core_ref, own_ref, other_ref, input_ref, gain_ref, router_ref, slot_ref,
    normed_ref, root_ref, probs_ref, sent_one_ref, sent_two_ref,
):
    core = core_ref[0]
    after = input_ref[...].astype(f32) + whole_value(own_ref[...], other_ref[...], core)
    root = lax.rsqrt(jnp.sum(after * after, axis=1, keepdims=True) * (1.0 / WIDTH) + EPSILON)
    normed = (after * root * gain_ref[...]).astype(bf16)
    normed_ref[...] = normed
    root_ref[...] = jnp.broadcast_to(root, root_ref.shape)
    logits = nt(router_ref[...], normed)
    weights = jnp.exp(logits - jnp.max(logits, axis=0, keepdims=True))
    probs = weights / jnp.sum(weights, axis=0, keepdims=True)
    probs_ref[...] = probs
    half = jnp.concatenate(
        [normed_ref[:, quarter_at(0, core)], normed_ref[:, quarter_at(1, core)]], axis=1
    )
    slot_row = lax.broadcasted_iota(jnp.int32, (N_CTX, SLOTS, HALF), 1)
    for e, sent_ref in enumerate((sent_one_ref, sent_two_ref)):
        part = slice(e * N_CTX, (e + 1) * N_CTX)
        hot = one_hot(slot_ref[part])
        gated = (hot.reshape(N_CTX, SLOTS, TOK) * probs[part][:, None, :]).astype(bf16)
        gate_row = nt(jnp.ones((8, TOK), bf16), gated.reshape(N_CTX * SLOTS, TOK))[:1]
        rows = nn(hot.astype(bf16), half).reshape(N_CTX, SLOTS, HALF)
        sent_ref[...] = jnp.where(slot_row == CAP, gate_row[None], rows).astype(bf16)


def column_of(row, ctx):
    groups = row.shape[0]
    lane = lax.broadcasted_iota(jnp.int32, (HALF, SLOTS), 0) - ctx * SLOTS
    picked = jnp.where(lane == lax.broadcasted_iota(jnp.int32, (HALF, SLOTS), 1), 1.0, 0.0)
    mine = nn(row.astype(bf16), picked.astype(bf16))
    square = (groups, SLOTS, SLOTS)
    same = lax.broadcasted_iota(jnp.int32, square, 1) == lax.broadcasted_iota(jnp.int32, square, 2)
    spread = jnp.where(same, mine[:, None, :], 0.0).reshape(groups * SLOTS, SLOTS)
    return jnp.sum(spread, axis=1, keepdims=True)


def shared_kernel(
    core_ref, normed_ref, grad_ref, weight_ref,
    own_ref, send_ref, in_own_ref, in_send_ref, grads_ref, pre_ref, back_ref,
):
    core = core_ref[0]

    def block(step):
        z, group = step // 4, lax.rem(step, 4)
        place = pl.ds(pl.multiple_of(step * 256, 256), 256)
        return z, group, place, weight_ref[pl.ds(group * 4, 4), z].reshape(256, 3 * FF_SH)

    pre_ref[...] = jnp.zeros(pre_ref.shape, f32)
    back_ref[...] = jnp.zeros(back_ref.shape, f32)

    def forward(step, carry):
        _, _, place, weight = block(step)
        pre_ref[...] += nn(normed_ref[:, place], weight[:, : 2 * FF_SH])
        back_ref[...] += nn(grad_ref[:, place], weight[:, 2 * FF_SH :])
        return carry

    lax.fori_loop(0, 8, forward, 0)
    gate, up, back = pre_ref[:, :FF_SH], pre_ref[:, FF_SH:], back_ref[...]
    sigmoid = 1.0 / (1.0 + jnp.exp(-gate))
    act = gate * sigmoid
    hidden = (act * up).astype(bf16)
    grad_gate = back * up * (sigmoid * (1.0 + gate * (1.0 - sigmoid)))
    grad_pre = jnp.concatenate([grad_gate, back * act], axis=1).astype(bf16)

    def backward(step, carry):
        z, group, place, weight = block(step)
        grads_ref[pl.ds(group * 4, 4), z, :, : 2 * FF_SH] = (
            tn(normed_ref[:, place], grad_pre).astype(bf16).reshape(4, 64, 2 * FF_SH)
        )
        grads_ref[pl.ds(group * 4, 4), z, :, 2 * FF_SH :] = (
            tn(grad_ref[:, place], hidden).astype(bf16).reshape(4, 64, FF_SH)
        )
        shared = nt(hidden, weight[:, 2 * FF_SH :])
        inner = nt(grad_pre, weight[:, : 2 * FF_SH])
        column = pl.ds(pl.multiple_of(z * QUARTER + lax.rem(group, 2) * 256, 256), 256)

        @pl.when(group // 2 == core)
        def _():
            own_ref[:, column] = shared
            in_own_ref[:, column] = inner

        @pl.when(group // 2 != core)
        def _():
            send_ref[:, column] = shared.astype(bf16)
            in_send_ref[:, column] = inner.astype(bf16)

        return carry

    lax.fori_loop(0, 8, backward, 0)


def shared(core, normed_two, grad_out, weights):
    run = pl.pallas_call(
        shared_kernel,
        in_specs=[pl.BlockSpec(memory_space=pltpu.SMEM)]
        + [pl.BlockSpec(memory_space=pltpu.VMEM)] * 3,
        out_specs=[pl.BlockSpec(memory_space=pltpu.VMEM)] * 5,
        out_shape=[
            out((TOK, HALF), f32),
            out((TOK, HALF), bf16),
            out((TOK, HALF), f32),
            out((TOK, HALF), bf16),
            out((16, 2, 64, 3 * FF_SH), bf16),
        ],
        scratch_shapes=[pltpu.VMEM((TOK, 2 * FF_SH), f32), pltpu.VMEM((TOK, FF_SH), f32)],
        compiler_params=pltpu.CompilerParams(vmem_limit_bytes=56 * MIB),
        cost_estimate=pl.CostEstimate(
            flops=18 * TOK * WIDTH * FF_SH, bytes_accessed=24 * MIB, transcendentals=0
        ),
        name="shared_experts",
    )
    return run(core, normed_two, grad_out, weights)


def expert_kernel(
    core_ref, own_ref, other_ref, grad_own_ref, grad_other_ref, wg_ref, wu_ref, wd_ref,
    back_own_ref, back_send_ref, y_own_ref, y_send_ref, dot_ref, scaled_ref, dg_ref, du_ref,
):
    core = core_ref[0]
    groups = own_ref.shape[0]
    rows = groups * SLOTS
    gate = jnp.zeros((rows, 352), f32)
    up = jnp.zeros((rows, 352), f32)
    plain = jnp.zeros((rows, 352), f32)
    for z in range(2):
        mine = slice(z * QUARTER, (z + 1) * QUARTER)
        for x_ref, g_ref, which in (
            (own_ref, grad_own_ref, core), (other_ref, grad_other_ref, 1 - core),
        ):
            place = quarter_at(z, which)
            x = x_ref[:, :, mine].reshape(rows, QUARTER)
            gate = gate + nt(x, wg_ref[0, :, place])
            up = up + nt(x, wu_ref[0, :, place])
            plain = plain + nt(g_ref[:, 0, :, mine].reshape(rows, QUARTER), wd_ref[0, :, place])
    sigmoid = 1.0 / (1.0 + jnp.exp(-gate))
    act = gate * sigmoid
    hidden = (act * up).astype(bf16)
    weight = column_of(own_ref[:, CAP, :], core_ref[1])
    scaled_ref[...] = (hidden.astype(f32) * weight).astype(bf16)
    dot_ref[...] = nt(jnp.ones((8, 352), bf16), (hidden.astype(f32) * plain).astype(bf16))
    back = plain * weight
    dg = (back * up * (sigmoid * (1.0 + gate * (1.0 - sigmoid)))).astype(bf16)
    du = (back * act).astype(bf16)
    dg_ref[...] = dg
    du_ref[...] = du
    for z in range(2):
        mine = slice(z * QUARTER, (z + 1) * QUARTER)
        for back_ref, y_ref, which in (
            (back_own_ref, y_own_ref, core), (back_send_ref, y_send_ref, 1 - core),
        ):
            place = quarter_at(z, which)
            part = nn(dg, wg_ref[0, :, place]) + nn(du, wu_ref[0, :, place])
            back_ref[:, :, mine] = part.astype(bf16).reshape(groups, SLOTS, QUARTER)
            part = nn(hidden, wd_ref[0, :, place])
            y_ref[:, :, mine] = part.astype(bf16).reshape(groups, SLOTS, QUARTER)


def expert(e, core, own, other, grad_own, grad_other, wg, wu, wd):
    total, step = N_CTX * SLOTS, 512
    rows = pl.BlockSpec((step // SLOTS, SLOTS, HALF), lambda i: (i, 0, 0))
    grads = pl.BlockSpec((step // SLOTS, 1, SLOTS, HALF), lambda i: (i, e, 0, 0))
    weight = pl.BlockSpec((1, 352, WIDTH), lambda i: (e, 0, 0))
    units = pl.BlockSpec((step, 352), lambda i: (i, 0))
    return pl.pallas_call(
        expert_kernel,
        grid=(total // step,),
        in_specs=[pl.BlockSpec(memory_space=pltpu.SMEM), rows, rows, grads, grads]
        + [weight] * 3,
        out_specs=[rows] * 4 + [pl.BlockSpec((8, step), lambda i: (0, i))] + [units] * 3,
        out_shape=[out((N_CTX, SLOTS, HALF), bf16)] * 4
        + [out((8, total), f32)] + [out((total, 352), bf16)] * 3,
        compiler_params=pltpu.CompilerParams(vmem_limit_bytes=56 * MIB),
        cost_estimate=pl.CostEstimate(
            flops=12 * total * WIDTH * 352, bytes_accessed=24 * MIB, transcendentals=0
        ),
        name="expert",
    )(core, own, other, grad_own, grad_other, wg, wu, wd)


def finish_rows_kernel(core_ref, own_ref, arrived_ref, dot_ref, dot_arrived_ref, sent_ref):
    slot_row = lax.broadcasted_iota(jnp.int32, (N_CTX, SLOTS, HALF), 1)
    rows = own_ref[...].astype(f32) + arrived_ref[...].astype(f32)
    dots = (dot_ref[:1] + dot_arrived_ref[:1]).reshape(1, 1, HALF)
    sent_ref[...] = jnp.where(slot_row == CAP, dots, rows).astype(bf16)


def add_kernel(core_ref, own_ref, arrived_ref, sum_ref):
    sum_ref[...] = (own_ref[...].astype(f32) + arrived_ref[...].astype(f32)).astype(bf16)


def keys_kernel(slot_ref, own_ref, zl_ref, core_ref, keys_ref):
    zl, core = slot_ref[SEQ_BLOCKS], slot_ref[SEQ_BLOCKS + 1]

    def block(place, carry):
        slot = slot_ref[place]
        half, pair = slot // SEQ_PAIRS, lax.rem(slot, SEQ_PAIRS)
        mine = jnp.where(half == zl, own_ref[pair], zl_ref[pair])
        other = core_ref[jnp.where(half == zl, 0, 1), pair]
        start = pl.multiple_of(place * BLOCK, BLOCK)
        here = pl.multiple_of(start + core * 64, 64)
        there = pl.multiple_of(start + (1 - core) * 64, 64)
        keys_ref[pl.ds(here, 64), :] = mine
        keys_ref[pl.ds(there, 64), :] = other
        return carry

    lax.fori_loop(0, SEQ_BLOCKS, block, 0)


def key_split_kernel(place_ref, own_ref, arrived_ref, mine_ref, sent_ref):
    zl = place_ref[SEQ_BLOCKS]

    def pair(i, carry):
        here, there = place_ref[zl * SEQ_PAIRS + i], place_ref[(1 - zl) * SEQ_PAIRS + i]
        mine_ref[i] = own_ref[here].astype(f32) + arrived_ref[here].astype(f32)
        sent_ref[i] = (own_ref[there].astype(f32) + arrived_ref[there].astype(f32)).astype(bf16)
        return carry

    lax.fori_loop(0, SEQ_PAIRS, pair, 0)


def key_spread_kernel(pair_ref, mine_ref, arrived_ref, sent_ref):
    sent_ref[...] = jnp.zeros(sent_ref.shape, bf16)

    def pair(i, carry):
        sent_ref[pair_ref[i]] = (mine_ref[i] + arrived_ref[i].astype(f32)).astype(bf16)
        return carry

    lax.fori_loop(0, SEQ_PAIRS, pair, 0)


def latent_back_kernel(
    core_ref, back_ref, pre_ref, root_ref, gain_ref, cos_ref, sin_ref, grad_ref, gain_grad_ref
):
    total = jnp.zeros((64, KEYS), f32)
    for i in range(N_CTX):
        total = total + back_ref[i].astype(f32)
    normed_grad, pre, root = total[:, :RANK], pre_ref[...], root_ref[...]
    gain_grad_ref[...] = jnp.sum(normed_grad * pre * root, axis=0, keepdims=True)
    scaled = normed_grad * gain_ref[...]
    mean = jnp.sum(scaled * pre, axis=1, keepdims=True) * (1.0 / RANK)
    grad_ref[:, :RANK] = (root * scaled - pre * (root * root * root * mean)).astype(bf16)
    grad_ref[:, RANK:] = turned(total[:, RANK:], cos_ref[...], -sin_ref[...]).astype(bf16)


def input_back_kernel(
    core_ref, compressed_ref, down_ref, normed_ref, part_ref, input_ref, root_ref, gain_ref,
    own_ref, send_ref, gain_grad_ref, down_grad_ref, total_ref,
):
    core, zl = core_ref[0], core_ref[1]
    quarter = quarter_at(zl, core)
    compressed = compressed_ref[...]
    down_grad_ref[...] = tn(compressed, normed_ref[:, quarter]).astype(bf16)
    total_ref[...] = part_ref[...]
    total_ref[:, quarter] += nn(compressed, down_ref[...])
    grad, source, root = total_ref[...], input_ref[...].astype(f32), root_ref[...]
    gain_grad_ref[...] = jnp.sum(grad * source * root, axis=0, keepdims=True)
    scaled = grad * gain_ref[...]
    mean = jnp.sum(scaled * source, axis=1, keepdims=True) * (1.0 / WIDTH)
    total_ref[...] = root * scaled - source * (root * root * root * mean)
    for z in range(2):
        mine = slice(z * QUARTER, (z + 1) * QUARTER)
        own_ref[:, mine] = total_ref[:, quarter_at(z, core)]
        send_ref[:, mine] = total_ref[:, quarter_at(z, 1 - core)].astype(bf16)


def expert_grads_kernel(
    core_ref, one_ref, one_other_ref, two_ref, two_other_ref, ga_ref, gb_ref,
    scaled_one_ref, dg_one_ref, du_one_ref, scaled_two_ref, dg_two_ref, du_two_ref,
    wg_ref, wu_ref, wd_ref,
):
    mine = lax.rem(pl.program_id(1), 2) == core_ref[0]
    rows = N_CTX * SLOTS
    grad = jnp.where(mine, ga_ref[...], gb_ref[...]).reshape(rows, QUARTER)
    for e, (own_ref, other_ref, scaled_ref, dg_ref, du_ref) in enumerate(
        (
            (one_ref, one_other_ref, scaled_one_ref, dg_one_ref, du_one_ref),
            (two_ref, two_other_ref, scaled_two_ref, dg_two_ref, du_two_ref),
        )
    ):

        @pl.when(pl.program_id(0) == e)
        def _(own_ref=own_ref, other_ref=other_ref, scaled_ref=scaled_ref, dg_ref=dg_ref,
              du_ref=du_ref):
            x = jnp.where(mine, own_ref[...], other_ref[...]).reshape(rows, QUARTER)
            wg_ref[0] = tn(dg_ref[...], x)
            wu_ref[0] = tn(du_ref[...], x)
            wd_ref[0] = tn(scaled_ref[...], grad)


def expert_grads(core, rows, grads, units):
    total = N_CTX * SLOTS
    first = pl.BlockSpec(
        (N_CTX, SLOTS, QUARTER), lambda e, q: (0, 0, jnp.where(e == 0, q // 2, 1))
    )
    second = pl.BlockSpec(
        (N_CTX, SLOTS, QUARTER), lambda e, q: (0, 0, jnp.where(e == 0, 0, q // 2))
    )
    grad = pl.BlockSpec((N_CTX, 1, SLOTS, QUARTER), lambda e, q: (0, e, 0, q // 2))
    unit = pl.BlockSpec((total, 352), lambda e, q: (0, 0))
    result = pl.BlockSpec((1, 352, QUARTER), lambda e, q: (e, 0, q))
    return pl.pallas_call(
        expert_grads_kernel,
        grid=(EXP_DEV, 4),
        in_specs=[pl.BlockSpec(memory_space=pltpu.SMEM), first, first, second, second, grad, grad]
        + [unit] * 6,
        out_specs=[result] * 3,
        out_shape=[out((EXP_DEV, 352, WIDTH), f32)] * 3,
        compiler_params=pltpu.CompilerParams(vmem_limit_bytes=56 * MIB),
        cost_estimate=pl.CostEstimate(
            flops=12 * total * WIDTH * 352, bytes_accessed=36 * MIB, transcendentals=0
        ),
        name="expert_grads",
    )(core, *rows, *grads, *units)


def combine_kernel(
    core_ref, one_ref, two_ref, slot_ref, own_ref, arrived_ref, half_ref, prob_ref
):
    half = own_ref[...] + arrived_ref[...].astype(f32)
    for e, back_ref in enumerate((one_ref, two_ref)):
        part = slice(e * N_CTX, (e + 1) * N_CTX)
        hot = one_hot(slot_ref[part])
        half = half + tn(hot.astype(bf16), back_ref[...].reshape(N_CTX * SLOTS, HALF))
        dots = column_of(back_ref[:, CAP, :], core_ref[1])
        prob_ref[part] = jnp.sum((hot * dots).reshape(N_CTX, SLOTS, TOK), axis=1)
    half_ref[...] = half.astype(bf16)


def outputs_kernel(core_ref, back_ref, slot_ref, probs_ref, own_ref, arrived_ref, half_ref):
    hot = one_hot(slot_ref[...]).reshape(N_CTX, SLOTS, TOK) * probs_ref[...][:, None, :]
    half = own_ref[...] + arrived_ref[...].astype(f32)
    half_ref[...] = half + tn(
        hot.reshape(N_CTX * SLOTS, TOK).astype(bf16), back_ref[...].reshape(N_CTX * SLOTS, HALF)
    )


def weight_rows(attn_ref, z, group, first, last):
    return attn_ref[z, group * 4 : group * 4 + 4, :, first:last].reshape(256, last - first)


def up_rows(attn_ref, z, head, first):
    rows = attn_ref[z, :, head * 16 : head * 16 + 16, first : first + 128]
    return rows.reshape(256, 128)


def turned(values, cos, sin):
    flipped = jnp.concatenate([values[:, ROPE // 2 :], values[:, : ROPE // 2]], axis=1)
    return values * cos + flipped * sin


def query_kernel(core_ref, normed_ref, attn_ref, cos_ref, sin_ref, query_ref, nope_ref):
    rows = jnp.zeros((TOK, 768), f32)
    for z in range(2):
        for group in range(4):
            place = (z * 4 + group) * 256
            rows = rows + nn(
                normed_ref[:, place : place + 256], weight_rows(attn_ref, z, group, 0, 768)
            )
    for h in range(HEADS):
        nope = rows[:, h * 192 : h * 192 + NOPE].astype(bf16)
        rope = turned(rows[:, h * 192 + NOPE : (h + 1) * 192], cos_ref[...], sin_ref[...])
        nope_ref[h] = nope
        for z in range(2):
            query_ref[h, :, z * 256 : (z + 1) * 256] = nt(
                nope, up_rows(attn_ref, z, h, 1280)
            ).astype(bf16)
        query_ref[h, :, RANK:] = rope.astype(bf16)


def attend_kernel(
    place_ref, q_ref, k_ref, attn_ref,
    out_ref, log_ref, flat_ref, own_ref, send_ref, top_ref, sum_ref, acc_ref,
):
    owner, chunk = pl.program_id(0), pl.program_id(1)
    place, core = place_ref[owner], place_ref[2]

    @pl.when(chunk == 0)
    def _():
        top_ref[...] = jnp.full(top_ref.shape, -1e30, f32)
        sum_ref[...] = jnp.zeros(sum_ref.shape, f32)
        acc_ref[...] = jnp.zeros(acc_ref.shape, f32)

    @pl.when(chunk * (CHUNK // BLOCK) <= place)
    def _():
        q = q_ref[...].reshape(HEADS * BLOCK, KEYS)
        k = k_ref[pl.ds(chunk * CHUNK, CHUNK), :]
        scores = nt(q, k) * SCALE
        column = lax.broadcasted_iota(jnp.int32, scores.shape, 1) + chunk * CHUNK
        scores = jnp.where(column < (place + 1) * BLOCK, scores, -1e30)
        top_old = top_ref[...][:, :1]
        top = jnp.maximum(top_old, jnp.max(scores, axis=1, keepdims=True))
        weights = jnp.exp(scores - top)
        fade = jnp.exp(top_old - top)
        total = sum_ref[...][:, :1] * fade + jnp.sum(weights, axis=1, keepdims=True)
        acc_ref[...] = acc_ref[...] * fade + nn(weights.astype(bf16), k[:, :RANK])
        top_ref[...] = jnp.broadcast_to(top, top_ref.shape)
        sum_ref[...] = jnp.broadcast_to(total, sum_ref.shape)

    @pl.when(chunk == pl.num_programs(1) - 1)
    def _():
        total = sum_ref[...][:, :1]
        value = acc_ref[...] / total
        out_ref[...] = value.reshape(out_ref.shape)
        log_ref[...] = (top_ref[...] + jnp.log(sum_ref[...])).reshape(log_ref.shape)
        value = value.astype(bf16)
        for h in range(HEADS):
            rows = value[h * BLOCK : (h + 1) * BLOCK]
            head = nn(rows[:, :256], up_rows(attn_ref, 0, h, 1408))
            head = head + nn(rows[:, 256:], up_rows(attn_ref, 1, h, 1408))
            flat_ref[:, h * VDIM : (h + 1) * VDIM] = head.astype(bf16)
        flat = flat_ref[...]
        for z in range(2):
            mine = slice(z * QUARTER, (z + 1) * QUARTER)
            weight = attn_ref[z, pl.ds(core * 8, 8), :, 768:1280].reshape(QUARTER, QUARTER)
            own_ref[:, mine] = nt(flat, weight)
            weight = attn_ref[z, pl.ds(8 - core * 8, 8), :, 768:1280].reshape(QUARTER, QUARTER)
            send_ref[:, mine] = nt(flat, weight).astype(bf16)


def attend(places, query, keys, attn_all):
    rows = HEADS * BLOCK
    tokens = pl.BlockSpec((BLOCK, HALF), lambda o, c, p: (o, 0))
    return pl.pallas_call(
        attend_kernel,
        grid_spec=pltpu.PrefetchScalarGridSpec(
            num_scalar_prefetch=1,
            grid=(2, SEQ_BLOCKS * BLOCK // CHUNK),
            in_specs=[
                pl.BlockSpec((HEADS, 1, BLOCK, KEYS), lambda o, c, p: (0, o, 0, 0)),
                pl.BlockSpec((SEQ_BLOCKS * BLOCK, KEYS), lambda o, c, p: (0, 0)),
                pl.BlockSpec((2, 16, 64, 1536), lambda o, c, p: (0, 0, 0, 0)),
            ],
            out_specs=[
                pl.BlockSpec((HEADS, 1, BLOCK, RANK), lambda o, c, p: (0, o, 0, 0)),
                pl.BlockSpec((HEADS, 1, BLOCK, BLOCK), lambda o, c, p: (0, o, 0, 0)),
                pl.BlockSpec((BLOCK, HEADS * VDIM), lambda o, c, p: (o, 0)),
                tokens,
                tokens,
            ],
            scratch_shapes=[
                pltpu.VMEM((rows, 128), f32),
                pltpu.VMEM((rows, 128), f32),
                pltpu.VMEM((rows, RANK), f32),
            ],
        ),
        out_shape=[
            out((HEADS, 2, BLOCK, RANK), f32),
            out((HEADS, 2, BLOCK, BLOCK), f32),
            out((TOK, HEADS * VDIM), bf16),
            out((TOK, HALF), f32),
            out((TOK, HALF), bf16),
        ],
        compiler_params=pltpu.CompilerParams(vmem_limit_bytes=56 * MIB),
        cost_estimate=pl.CostEstimate(
            flops=2 * 2 * rows * 1280 * (KEYS + RANK), bytes_accessed=16 * MIB, transcendentals=0
        ),
        name="attend",
    )(places, query, keys, attn_all)


def back_kernel(
    core, own_ref, other_ref, sum_own_ref, sum_other_ref, input_ref, root_ref, gain_ref,
    grad_ref, router_ref, probs_ref, prob_grad_ref, attn_ref,
    after_grad_ref, attn_grad_ref, logit_ref, gain_grad_ref, head_ref, latent_ref,
):
    probs, prob_grad = probs_ref[...], prob_grad_ref[...]
    inner = jnp.sum(probs * prob_grad, axis=0, keepdims=True)
    logit_grad = (probs * (prob_grad - inner)).astype(bf16)
    logit_ref[...] = logit_grad
    after = input_ref[...].astype(f32) + whole_value(sum_own_ref[...], sum_other_ref[...], core)
    normed_grad = whole_value(own_ref[...], other_ref[...], core)
    normed_grad = normed_grad + tn(logit_grad, router_ref[...])
    root = root_ref[:, :1]
    gain_grad_ref[...] = jnp.sum(normed_grad * after * root, axis=0, keepdims=True)
    scaled = normed_grad * gain_ref[...]
    mean = jnp.sum(scaled * after, axis=1, keepdims=True) * (1.0 / WIDTH)
    after_grad = grad_ref[...].astype(f32) + root * scaled - after * (root * root * root * mean)
    after_grad_ref[...] = after_grad
    attn_grad = after_grad.astype(bf16)
    attn_grad_ref[...] = attn_grad
    head = jnp.zeros((TOK, QUARTER), f32)
    for z in range(2):
        for group in range(4):
            place = (z * 4 + group) * 256
            head = head + nn(
                attn_grad[:, place : place + 256], weight_rows(attn_ref, z, group, 768, 1280)
            )
    head = head.astype(bf16)
    head_ref[...] = head
    for h in range(HEADS):
        for z in range(2):
            latent_ref[h, :, z * 256 : (z + 1) * 256] = nt(
                head[:, h * VDIM : (h + 1) * VDIM], up_rows(attn_ref, z, h, 1408)
            ).astype(bf16)


def query_back_kernel(
    core_ref, dq_ref, nope_ref, normed_ref, attn_ref, cos_ref, sin_ref,
    value_ref, head_ref, attn_grad_ref, flat_ref, sums_ref, back_ref,
):
    parts = []
    for h in range(HEADS):
        lat = dq_ref[h, :, :RANK].astype(bf16)
        nope = nn(lat[:, :256], up_rows(attn_ref, 0, h, 1280))
        nope = nope + nn(lat[:, 256:], up_rows(attn_ref, 1, h, 1280))
        parts += [nope, turned(dq_ref[h, :, RANK:], cos_ref[...], -sin_ref[...])]
        heads = slice(h * 16, h * 16 + 16)
        key_grad = tn(lat, nope_ref[h]).astype(bf16)
        value_grad = tn(value_ref[h].astype(bf16), head_ref[:, h * VDIM : (h + 1) * VDIM])
        value_grad = value_grad.astype(bf16)
        for z in range(2):
            rows = slice(z * 256, (z + 1) * 256)
            sums_ref[:, z, heads, 1280:1408] = key_grad[rows].reshape(16, 16, 128)
            sums_ref[:, z, heads, 1408:1536] = value_grad[rows].reshape(16, 16, 128)
    query_grad = jnp.concatenate(parts, axis=1).astype(bf16)
    flat = flat_ref[...]
    for z in range(2):
        for group in range(4):
            place = slice((z * 4 + group) * 256, (z * 4 + group + 1) * 256)
            where = slice(group * 4, group * 4 + 4)
            sums_ref[where, z, :, :768] = (
                tn(normed_ref[:, place], query_grad).astype(bf16).reshape(4, 64, 768)
            )
            sums_ref[where, z, :, 768:1280] = (
                tn(attn_grad_ref[:, place], flat).astype(bf16).reshape(4, 64, QUARTER)
            )
            back_ref[:, place] = nt(query_grad, weight_rows(attn_ref, z, group, 0, 768))


def attend_back_kernel(
    place_ref, in_own_ref, in_other_ref, sum_own_ref, sum_other_ref, input_ref, root_ref, gain_ref,
    grad_ref, router_ref, probs_ref, prob_grad_ref, attn_ref, q_ref, k_ref, out_ref, log_ref,
    after_grad_ref, attn_grad_ref, logit_ref, gain_grad_ref, head_ref,
    dq_ref, own_ref, send_ref, latent_ref, inner_ref, dk_ref,
):
    owner, chunk = pl.program_id(0), pl.program_id(1)
    place, core = place_ref[owner], place_ref[2]
    rows = HEADS * BLOCK

    @pl.when((owner == 0) & (chunk == 0))
    def _():
        dk_ref[...] = jnp.zeros(dk_ref.shape, f32)
        back_kernel(
            core, in_own_ref, in_other_ref, sum_own_ref, sum_other_ref, input_ref, root_ref,
            gain_ref, grad_ref, router_ref, probs_ref, prob_grad_ref, attn_ref,
            after_grad_ref, attn_grad_ref, logit_ref, gain_grad_ref, head_ref, latent_ref,
        )

    tokens = pl.ds(pl.multiple_of(owner * BLOCK, BLOCK), BLOCK)

    @pl.when(chunk == 0)
    def _():
        dq_ref[...] = jnp.zeros(dq_ref.shape, f32)
        grad = latent_ref[:, tokens, :].reshape(rows, RANK)
        inner = jnp.sum(
            grad.astype(f32) * out_ref[...].reshape(rows, RANK), axis=1, keepdims=True
        )
        inner_ref[...] = jnp.broadcast_to(inner, inner_ref.shape)

    @pl.when(chunk * (CHUNK // BLOCK) <= place)
    def _():
        q = q_ref[...].reshape(rows, KEYS)
        grad = latent_ref[:, tokens, :].reshape(rows, RANK)
        part = pl.ds(chunk * CHUNK, CHUNK)
        k = k_ref[part, :]
        scores = nt(q, k) * SCALE
        column = lax.broadcasted_iota(jnp.int32, scores.shape, 1) + chunk * CHUNK
        log_total = log_ref[...].reshape(rows, BLOCK)[:, :1]
        probs = jnp.where(column < (place + 1) * BLOCK, jnp.exp(scores - log_total), 0.0)
        prob_back = nt(grad, k[:, :RANK])
        score_grad = (probs * (prob_back - inner_ref[...][:, :1])).astype(bf16)
        dq_ref[...] += (nn(score_grad, k) * SCALE).reshape(dq_ref.shape)
        dk_ref[part, :] += tn(score_grad, q) * SCALE
        dk_ref[part, :RANK] += tn(probs.astype(bf16), grad)

    @pl.when((owner == 1) & (chunk == pl.num_programs(1) - 1))
    def _():
        def block(i, carry):
            start = i * BLOCK
            own_ref[i] = dk_ref[pl.ds(pl.multiple_of(start + core * 64, 64), 64), :].astype(bf16)
            send_ref[i] = dk_ref[
                pl.ds(pl.multiple_of(start + (1 - core) * 64, 64), 64), :
            ].astype(bf16)
            return carry

        lax.fori_loop(0, SEQ_BLOCKS, block, 0)


def attend_back(places, *arrays):
    rows = HEADS * BLOCK

    def whole(array):
        zeros = (0,) * len(array.shape)
        return pl.BlockSpec(
            array.shape, lambda o, c, p: zeros, pipeline_mode=pl.Buffered(buffer_count=1)
        )

    def per_owner(width):
        return pl.BlockSpec((HEADS, 1, BLOCK, width), lambda o, c, p: (0, o, 0, 0))

    results = [
        out((TOK, WIDTH), f32),
        out((TOK, WIDTH), bf16),
        out((EXPERTS, TOK), bf16),
        out((1, WIDTH), f32),
        out((TOK, QUARTER), bf16),
    ]
    halves = [out((SEQ_BLOCKS, 64, KEYS), bf16)] * 2
    return pl.pallas_call(
        attend_back_kernel,
        grid_spec=pltpu.PrefetchScalarGridSpec(
            num_scalar_prefetch=1,
            grid=(2, SEQ_BLOCKS * BLOCK // CHUNK),
            in_specs=[whole(a) for a in arrays[:12]]
            + [per_owner(KEYS), whole(arrays[13]), per_owner(RANK), per_owner(BLOCK)],
            out_specs=[whole(a) for a in results] + [per_owner(KEYS)] + [whole(a) for a in halves],
            scratch_shapes=[
                pltpu.VMEM((HEADS, TOK, RANK), bf16),
                pltpu.VMEM((rows, 128), f32),
                pltpu.VMEM((SEQ_BLOCKS * BLOCK, KEYS), f32),
            ],
        ),
        out_shape=results + [out((HEADS, 2, BLOCK, KEYS), f32)] + halves,
        compiler_params=pltpu.CompilerParams(vmem_limit_bytes=58 * MIB),
        cost_estimate=pl.CostEstimate(
            flops=2 * 2 * rows * 1280 * 5 * KEYS, bytes_accessed=36 * MIB, transcendentals=0
        ),
        name="attend_back",
    )(places, *arrays)


def on_device(
    hidden_in,
    grad_out,
    block_ids,
    expert_ids,
    claim_order,
    attn_gain,
    latent_gain,
    ffn_gain,
    query_weight,
    latent_down,
    latent_up,
    output_weight,
    router_weight,
    expert_gate,
    expert_up,
    expert_down,
    shared_gate,
    shared_up,
    shared_down,
):
    ctx = lax.axis_index(CTX)
    zl = lax.axis_index("zl")
    core = lax.axis_index("core")
    ws = zl * 2 + core
    column_start = ws * QUARTER

    gains = jnp.concatenate([attn_gain, latent_gain, ffn_gain])
    gains = gather_two(gather_two(gains, "core", 0), "zl", 0).reshape(-1)
    small = jnp.concatenate(
        [
            latent_down.T,
            router_weight.T,
            jnp.pad(gains, (0, QUARTER - gains.shape[0]))[None],
            jnp.zeros((3, QUARTER), bf16),
        ],
        axis=0,
    )
    small_all = share_ctx(small, "small_weights")
    down_t = small_all[:, :18].reshape(KEYS, QUARTER)
    gains_all = small_all[:, 20, : 4 * 36].reshape(N_CTX, 4, 36).astype(f32)
    gain_one = gains_all[..., :16].reshape(-1)
    gain_kv = gains_all[..., 16:20].reshape(-1)
    gain_two = gains_all[..., 20:].reshape(-1)
    router_mine = small_all[:, 18:20]

    shared_pair_mine = gather_two(
        jnp.concatenate([shared_gate, shared_up, shared_down.T], axis=1), "zh", 0
    )
    up_mine = latent_up.reshape(16, HEADS, NOPE + VDIM).transpose(1, 0, 2).reshape(64, NOPE + VDIM)
    attn_all = gather_ctx(
        jnp.concatenate([query_weight, output_weight.T, up_mine], axis=1), "attn_weights"
    )

    core_is = jnp.stack([core, ctx])
    slot_by, grad_sent = call(
        cotangents_kernel,
        [out((EXPERTS, TOK), f32), out((N_CTX, EXP_DEV, SLOTS, HALF), bf16)],
        "cotangents",
        4 * N_CTX * SLOTS * TOK * HALF,
    )(
        core_is,
        jnp.pad(expert_ids.T, ((0, 2), (0, 0)), constant_values=-1),
        claim_order.reshape(1, TOK),
        claim_order.reshape(TOK, 1),
        grad_out,
    )

    local_ids = lax.dynamic_slice_in_dim(block_ids, ctx * 2, 2)
    places = local_ids % SEQ_BLOCKS
    sequence = local_ids[0] // SEQ_BLOCKS
    positions = (places[:, None] * BLOCK + jnp.arange(BLOCK)[None, :]).reshape(-1)
    pair_ids = block_ids.reshape(N_CTX, 2)
    in_seq = (pair_ids[:, 0] // SEQ_BLOCKS) == sequence
    rank = jnp.cumsum(in_seq.astype(jnp.int32)) - 1
    is_pair = in_seq[None, :] & (rank[None, :] == jnp.arange(SEQ_PAIRS)[:, None])
    pairs = jnp.sum(jnp.where(is_pair, jnp.arange(N_CTX)[None, :], 0), axis=1)
    pair_places = pair_ids[pairs] % SEQ_BLOCKS
    place_of = pair_places.T.reshape(-1)
    slot_of = jnp.sum(
        jnp.where(
            place_of[None, :] == jnp.arange(SEQ_BLOCKS)[:, None],
            jnp.arange(SEQ_BLOCKS)[None, :],
            0,
        ),
        axis=1,
    )

    inputs = hidden_in.astype(f32)
    root_one = lax.rsqrt(jnp.mean(inputs * inputs, axis=-1, keepdims=True) + EPSILON)
    normed_one = (inputs * root_one * gain_one).astype(bf16)
    normed_quarter = lax.dynamic_slice_in_dim(normed_one, column_start, QUARTER, 1)
    compressed_part = nt(normed_quarter, down_t).reshape(2, 2, 64, KEYS)
    compressed_half = pick(compressed_part, core, 1) + swap(
        pick(compressed_part, 1 - core, 1), "core"
    )
    compressed = pick(compressed_half, zl, 0) + swap(pick(compressed_half, 1 - zl, 0), "zl")
    row_start = ws * 64
    my_positions = lax.dynamic_slice_in_dim(positions, row_start, 64)
    latent_pre = compressed[:, :RANK]
    root_kv = lax.rsqrt(jnp.mean(latent_pre * latent_pre, axis=-1, keepdims=True) + EPSILON)
    latent_rows = jnp.concatenate(
        [
            (latent_pre * root_kv * gain_kv).astype(bf16),
            rotate(compressed[:, RANK:], my_positions, 1.0).astype(bf16),
        ],
        axis=1,
    )
    latent_ctx = after(share_ctx(latent_rows, "latents"), grad_sent)
    latent_mine = latent_ctx[pairs]
    latent_zl = swap(latent_mine, "zl")
    latent_core = swap(jnp.stack([latent_mine, latent_zl]), "core")
    (keys,) = call(keys_kernel, [out((SEQ_BLOCKS * BLOCK, KEYS), bf16)], "keys", 1)(
        jnp.concatenate([slot_of, jnp.stack([zl, core])]), latent_mine, latent_zl, latent_core
    )

    frequency = ROPE_BASE ** (-2.0 * jnp.arange(ROPE // 2, dtype=f32) / ROPE)
    angles = positions.astype(f32)[:, None] * frequency[None, :]
    cos = jnp.cos(angles)
    sin = jnp.sin(angles)
    cos, sin = jnp.concatenate([cos, cos], axis=1), jnp.concatenate([-sin, sin], axis=1)
    query, query_nope = call(
        query_kernel,
        [out((HEADS, TOK, KEYS), bf16), out((HEADS, TOK, NOPE), bf16)],
        "queries",
        2 * TOK * 768 * (WIDTH + RANK),
    )(core_is, normed_one, attn_all, cos, sin)
    query = query.reshape(HEADS, 2, BLOCK, KEYS)
    grad_own = exchange_ctx(grad_sent, "cotangent_rows", latent_core)
    grad_other = swap(grad_own, "core")
    places_core = jnp.concatenate([places, core[None]])
    value, log_total, head_flat, attn_own, attn_send = attend(places_core, query, keys, attn_all)
    attn_half = zl_sum(attn_own + swap(attn_send, "core").astype(f32))
    attn_other = swap(attn_half, "core")

    router_t = gather_two(gather_two(after(router_mine, keys), "zl", 0), "core", 1)
    router_t = router_t.transpose(3, 2, 0, 1, 4).reshape(EXPERTS, WIDTH)

    gain_row = gain_two.reshape(1, WIDTH)
    buffer = out((N_CTX, SLOTS, HALF), bf16)
    normed_two, root_two, probs, sent_one, sent_two = call(
        middle_kernel,
        [
            out((TOK, WIDTH), bf16),
            out((TOK, 128), f32),
            out((EXPERTS, TOK), f32),
            buffer,
            buffer,
        ],
        "middle",
        4 * N_CTX * SLOTS * TOK * HALF,
    )(core_is, attn_half, attn_other, hidden_in, gain_row, router_t, slot_by)

    weights = (expert_gate.transpose(0, 2, 1), expert_up.transpose(0, 2, 1), expert_down)
    one = exchange_ctx(sent_one, "rows_to_experts", grad_own)
    two = exchange_ctx(sent_two, "rows_to_experts", one)
    one_other = swap(one, "core")
    back_own, back_send, y_one, y_one_send, dots, *units_one = expert(
        0, core_is, one, one_other, grad_own, grad_other, *weights
    )
    two = after(two, dots)
    two_other = swap(two, "core")
    (sent_one,) = call(finish_rows_kernel, [buffer], "finish_rows", 1)(
        core_is, after(back_own, two), swap(back_send, "core"), dots, swap(dots, "core")
    )
    back_one = exchange_ctx(sent_one, "row_grads_back", two)
    back_own, back_send, y_two, y_two_send, dots, *units_two = expert(
        1, core_is, two, two_other, grad_own, grad_other, *weights
    )
    (sent_two,) = call(finish_rows_kernel, [buffer], "finish_rows", 1)(
        core_is, back_own, swap(after(back_send, back_one), "core"), dots,
        swap(after(dots, back_one), "core"),
    )
    back_two = exchange_ctx(sent_two, "row_grads_back", back_one)

    with jax.named_scope("shared_weights"):
        shared_all = lax.all_gather(after(shared_pair_mine, one), ("y", "x"), tiled=False)
    shared_own, shared_send, in_own, in_send, shared_grads = shared(
        core_is, after(normed_two, sent_two), grad_out, shared_all
    )
    back_two = after(back_two, in_own)

    in_half, prob_grad = call(
        combine_kernel,
        [out((TOK, HALF), bf16), out((EXPERTS, TOK), f32)],
        "combine",
        4 * N_CTX * SLOTS * TOK * HALF,
    )(core_is, back_one, back_two, slot_by, in_own, swap(in_send, "core"))
    (outs_one,) = call(add_kernel, [buffer], "outputs_sum", 1)(
        core_is, after(y_one, in_half), swap(y_one_send, "core")
    )
    prob_grad = prob_grad + swap(prob_grad, "zl")
    in_half = in_half.astype(f32) + swap(in_half, "zl").astype(f32)
    in_other = swap(in_half, "core")
    outs_one = exchange_ctx(after(outs_one, (in_other, prob_grad)), "outputs_back")
    (
        after_grad, attn_grad, logit_grad, gain_two_part, head_grad,
        grad_query_lat, keys_own, keys_send,
    ) = attend_back(
        places_core, in_half, in_other, attn_half, attn_other, hidden_in, root_two, gain_row,
        grad_out, router_t, probs, prob_grad, attn_all, query, keys, value, log_total,
    )
    grad_query_lat = grad_query_lat.reshape(HEADS, TOK, KEYS)
    normed_two_quarter = lax.dynamic_slice_in_dim(normed_two, column_start, QUARTER, 1)
    router_part = nn(logit_grad, normed_two_quarter).reshape(EXP_DEV, N_CTX, QUARTER)
    router_part = router_part.transpose(1, 0, 2)
    gain_two_mine = pick(gain_two_part.reshape(N_CTX, 4, 16), ws, 1)

    keys_mine, keys_other = call(
        key_split_kernel,
        [out((SEQ_PAIRS, 64, KEYS), f32), out((SEQ_PAIRS, 64, KEYS), bf16)],
        "key_split",
        1,
    )(jnp.concatenate([place_of, zl[None]]), after(keys_own, outs_one), swap(keys_send, "core"))
    (keys_sent,) = call(key_spread_kernel, [out((N_CTX, 64, KEYS), bf16)], "key_spread", 1)(
        pairs, keys_mine, swap(keys_other, "zl")
    )
    keys_back = exchange_ctx(keys_sent, "key_grads")

    attn_parts, normed_one_part = call(
        query_back_kernel,
        [out((16, 2, 64, 1536), bf16), out((TOK, WIDTH), f32)],
        "query_back",
        2 * TOK * WIDTH * 2048 + 2 * TOK * RANK * 1536,
    )(
        core_is, after(grad_query_lat, keys_other), query_nope, normed_one, attn_all, cos, sin,
        value.reshape(HEADS, TOK, RANK), head_grad, attn_grad, head_flat,
    )

    half_out = out((TOK, HALF), f32)
    (routed_half,) = call(outputs_kernel, [half_out], "outputs", 1)(
        core_is, after(outs_one, keys_sent), slot_by[:N_CTX], probs[:N_CTX],
        shared_own, swap(shared_send, "core"),
    )
    (outs_two,) = call(add_kernel, [buffer], "outputs_sum", 1)(
        core_is, after(y_two, keys_sent), swap(y_two_send, "core")
    )

    filled = expert_grads(
        core_is, (one, one_other, two, two_other), (grad_own, grad_other),
        (after(units_one[0], keys_sent), *units_one[1:], *units_two),
    )
    grad_expert_gate = filled[0].transpose(0, 2, 1)
    grad_expert_up = filled[1].transpose(0, 2, 1)
    grad_expert_down = filled[2]
    keys_back = after(keys_back, (filled[0], normed_one_part, routed_half, outs_two))

    compressed_grad, gain_kv_part = call(
        latent_back_kernel, [out((64, KEYS), bf16), out((1, RANK), f32)], "latent_back", 1
    )(
        core_is, keys_back, latent_pre, root_kv, gain_kv.reshape(1, RANK),
        lax.dynamic_slice_in_dim(cos, row_start, 64), lax.dynamic_slice_in_dim(sin, row_start, 64),
    )
    compressed_grad = gather_two(gather_two(compressed_grad, "core", 0), "zl", 0).reshape(TOK, KEYS)
    input_own, input_send, gain_one_part, grad_down_part = call(
        input_back_kernel,
        [
            out((TOK, HALF), f32),
            out((TOK, HALF), bf16),
            out((1, WIDTH), f32),
            out((KEYS, QUARTER), bf16),
        ],
        "input_back",
        4 * TOK * KEYS * QUARTER,
        [pltpu.VMEM((TOK, WIDTH), f32)],
    )(
        jnp.stack([core, zl]), compressed_grad, down_t, normed_one, normed_one_part, hidden_in,
        root_one, gain_one.reshape(1, WIDTH),
    )
    grad_down_part = grad_down_part.reshape(N_CTX, 18, QUARTER)
    input_quarter = zl_quarter(input_own + swap(input_send, "core").astype(f32), zl)
    grad_in = lax.dynamic_slice_in_dim(after_grad, column_start, QUARTER, 1) + input_quarter
    gain_parts = jnp.concatenate(
        [gain_one_part.reshape(N_CTX, 2, 2, 16), gain_kv_part.reshape(N_CTX, 2, 2, 4)], axis=-1
    )
    gain_core = pick(gain_parts, core, 2) + swap(pick(gain_parts, 1 - core, 2), "core")
    gain_mine = pick(gain_core, zl, 1) + swap(pick(gain_core, 1 - zl, 1), "zl")

    shared_pair = scatter_yx(
        after(shared_grads, back_two).reshape(WIDTH, 3 * FF_SH), "shared_weight_grads"
    )
    attn_pair = scatter_yx(
        after(attn_parts, shared_pair).reshape(WIDTH, 1536), "attn_weight_grads"
    )
    shared_sum = scatter_zh(shared_pair, "shared_weight_grads")
    attn_sum = scatter_zh(attn_pair, "attn_weight_grads")
    gain_rows = jnp.concatenate([gain_mine, gain_two_mine], axis=1)
    gain_rows = jnp.pad(gain_rows, ((0, 0), (0, QUARTER - 36)))[:, None, :]
    small_parts = jnp.concatenate(
        [
            grad_down_part,
            router_part.astype(bf16),
            gain_rows.astype(bf16),
            jnp.zeros((N_CTX, 3, QUARTER), bf16),
        ],
        axis=1,
    )
    small_back = exchange_ctx(small_parts, "small_weight_grads", keys_back)
    small_sum = jnp.sum(small_back.astype(f32), axis=0)
    outs_two = exchange_ctx(outs_two, "outputs_back", small_back)
    (routed_half,) = call(outputs_kernel, [half_out], "outputs", 1)(
        core_is, outs_two, slot_by[N_CTX:], probs[N_CTX:], routed_half,
        jnp.zeros((TOK, HALF), bf16),
    )
    layer_out = (
        lax.dynamic_slice_in_dim(hidden_in, column_start, QUARTER, 1).astype(f32)
        + lax.dynamic_slice_in_dim(attn_half, zl * QUARTER, QUARTER, 1)
        + zl_quarter(routed_half, zl)
    ).astype(bf16)
    up_sum = (
        attn_sum[:, 768 + QUARTER :]
        .reshape(HEADS, 16, NOPE + VDIM)
        .transpose(1, 0, 2)
        .reshape(16, HEADS * (NOPE + VDIM))
    )
    return (
        layer_out,
        grad_in,
        small_sum[20, :16],
        small_sum[20, 16:20],
        small_sum[20, 20:36],
        attn_sum[:, :768],
        small_sum[:18].T,
        up_sum,
        attn_sum[:, 768 : 768 + QUARTER].T,
        small_sum[18:20].T,
        grad_expert_gate,
        grad_expert_up,
        grad_expert_down,
        shared_sum[:, :FF_SH],
        shared_sum[:, FF_SH : 2 * FF_SH],
        shared_sum[:, 2 * FF_SH :].T,
    )


def solution(mesh):
    grid = Mesh(mesh.devices.reshape(2, 4, 4, 2, 2), CTX + ("zl", "core"))
    ctx, ws, both = CTX, ("zl", "core"), CTX + ("zl", "core")
    placed = (
        P(ctx, None),
        P(ctx, None),
        P(),
        P(ctx, None),
        P(ctx),
        P(both),
        P(both),
        P(both),
        P(ctx, ws),
        P(ws, ctx),
        P(ctx, ws),
        P(ws, ctx),
        P(ws, ctx),
        P(ctx, None, ws),
        P(ctx, None, ws),
        P(ctx, ws, None),
        P(ctx, ws),
        P(ctx, ws),
        P(ws, ctx),
    )
    return jax.shard_map(
        on_device,
        mesh=grid,
        in_specs=placed,
        out_specs=(
            P(ctx, ws),
            P(ctx, ws),
            P(both),
            P(both),
            P(both),
            P(ctx, ws),
            P(ws, ctx),
            P(ctx, ws),
            P(ws, ctx),
            P(ws, ctx),
            P(ctx, None, ws),
            P(ctx, None, ws),
            P(ctx, ws, None),
            P(ctx, ws),
            P(ctx, ws),
            P(ws, ctx),
        ),
        check_vma=False,
    )
```

time: 1080 us -> 729 us (0.68)
  Pallas kernels: 30.5 us -> 206 us
  local copies, waits for them, and re-layouts: 202 us -> 48.3 us
  matrix products: 141 us -> 1.5 us
  starting transfers between devices: 206 us -> 97.1 us
  other arithmetic: 110 us -> 33.3 us
  waiting for transfers between devices: 371 us -> 299 us
  blocking collectives: 0 us -> 19.9 us
    ppermute x110 -> x37, waiting for transfers between devices: 312 us -> 147 us  [shift(): lax.ppermute(value, axis, [(i, (i + step) % size) for i in range(size)])]
    pallas_call x0 -> x20, Pallas kernels: none -> 161 us  [the longest x16 77.3 us: run(): pl.pallas_call(body, in_specs=[pl.BlockSpec(memory_space=pltpu.SMEM)] + [...]
    dot_general x51 -> x2, matrix products: 135 us -> 1.5 us  [dot(): lax.dot_general(a, b, ((contract[0], contract[1]), ((), ())), preferred_e...]
    ppermute x110 -> x37, starting transfers between devices: 141 us -> 25.2 us  [shift(): lax.ppermute(value, axis, [(i, (i + step) % size) for i in range(size)])]
    all_to_all x9 -> x10, waiting for transfers between devices: 59 us -> 142 us  [exchange_ctx(): return lax.all_to_all(value, CTX, 0, 0, tiled=True)]
    dynamic_update_slice x47 -> x0, local copies, waits for them, and re-layouts: 61.7 us -> none  [the longest x43 47.8 us: gather_four(): lax.dynamic_update_slice_in_dim(result, jnp.expand_dims(piece, dim), (her...]
    convert_element_type x28 -> x3, other arithmetic: 26.3 us -> 1.92 us  [the longest x1 1.81 us: on_device(): layer_out = (lax.dynamic_slice_in_dim(hidden_in, column_start, QUARTER, 1...]
    all_to_all x0 -> x1, blocking collectives: none -> 19.9 us  [exchange_ctx(): return lax.all_to_all(value, CTX, 0, 0, tiled=True)]
  transfers between devices with their start and end apart: 119 -> 51, of which waited for: 44 -> 34; matrix products, arithmetic and copies ran while one was open for 37% -> 9% of each run, Pallas kernels for 2% -> 29%
where the time goes in v2:
time: 729 us; the launch traced here: 720 us
  waiting for transfers between devices  299 us (41%)
  Pallas kernels  206 us (28%)
  starting transfers between devices  97.1 us (13%)
  local copies, waits for them, and re-layouts  48.3 us (7%)
  other arithmetic  33.3 us (5%)
  blocking collectives  19.9 us (3%)
  between operations  15.3 us (2%)
    ppermute x37, waiting for transfers between devices, shift(): lax.ppermute(value, axis, [(i, (i + step) % size) for i in range(size)])  147 us
    all_to_all x10, waiting for transfers between devices, exchange_ctx(): return lax.all_to_all(value, CTX, 0, 0, tiled=True)  142 us
    pallas_call x16, Pallas kernels, run(): pl.pallas_call(body, in_specs=[pl.BlockSpec(memory_space=pltpu.SMEM)] + [...  77.3 us
    all_to_all x10, starting transfers between devices, exchange_ctx(): return lax.all_to_all(value, CTX, 0, 0, tiled=True)  71.7 us
    pallas_call x2, Pallas kernels, expert(): pl.pallas_call(expert_kernel, grid=(total // step,), in_specs=[pl.BlockSp...  40.6 us
    pallas_call x1, Pallas kernels, attend_back(): pl.pallas_call(attend_back_kernel, grid_spec=pltpu.PrefetchScalarGridSpec...  26.3 us
    ppermute x37, starting transfers between devices, shift(): lax.ppermute(value, axis, [(i, (i + step) % size) for i in range(size)])  25.2 us
    pallas_call x1, Pallas kernels, expert_grads(): pl.pallas_call(expert_grads_kernel, grid=(EXP_DEV, 4), in_specs=[pl.Block...  23 us
  transfers between devices with their start and end apart: 51, of which 34 were waited for; matrix products, arithmetic and copies ran while one was open for 9% of the time, Pallas kernels for 29%

profile of v2, /device:TPU:0, one launch (start us, length us, event | category | flops | bytes accessed | tf_op | source)
XLA Modules:
  0.0 720.5 jit_solution(3130474371013933885)
XLA Ops:
  18.0 10.7 %all-to-all-start = ((bf16[32,24,512]{2,1,0:T(8,128)(2,1)}), bf16[32,24,512]{2,1,0:T(8,128)(2,1)S(1)}, u32[]{:S(2)}, u32[]{:S(2)}) async-start(bf16[32,24,512]{2,1,0:T(8,128)(2,1)} %broadcast_in_dim.41), calls=%async_computation | async-start | bytes 1572864 | tf_op jit(solution)/shard_map/small_weights/all_to_all | solution.py:133
  29.0 15.5 %all-to-all-done = bf16[32,24,512]{2,1,0:T(8,128)(2,1)S(1)} async-done(((bf16[32,24,512]{2,1,0:T(8,128)(2,1)}), bf16[32,24,512]{2,1,0:T(8,128)(2,1)S(1)}, u32[]{:S(2)}, u32[]{:S(2)}) %all-to-all-start) | async-done | bytes 786464 | tf_op jit(solution)/shard_map/small_weights/all_to_all | solution.py:133
  51.3 8.0 %collective-permute-done.3 = f32[64,576]{1,0:T(8,128)S(1)} collective-permute-done((f32[64,576]{1,0:T(8,128)S(1)}, f32[64,576]{1,0:T(8,128)S(1)}, u32[]{:S(2)}, u32[]{:S(2)}) %collective-permute-start.3) | collective-permute-done | bytes 147488 | tf_op jit(solution)/shard_map/ppermute | solution.py:87
  62.8 5.6 all-to-all-start.1
  76.4 33.4 %all-to-all-done.1 = bf16[32,64,576]{2,1,0:T(8,128)(2,1)S(1)} async-done(((bf16[32,64,576]{2,1,0:T(8,128)(2,1)}), bf16[32,64,576]{2,1,0:T(8,128)(2,1)S(1)}, u32[]{:S(2)}, u32[]{:S(2)}) %all-to-all-start.1) | async-done | bytes 2359328 | tf_op jit(solution)/shard_map/latents/all_to_all | solution.py:133
  114.9 20.1 %collective-permute-done.4.zl_ref = bf16[8,64,576]{2,1,0:T(8,128)(2,1)S(1)} collective-permute-done((bf16[8,64,576]{2,1,0:T(8,128)(2,1)S(1)}, bf16[8,64,576]{2,1,0:T(8,128)(2,1)S(1)}, u32[]{:S(2)}, u32[]{:S(2)}) %collective-permute-start.4) | collective-permute-done | bytes 589856 | tf_op jit(solution)/shard_map/ppermute | solution.py:87
  138.4 10.7 %all-to-all-start.2 = ((bf16[32,2,32,1024]{3,2,1,0:T(8,128)(2,1)}), bf16[32,2,32,1024]{3,2,1,0:T(8,128)(2,1)}, u32[]{:S(2)}, u32[]{:S(2)}) async-start(bf16[32,2,32,1024]{3,2,1,0:T(8,128)(2,1)} %get-tuple-element.109), calls=%async_computation.2 | async-start | bytes 8388608 | tf_op jit(solution)/shard_map/cotangent_rows/all_to_all | solution.py:133
  157.5 5.9 queries.1
  163.4 18.8 %attend.1 = (f32[4,2,128,512]{3,2,1,0:T(8,128)}, f32[4,2,128,128]{3,2,1,0:T(8,128)}, bf16[256,512]{1,0:T(8,128)(2,1)}, f32[256,1024]{1,0:T(8,128)}, bf16[256,1024]{1,0:T(8,128)(2,1)}) custom-call(s32[3]{0:T(128)} %pad_add_fusion.place_ref, bf16[4,2,128,576]{3,2,1,0:T(8,128)(2,1)} %bitcast.182, bf16[2048,576]{1,0:T(8,128)(2,1)} %keys.1.k_ref, ...), custom_call_target="tpu_custom_call" | custom-call | flops 2852126720 | bytes 16777216 | tf_op jit(solution)/shard_map/attend/pallas_call | solution.py:659
  185.8 23.4 %collective-permute-done.7 = bf16[256,1024]{1,0:T(8,128)(2,1)S(1)} collective-permute-done((bf16[256,1024]{1,0:T(8,128)(2,1)S(1)}, bf16[256,1024]{1,0:T(8,128)(2,1)S(1)}, u32[]{:S(2)}, u32[]{:S(2)}) %collective-permute-start.7) | collective-permute-done | bytes 524320 | tf_op jit(solution)/shard_map/ppermute | solution.py:87
  218.2 6.3 middle.1
  224.5 9.9 %all-to-all-start.3 = ((bf16[32,32,1024]{2,1,0:T(8,128)(2,1)}), bf16[32,32,1024]{2,1,0:T(8,128)(2,1)S(1)}, u32[]{:S(2)}, u32[]{:S(2)}) async-start(bf16[32,32,1024]{2,1,0:T(8,128)(2,1)} %get-tuple-element.110), calls=%async_computation.3 | async-start | bytes 4194304 | tf_op jit(solution)/shard_map/rows_to_experts/all_to_all | solution.py:133
  238.9 28.4 %collective-permute-done.18 = bf16[64,2112]{1,0:T(8,128)(2,1)} collective-permute-done((bf16[64,2112]{1,0:T(8,128)(2,1)S(1)}, bf16[64,2112]{1,0:T(8,128)(2,1)}, u32[]{:S(2)}, u32[]{:S(2)}) %collective-permute-start.18) | collective-permute-done | bytes 270368 | tf_op jit(solution)/shard_map/ppermute | solution.py:87
  270.6 6.7 all-to-all-start.4
  279.6 20.2 %expert.2 = (bf16[32,32,1024]{2,1,0:T(8,128)(2,1)}, bf16[32,32,1024]{2,1,0:T(8,128)(2,1)}, bf16[32,32,1024]{2,1,0:T(8,128)(2,1)}, bf16[32,32,1024]{2,1,0:T(8,128...) custom-call(s32[2]{0:T(128)} %pad_add_fusion.1.core_ref, ...), custom_call_target="tpu_custom_call" | custom-call | flops 8858370048 | bytes 25165824 | tf_op jit(solution)/shard_map/expert/pallas_call | solution.py:400
  300.1 15.3 %all-to-all-done.4.own_ref.two_ref = bf16[32,32,1024]{2,1,0:T(8,128)(2,1)} async-done(((bf16[32,32,1024]{2,1,0:T(8,128)(2,1)}), bf16[32,32,1024]{2,1,0:T(8,128)(2,1)}, u32[]{:S(2)}, u32[]{:S(2)}) %all-to-all-start.4) | async-done | bytes 2097184 | tf_op jit(solution)/shard_map/rows_to_experts/all_to_all | solution.py:133
  325.4 5.7 all-to-all-start.5
  331.1 20.4 %expert.3 = (bf16[32,32,1024]{2,1,0:T(8,128)(2,1)}, bf16[32,32,1024]{2,1,0:T(8,128)(2,1)}, bf16[32,32,1024]{2,1,0:T(8,128)(2,1)}, bf16[32,32,1024]{2,1,0:T(8,128...) custom-call(s32[2]{0:T(128)} %pad_add_fusion.1.core_ref, ...), custom_call_target="tpu_custom_call" | custom-call | flops 8858370048 | bytes 25165824 | tf_op jit(solution)/shard_map/expert/pallas_call | solution.py:400
  351.5 32.2 %all-to-all-done.5.one_ref = bf16[32,32,1024]{2,1,0:T(8,128)(2,1)S(1)} async-done(((bf16[32,32,1024]{2,1,0:T(8,128)(2,1)}), bf16[32,32,1024]{2,1,0:T(8,128)(2,1)S(1)}, u32[]{:S(2)}, u32[]{:S(2)}) %all-to-all-start.5) | async-done | bytes 2097184 | tf_op jit(solution)/shard_map/row_grads_back/all_to_all | solution.py:133
  398.2 20.1 %shared_experts.1 = (f32[256,1024]{1,0:T(8,128)}, bf16[256,1024]{1,0:T(8,128)(2,1)}, f32[256,1024]{1,0:T(8,128)}, bf16[256,1024]{1,0:T(8,128)(2,1)}, bf16[16,2,64,2112]{3,2,1,0:T(8,128)(2,1)}) custom-call(s32[2]{0:T(128)} %pad_add_fusion.1.core_ref, bf16[256,2048]{1,0:T(8,128)(2,1)} %get-tuple-element.126.normed_ref, bf16[256,2048]{1,0:T(8,128)(2,1)} %grad_ref.5, ...), custom_call_target="tpu_custom_call" | custom-call | flops 6643777536 | bytes 25165824 | tf_op jit(solution)/shard_map/shared_experts/pallas_call | solution.py:348
  418.3 9.4 %all-to-all-done.6.two_ref = bf16[32,32,1024]{2,1,0:T(8,128)(2,1)S(1)} async-done(((bf16[32,32,1024]{2,1,0:T(8,128)(2,1)}), bf16[32,32,1024]{2,1,0:T(8,128)(2,1)S(1)}, u32[]{:S(2)}, u32[]{:S(2)}) %all-to-all-start.6) | async-done | bytes 2097184 | tf_op jit(solution)/shard_map/row_grads_back/all_to_all | solution.py:133
  439.1 13.1 %collective-permute-done.20 = bf16[256,1024]{1,0:T(8,128)(2,1)S(1)} collective-permute-done((bf16[256,1024]{1,0:T(8,128)(2,1)}, bf16[256,1024]{1,0:T(8,128)(2,1)S(1)}, u32[]{:S(2)}, u32[]{:S(2)}) %collective-permute-start.20) | collective-permute-done | bytes 524320 | tf_op jit(solution)/shard_map/ppermute | solution.py:87
  466.3 26.3 %attend_back.1 = (f32[256,2048]{1,0:T(8,128)}, bf16[256,2048]{1,0:T(8,128)(2,1)}, bf16[64,256]{1,0:T(8,128)(2,1)}, f32[1,2048]{1,0:T(1,128)}, bf16[256,512]{1,0:...) custom-call(s32[3]{0:T(128)} %pad_add_fusion.place_ref, ...), custom_call_target="tpu_custom_call" | custom-call | flops 7549747200 | bytes 37748736 | tf_op jit(solution)/shard_map/attend_back/pallas_call | solution.py:845
  493.6 10.8 %all-to-all-done.7.back_ref = bf16[32,32,1024]{2,1,0:T(8,128)(2,1)S(1)} async-done(((bf16[32,32,1024]{2,1,0:T(8,128)(2,1)}), bf16[32,32,1024]{2,1,0:T(8,128)(2,1)S(1)}, u32[]{:S(2)}, u32[]{:S(2)}) %all-to-all-start.7) | async-done | bytes 2097184 | tf_op jit(solution)/shard_map/outputs_back/all_to_all | solution.py:133
  508.5 11.5 %query_back.1 = (bf16[16,2,64,1536]{3,2,1,0:T(8,128)(2,1)}, f32[256,2048]{1,0:T(8,128)}) custom-call(s32[2]{0:T(128)} %pad_add_fusion.1.core_ref, f32[4,256,576]{2,1,0:T(8,128)} %bitcast.147, bf16[4,256,128]{2,1,0:T(8,128)(2,1)} %get-tuple-element.158.nope_ref, bf16[256,2048]{1,0:T(8,128)(2,1)} %copy-done, bf16[2,16,64,1536]{3,2,1,0:T(8,128)(2,1)} %bitcast.141, ...), custom_call_target="tpu_custom_call" | custom-call | flops 2550136832 | bytes 22151168 | tf_op jit(solution)/shard_map/query_back/pallas_call | solution.py:180
  520.0 10.4 %reduce-scatter.3.cloned.1.call-done = bf16[128,2112]{1,0:T(8,128)(2,1)} async-done(((bf16[2048,2112]{1,0:T(8,128)(2,1)}), bf16[128,2112]{1,0:T(8,128)(2,1)}) %reduce-scatter.3.cloned.1.call-update) | async-done | bytes 540688 | tf_op jit(solution)/shard_map/shared_weight_grads/reduce_scatter | solution.py:114
  533.0 14.6 %collective-permute-done.25.arrived_ref = bf16[8,64,576]{2,1,0:T(8,128)(2,1)S(1)} collective-permute-done((bf16[8,64,576]{2,1,0:T(8,128)(2,1)S(1)}, bf16[8,64,576]{2,1,0:T(8,128)(2,1)S(1)}, u32[]{:S(2)}, u32[]{:S(2)}) %collective-permute-start.25) | collective-permute-done | bytes 589856 | tf_op jit(solution)/shard_map/ppermute | solution.py:87
  551.8 7.9 %all-to-all-start.8 = ((bf16[32,64,576]{2,1,0:T(8,128)(2,1)}), bf16[32,64,576]{2,1,0:T(8,128)(2,1)S(1)}, u32[]{:S(2)}, u32[]{:S(2)}) async-start(bf16[32,64,576]{2,1,0:T(8,128)(2,1)} %key_spread.1), calls=%async_computation.8 | async-start | bytes 5242880 | tf_op jit(solution)/shard_map/key_grads/all_to_all | solution.py:133
  574.6 23.0 %expert_grads.1 = (f32[2,352,2048]{2,1,0:T(8,128)}, f32[2,352,2048]{2,1,0:T(8,128)}, f32[2,352,2048]{2,1,0:T(8,128)}) custom-call(s32[2]{0:T(128)} %pad_add_fusion.1.core_ref, bf16[32,32,1024]{2,1,0:T(8,128)(2,1)} %copy-done.17, bf16[32,32,1024]{2,1,0:T(8,128)(2,1)} %collective-permute-done.11.other_ref.one_other_ref, ...), custom_call_target="tpu_custom_call" | custom-call | flops 8858370048 | bytes 37748736 | tf_op jit(solution)/shard_map/expert_grads/pallas_call | solution.py:537
  597.6 5.8 all-to-all-done.8.back_ref
  631.0 19.9 %all_to_all.55 = bf16[32,24,512]{2,1,0:T(8,128)(2,1)} all-to-all(bf16[32,24,512]{2,1,0:T(8,128)(2,1)S(1)} %maximum_maximum_fusion), channel_id=1, replica_groups=mesh['zh'=2,'y'=4,'x'=4,'zl'=2,'core'=2] {'zh','y','x'}, dimensions={0} | all-to-all | bytes 1572864 | tf_op jit(solution)/shard_map/small_weight_grads/all_to_all | solution.py:133
  665.1 19.1 %all-to-all-done.10.back_ref = bf16[32,32,1024]{2,1,0:T(8,128)(2,1)S(1)} async-done(((bf16[32,32,1024]{2,1,0:T(8,128)(2,1)}), bf16[32,32,1024]{2,1,0:T(8,128)(2,1)S(1)}, u32[]{:S(2)}, u32[]{:S(2)}) %all-to-all-start.10) | async-done | bytes 2097184 | tf_op jit(solution)/shard_map/outputs_back/all_to_all | solution.py:133
  (326 shorter events, 216.2 us)
Async XLA Ops:
  7.2 150.3 %all-gather.5.cloned.1.call-start = ((), (), s32[]{:S(2)}) async-start(), calls=%async_computation.15 | async-start | bytes 6488064 | tf_op jit(solution)/shard_map/attn_weights/all_gather | solution.py:108
  18.0 26.6 %all-to-all-start = ((bf16[32,24,512]{2,1,0:T(8,128)(2,1)}), bf16[32,24,512]{2,1,0:T(8,128)(2,1)S(1)}, u32[]{:S(2)}, u32[]{:S(2)}) async-start(bf16[32,24,512]{2,1,0:T(8,128)(2,1)} %broadcast_in_dim.41), calls=%async_computation | async-start | bytes 1572864 | tf_op jit(solution)/shard_map/small_weights/all_to_all | solution.py:133
  49.9 9.4 %collective-permute-start.3 = (f32[64,576]{1,0:T(8,128)S(1)}, f32[64,576]{1,0:T(8,128)S(1)}, u32[]{:S(2)}, u32[]{:S(2)}) collective-permute-start(f32[64,576]{1,0:T(8,128)S(1)} %dynamic-slice_bitcast_fusion.3), channel_id=1, source_target_pairs={{0,2},{2,0},{1,3},{3,1},{4,6},{6,4},{5,7},{7,5},{8,10},{10,8},{9,1... | collective-permute-start | bytes 442376 | tf_op jit(solution)/shard_map/ppermute | solution.py:87
  62.8 47.1 %all-to-all-start.1 = ((bf16[32,64,576]{2,1,0:T(8,128)(2,1)}), bf16[32,64,576]{2,1,0:T(8,128)(2,1)S(1)}, u32[]{:S(2)}, u32[]{:S(2)}) async-start(bf16[32,64,576]{2,1,0:T(8,128)(2,1)} %broadcast_in_dim.46), calls=%async_computation.1 | async-start | bytes 5242880 | tf_op jit(solution)/shard_map/latents/all_to_all | solution.py:133
  113.8 21.2 %collective-permute-start.4 = (bf16[8,64,576]{2,1,0:T(8,128)(2,1)S(1)}, bf16[8,64,576]{2,1,0:T(8,128)(2,1)S(1)}, u32[]{:S(2)}, u32[]{:S(2)}) collective-permute-start(bf16[8,64,576]{2,1,0:T(8,128)(2,1)S(1)} %gather_fusion.1), channel_id=1, source_target_pairs={{0,2},{2,0},{1,3},{3,1},{4,6},{6,4},{5,7},{7,5},{8,10},{10,8},{9,1... | collective-permute-start | bytes 1769480 | tf_op jit(solution)/shard_map/ppermute | solution.py:87
  138.4 86.1 %all-to-all-start.2 = ((bf16[32,2,32,1024]{3,2,1,0:T(8,128)(2,1)}), bf16[32,2,32,1024]{3,2,1,0:T(8,128)(2,1)}, u32[]{:S(2)}, u32[]{:S(2)}) async-start(bf16[32,2,32,1024]{3,2,1,0:T(8,128)(2,1)} %get-tuple-element.109), calls=%async_computation.2 | async-start | bytes 8388608 | tf_op jit(solution)/shard_map/cotangent_rows/all_to_all | solution.py:133
  185.7 23.5 %collective-permute-start.7 = (bf16[256,1024]{1,0:T(8,128)(2,1)S(1)}, bf16[256,1024]{1,0:T(8,128)(2,1)S(1)}, u32[]{:S(2)}, u32[]{:S(2)}) collective-permute-start(bf16[256,1024]{1,0:T(8,128)(2,1)S(1)} %add_convert_fusion), channel_id=1, source_target_pairs={{0,2},{2,0},{1,3},{3,1},{4,6},{6,4},{5,7},{7,5},{8,10},{10,8},{9,1... | collective-permute-start | bytes 1572872 | tf_op jit(solution)/shard_map/ppermute | solution.py:87
  209.4 8.8 %collective-permute-start.8 = (f32[256,1024]{1,0:T(8,128)S(1)}, f32[256,1024]{1,0:T(8,128)}, u32[]{:S(2)}, u32[]{:S(2)}) collective-permute-start(f32[256,1024]{1,0:T(8,128)S(1)} %convert_add_fusion.2.own_ref.sum_own_ref), channel_id=1, source_target_pairs={{0,1},{1,0},{2,3},{3,2},{4,5},{5,4},{6,7},{7,6},{8,9},{9,8},{10,11... | collective-permute-start | bytes 3145736 | tf_op jit(solution)/shard_map/ppermute | solution.py:87
  224.5 44.7 %all-to-all-start.3 = ((bf16[32,32,1024]{2,1,0:T(8,128)(2,1)}), bf16[32,32,1024]{2,1,0:T(8,128)(2,1)S(1)}, u32[]{:S(2)}, u32[]{:S(2)}) async-start(bf16[32,32,1024]{2,1,0:T(8,128)(2,1)} %get-tuple-element.110), calls=%async_computation.3 | async-start | bytes 4194304 | tf_op jit(solution)/shard_map/rows_to_experts/all_to_all | solution.py:133
  234.5 163.8 %all-gather.7.cloned.1.call-start = ((), (), s32[]{:S(2)}) async-start(), calls=%async_computation.16 | async-start | bytes 9469952 | tf_op jit(solution)/shard_map/shared_weights/all_gather | solution.py:1044
  235.6 31.8 %collective-permute-start.18 = (bf16[64,2112]{1,0:T(8,128)(2,1)S(1)}, bf16[64,2112]{1,0:T(8,128)(2,1)}, u32[]{:S(2)}, u32[]{:S(2)}) collective-permute-start(bf16[64,2112]{1,0:T(8,128)(2,1)S(1)} %concatenate.52), channel_id=1, source_target_pairs={{0,64},{64,0},{1,65},{65,1},{2,66},{66,2},{3,67},{67,3},{4,68},{68... | collective-permute-start | bytes 811016 | tf_op jit(solution)/shard_map/ppermute | solution.py:87
  269.3 8.6 %collective-permute-start.12 = (bf16[32,2,32,1024]{3,2,1,0:T(8,128)(2,1)}, bf16[32,2,32,1024]{3,2,1,0:T(8,128)(2,1)}, u32[]{:S(2)}, u32[]{:S(2)}) collective-permute-start(bf16[32,2,32,1024]{3,2,1,0:T(8,128)(2,1)} %all-to-all-done.2.grad_own_ref.ga_ref), channel_id=1, source_target_pairs={{0,1},{1,0},{2,3},{3,2},{4,5},{5,4},{6,7},{7,6},{8,9},{9,8},{10,11... | collective-permute-start | bytes 12582920 | tf_op jit(solution)/shard_map/ppermute | solution.py:87
  269.3 10.3 %collective-permute-start.11 = (bf16[32,32,1024]{2,1,0:T(8,128)(2,1)S(1)}, bf16[32,32,1024]{2,1,0:T(8,128)(2,1)}, u32[]{:S(2)}, u32[]{:S(2)}) collective-permute-start(bf16[32,32,1024]{2,1,0:T(8,128)(2,1)S(1)} %all-to-all-done.3.own_ref.one_ref), channel_id=1, source_target_pairs={{0,1},{1,0},{2,3},{3,2},{4,5},{5,4},{6,7},{7,6},{8,9},{9,8},{10,11... | collective-permute-start | bytes 6291464 | tf_op jit(solution)/shard_map/ppermute | solution.py:87
  270.6 44.7 %all-to-all-start.4 = ((bf16[32,32,1024]{2,1,0:T(8,128)(2,1)}), bf16[32,32,1024]{2,1,0:T(8,128)(2,1)}, u32[]{:S(2)}, u32[]{:S(2)}) async-start(bf16[32,32,1024]{2,1,0:T(8,128)(2,1)} %get-tuple-element.111), calls=%async_computation.4 | async-start | bytes 4194304 | tf_op jit(solution)/shard_map/rows_to_experts/all_to_all | solution.py:133
  299.8 19.5 %collective-permute-start.14 = (bf16[32,32,1024]{2,1,0:T(8,128)(2,1)}, bf16[32,32,1024]{2,1,0:T(8,128)(2,1)S(1)}, u32[]{:S(2)}, u32[]{:S(2)}) collective-permute-start(bf16[32,32,1024]{2,1,0:T(8,128)(2,1)} %get-tuple-element.117), channel_id=1, source_target_pairs={{0,1},{1,0},{2,3},{3,2},{4,5},{5,4},{6,7},{7,6},{8,9},{9,8},{10,11... | collective-permute-start | bytes 6291464 | tf_op jit(solution)/shard_map/ppermute | solution.py:87
  315.3 15.8 %collective-permute-start.13 = (bf16[32,32,1024]{2,1,0:T(8,128)(2,1)}, bf16[32,32,1024]{2,1,0:T(8,128)(2,1)}, u32[]{:S(2)}, u32[]{:S(2)}) collective-permute-start(bf16[32,32,1024]{2,1,0:T(8,128)(2,1)} %all-to-all-done.4.own_ref.two_ref), channel_id=1, source_target_pairs={{0,1},{1,0},{2,3},{3,2},{4,5},{5,4},{6,7},{7,6},{8,9},{9,8},{10,11... | collective-permute-start | bytes 6291464 | tf_op jit(solution)/shard_map/ppermute | solution.py:87
  325.4 58.3 %all-to-all-start.5 = ((bf16[32,32,1024]{2,1,0:T(8,128)(2,1)}), bf16[32,32,1024]{2,1,0:T(8,128)(2,1)S(1)}, u32[]{:S(2)}, u32[]{:S(2)}) async-start(bf16[32,32,1024]{2,1,0:T(8,128)(2,1)} %finish_rows.2), calls=%async_computation.5 | async-start | bytes 4194304 | tf_op jit(solution)/shard_map/row_grads_back/all_to_all | solution.py:133
  393.5 34.2 %all-to-all-start.6 = ((bf16[32,32,1024]{2,1,0:T(8,128)(2,1)}), bf16[32,32,1024]{2,1,0:T(8,128)(2,1)S(1)}, u32[]{:S(2)}, u32[]{:S(2)}) async-start(bf16[32,32,1024]{2,1,0:T(8,128)(2,1)} %finish_rows.3), calls=%async_computation.6 | async-start | bytes 4194304 | tf_op jit(solution)/shard_map/row_grads_back/all_to_all | solution.py:133
  398.2 132.2 %reduce-scatter.3.cloned.1.call-start = ((), (), s32[]{:S(2)}) async-start(), calls=%async_computation.13 | async-start | bytes 9469952 | tf_op jit(solution)/shard_map/shared_weight_grads/reduce_scatter | solution.py:114
  429.1 25.8 %collective-permute-start.23 = (bf16[32,32,1024]{2,1,0:T(8,128)(2,1)}, bf16[32,32,1024]{2,1,0:T(8,128)(2,1)S(1)}, u32[]{:S(2)}, u32[]{:S(2)}) collective-permute-start(bf16[32,32,1024]{2,1,0:T(8,128)(2,1)} %get-tuple-element.140), channel_id=1, source_target_pairs={{0,1},{1,0},{2,3},{3,2},{4,5},{5,4},{6,7},{7,6},{8,9},{9,8},{10,11... | collective-permute-start | bytes 6291464 | tf_op jit(solution)/shard_map/ppermute | solution.py:87
  438.0 14.2 %collective-permute-start.20 = (bf16[256,1024]{1,0:T(8,128)(2,1)}, bf16[256,1024]{1,0:T(8,128)(2,1)S(1)}, u32[]{:S(2)}, u32[]{:S(2)}) collective-permute-start(bf16[256,1024]{1,0:T(8,128)(2,1)} %get-tuple-element.131), channel_id=1, source_target_pairs={{0,2},{2,0},{1,3},{3,1},{4,6},{6,4},{5,7},{7,5},{8,10},{10,8},{9,1... | collective-permute-start | bytes 1572872 | tf_op jit(solution)/shard_map/ppermute | solution.py:87
  461.0 43.4 %all-to-all-start.7 = ((bf16[32,32,1024]{2,1,0:T(8,128)(2,1)}), bf16[32,32,1024]{2,1,0:T(8,128)(2,1)S(1)}, u32[]{:S(2)}, u32[]{:S(2)}) async-start(bf16[32,32,1024]{2,1,0:T(8,128)(2,1)} %outputs_sum.2), calls=%async_computation.7 | async-start | bytes 4194304 | tf_op jit(solution)/shard_map/outputs_back/all_to_all | solution.py:133
  466.2 236.1 %reduce-scatter.5.cloned.1.call-start = ((), (), s32[]{:S(2)}) async-start(), calls=%async_computation.14 | async-start | bytes 6684672 | tf_op jit(solution)/shard_map/attn_weight_grads/reduce_scatter | solution.py:114
  492.6 11.8 %collective-permute-start.24 = (bf16[16,64,576]{2,1,0:T(8,128)(2,1)}, bf16[16,64,576]{2,1,0:T(8,128)(2,1)}, u32[]{:S(2)}, u32[]{:S(2)}) collective-permute-start(bf16[16,64,576]{2,1,0:T(8,128)(2,1)} %get-tuple-element.143), channel_id=1, source_target_pairs={{0,1},{1,0},{2,3},{3,2},{4,5},{5,4},{6,7},{7,6},{8,9},{9,8},{10,11... | collective-permute-start | bytes 3538952 | tf_op jit(solution)/shard_map/ppermute | solution.py:87
  530.4 36.3 %collective-permute-start.26 = (bf16[32,32,1024]{2,1,0:T(8,128)(2,1)}, bf16[32,32,1024]{2,1,0:T(8,128)(2,1)}, u32[]{:S(2)}, u32[]{:S(2)}) collective-permute-start(bf16[32,32,1024]{2,1,0:T(8,128)(2,1)} %get-tuple-element.147), channel_id=1, source_target_pairs={{0,1},{1,0},{2,3},{3,2},{4,5},{5,4},{6,7},{7,6},{8,9},{9,8},{10,11... | collective-permute-start | bytes 6291464 | tf_op jit(solution)/shard_map/ppermute | solution.py:87
  531.5 16.2 %collective-permute-start.25 = (bf16[8,64,576]{2,1,0:T(8,128)(2,1)S(1)}, bf16[8,64,576]{2,1,0:T(8,128)(2,1)S(1)}, u32[]{:S(2)}, u32[]{:S(2)}) collective-permute-start(bf16[8,64,576]{2,1,0:T(8,128)(2,1)S(1)} %copy-done.42), channel_id=1, source_target_pairs={{0,2},{2,0},{1,3},{3,1},{4,6},{6,4},{5,7},{7,5},{8,10},{10,8},{9,1... | collective-permute-start | bytes 1769480 | tf_op jit(solution)/shard_map/ppermute | solution.py:87
  551.8 51.6 %all-to-all-start.8 = ((bf16[32,64,576]{2,1,0:T(8,128)(2,1)}), bf16[32,64,576]{2,1,0:T(8,128)(2,1)S(1)}, u32[]{:S(2)}, u32[]{:S(2)}) async-start(bf16[32,64,576]{2,1,0:T(8,128)(2,1)} %key_spread.1), calls=%async_computation.8 | async-start | bytes 5242880 | tf_op jit(solution)/shard_map/key_grads/all_to_all | solution.py:133
  559.7 11.1 %collective-permute-start.27 = (bf16[256,1024]{1,0:T(8,128)(2,1)}, bf16[256,1024]{1,0:T(8,128)(2,1)}, u32[]{:S(2)}, u32[]{:S(2)}) collective-permute-start(bf16[256,1024]{1,0:T(8,128)(2,1)} %get-tuple-element.165), channel_id=1, source_target_pairs={{0,1},{1,0},{2,3},{3,2},{4,5},{5,4},{6,7},{7,6},{8,9},{9,8},{10,11... | collective-permute-start | bytes 1572872 | tf_op jit(solution)/shard_map/ppermute | solution.py:87
  651.0 33.2 %all-to-all-start.10 = ((bf16[32,32,1024]{2,1,0:T(8,128)(2,1)}), bf16[32,32,1024]{2,1,0:T(8,128)(2,1)S(1)}, u32[]{:S(2)}, u32[]{:S(2)}) async-start(bf16[32,32,1024]{2,1,0:T(8,128)(2,1)} %outputs_sum.3), calls=%async_computation.10 | async-start | bytes 4194304 | tf_op jit(solution)/shard_map/outputs_back/all_to_all | solution.py:133
  660.8 32.5 %collective-permute-start.34 = (bf16[256,512]{1,0:T(8,128)(2,1)}, bf16[256,512]{1,0:T(8,128)(2,1)S(1)}, u32[]{:S(2)}, u32[]{:S(2)}) collective-permute-start(bf16[256,512]{1,0:T(8,128)(2,1)} %dynamic-slice_convert_fusion), channel_id=1, source_target_pairs={{0,2},{2,0},{1,3},{3,1},{4,6},{6,4},{5,7},{7,5},{8,10},{10,8},{9,1... | collective-permute-start | bytes 786440 | tf_op jit(solution)/shard_map/ppermute | solution.py:87
  690.7 8.1 %collective-permute-start.32 = (bf16[256,512]{1,0:T(8,128)(2,1)S(1)}, bf16[256,512]{1,0:T(8,128)(2,1)S(1)}, u32[]{:S(2)}, u32[]{:S(2)}) collective-permute-start(bf16[256,512]{1,0:T(8,128)(2,1)S(1)} %dynamic-slice_convert_fusion.1), channel_id=1, source_target_pairs={{0,2},{2,0},{1,3},{3,1},{4,6},{6,4},{5,7},{7,5},{8,10},{10,8},{9,1... | collective-permute-start | bytes 786440 | tf_op jit(solution)/shard_map/ppermute | solution.py:87
  691.4 10.8 %collective-permute-start.36 = (bf16[64,2112]{1,0:T(8,128)(2,1)S(1)}, bf16[64,2112]{1,0:T(8,128)(2,1)S(1)}, u32[]{:S(2)}, u32[]{:S(2)}) collective-permute-start(bf16[64,2112]{1,0:T(8,128)(2,1)S(1)} %dynamic-slice_bitcast_fusion.1), channel_id=1, source_target_pairs={{0,64},{64,0},{1,65},{65,1},{2,66},{66,2},{3,67},{67,3},{4,68},{68... | collective-permute-start | bytes 811016 | tf_op jit(solution)/shard_map/shared_weight_grads/ppermute | solution.py:87
  (66 other events, 388.5 us)
Sparse Core Ops, SparseCore 0:
  11.7 133.0 all-gather.4
  269.4 112.4 all-gather.6
  427.9 102.4 reduce-scatter.2
  534.0 103.0 reduce-scatter.4

commit v3 on v2

--- a/solution.py
+++ b/solution.py
@@ -103,12 +103,6 @@
     )
 
 
-def gather_ctx(value, name):
-    with jax.named_scope(name):
-        gathered = lax.all_gather(value, CTX, axis=0, tiled=False)
-        return gathered.reshape((2, 16) + value.shape)
-
-
 def scatter_yx(value, name):
     with jax.named_scope(name):
         pair = lax.psum_scatter(value, ("y", "x"), scatter_dimension=0, tiled=True)
@@ -172,7 +166,7 @@
     return lax.dynamic_slice_in_dim(half, zl * QUARTER, QUARTER, 1) + arrived.astype(f32)
 
 
-def call(body, outs, name, flops, scratch=(), limit=56):
+def call(body, outs, name, flops, scratch=(), limit=26):
     def run(scalars, *arrays):
         spec = pl.BlockSpec(memory_space=pltpu.VMEM)
         moved = sum(a.size * a.dtype.itemsize for a in arrays)
@@ -414,7 +408,7 @@
 
 
 def finish_rows_kernel(core_ref, own_ref, arrived_ref, dot_ref, dot_arrived_ref, sent_ref):
-    slot_row = lax.broadcasted_iota(jnp.int32, (N_CTX, SLOTS, HALF), 1)
+    slot_row = lax.broadcasted_iota(jnp.int32, own_ref.shape, 1)
     rows = own_ref[...].astype(f32) + arrived_ref[...].astype(f32)
     dots = (dot_ref[:1] + dot_arrived_ref[:1]).reshape(1, 1, HALF)
     sent_ref[...] = jnp.where(slot_row == CAP, dots, rows).astype(bf16)
@@ -480,16 +474,16 @@
 
 def input_back_kernel(
     core_ref, compressed_ref, down_ref, normed_ref, part_ref, input_ref, root_ref, gain_ref,
-    own_ref, send_ref, gain_grad_ref, down_grad_ref, total_ref,
+    logit_ref, normed_two_ref, gain_two_ref, gain_kv_ref,
+    own_ref, send_ref, small_ref, total_ref,
 ):
     core, zl = core_ref[0], core_ref[1]
     quarter = quarter_at(zl, core)
     compressed = compressed_ref[...]
-    down_grad_ref[...] = tn(compressed, normed_ref[:, quarter]).astype(bf16)
     total_ref[...] = part_ref[...]
     total_ref[:, quarter] += nn(compressed, down_ref[...])
     grad, source, root = total_ref[...], input_ref[...].astype(f32), root_ref[...]
-    gain_grad_ref[...] = jnp.sum(grad * source * root, axis=0, keepdims=True)
+    gain_one = jnp.sum(grad * source * root, axis=0, keepdims=True)
     scaled = grad * gain_ref[...]
     mean = jnp.sum(scaled * source, axis=1, keepdims=True) * (1.0 / WIDTH)
     total_ref[...] = root * scaled - source * (root * root * root * mean)
@@ -497,6 +491,22 @@
         mine = slice(z * QUARTER, (z + 1) * QUARTER)
         own_ref[:, mine] = total_ref[:, quarter_at(z, core)]
         send_ref[:, mine] = total_ref[:, quarter_at(z, 1 - core)].astype(bf16)
+    column = lax.broadcasted_iota(jnp.int32, (KEYS, N_CTX * 32), 1)
+    place = (column >> 5) * 18 + (column & 31)
+    same = (place == lax.broadcasted_iota(jnp.int32, place.shape, 0)) & ((column & 31) < 18)
+    spread = nn(compressed, jnp.where(same, 1.0, 0.0).astype(bf16)).astype(bf16)
+    down = tn(spread, normed_ref[:, quarter]).reshape(N_CTX, 32, QUARTER)
+    router = nn(logit_ref[...], normed_two_ref[:, quarter])
+    row = lax.broadcasted_iota(jnp.int32, down.shape, 1)
+    small = down
+    for e in range(EXP_DEV):
+        small = jnp.where(row == 18 + e, router[e * N_CTX : (e + 1) * N_CTX][:, None, :], small)
+    for k in range(4):
+        part = slice(k * QUARTER, (k + 1) * QUARTER)
+        small = jnp.where(row == 20 + k, gain_one[:, part][None], small)
+        small = jnp.where(row == 24 + k, gain_two_ref[:, part][None], small)
+    small = jnp.where(row == 28, gain_kv_ref[...][None], small)
+    small_ref[...] = small.astype(bf16)
 
 
 def expert_grads_kernel(
@@ -560,6 +570,12 @@
         dots = column_of(back_ref[:, CAP, :], core_ref[1])
         prob_ref[part] = jnp.sum((hot * dots).reshape(N_CTX, SLOTS, TOK), axis=1)
     half_ref[...] = half.astype(bf16)
+
+
+def outputs_two_kernel(core_ref, back_ref, slot_ref, probs_ref, own_ref, half_ref):
+    hot = one_hot(slot_ref[...]).reshape(N_CTX, SLOTS, TOK) * probs_ref[...][:, None, :]
+    hot = hot.reshape(N_CTX * SLOTS, TOK).astype(bf16)
+    half_ref[...] = own_ref[...] + tn(hot, back_ref[...].reshape(N_CTX * SLOTS, HALF))
 
 
 def outputs_kernel(core_ref, back_ref, slot_ref, probs_ref, own_ref, arrived_ref, half_ref):
@@ -915,9 +931,9 @@
         jnp.concatenate([shared_gate, shared_up, shared_down.T], axis=1), "zh", 0
     )
     up_mine = latent_up.reshape(16, HEADS, NOPE + VDIM).transpose(1, 0, 2).reshape(64, NOPE + VDIM)
-    attn_all = gather_ctx(
-        jnp.concatenate([query_weight, output_weight.T, up_mine], axis=1), "attn_weights"
-    )
+    with jax.named_scope("attn_weights"):
+        attn_mine = jnp.concatenate([query_weight, output_weight.T, up_mine], axis=1)
+        attn_all = lax.all_gather(attn_mine, CTX, tiled=False).reshape(2, 16, 64, 1536)
 
     core_is = jnp.stack([core, ctx])
     slot_by, grad_sent = call(
@@ -973,7 +989,7 @@
         ],
         axis=1,
     )
-    latent_ctx = after(share_ctx(latent_rows, "latents"), grad_sent)
+    latent_ctx = after(share_ctx(after(latent_rows, shared_pair_mine), "latents"), grad_sent)
     latent_mine = latent_ctx[pairs]
     latent_zl = swap(latent_mine, "zl")
     latent_core = swap(jnp.stack([latent_mine, latent_zl]), "core")
@@ -1027,25 +1043,28 @@
     )
     two = after(two, dots)
     two_other = swap(two, "core")
-    (sent_one,) = call(finish_rows_kernel, [buffer], "finish_rows", 1)(
+    (sent_one,) = call(finish_rows_kernel, [buffer], "finish_rows", 1, limit=20)(
         core_is, after(back_own, two), swap(back_send, "core"), dots, swap(dots, "core")
     )
     back_one = exchange_ctx(sent_one, "row_grads_back", two)
     back_own, back_send, y_two, y_two_send, dots, *units_two = expert(
         1, core_is, two, two_other, grad_own, grad_other, *weights
     )
-    (sent_two,) = call(finish_rows_kernel, [buffer], "finish_rows", 1)(
+    (sent_two,) = call(finish_rows_kernel, [buffer], "finish_rows", 1, limit=20)(
         core_is, back_own, swap(after(back_send, back_one), "core"), dots,
         swap(after(dots, back_one), "core"),
     )
     back_two = exchange_ctx(sent_two, "row_grads_back", back_one)
 
     with jax.named_scope("shared_weights"):
-        shared_all = lax.all_gather(after(shared_pair_mine, one), ("y", "x"), tiled=False)
+        shared_all = lax.all_gather(after(shared_pair_mine, latent_core), ("y", "x"), tiled=False)
     shared_own, shared_send, in_own, in_send, shared_grads = shared(
         core_is, after(normed_two, sent_two), grad_out, shared_all
     )
-    back_two = after(back_two, in_own)
+    (outs_one,) = call(add_kernel, [buffer], "outputs_sum", 1)(
+        core_is, after(y_one, sent_two), swap(y_one_send, "core")
+    )
+    back_two = after(back_two, (in_own, outs_one))
 
     in_half, prob_grad = call(
         combine_kernel,
@@ -1053,9 +1072,6 @@
         "combine",
         4 * N_CTX * SLOTS * TOK * HALF,
     )(core_is, back_one, back_two, slot_by, in_own, swap(in_send, "core"))
-    (outs_one,) = call(add_kernel, [buffer], "outputs_sum", 1)(
-        core_is, after(y_one, in_half), swap(y_one_send, "core")
-    )
     prob_grad = prob_grad + swap(prob_grad, "zl")
     in_half = in_half.astype(f32) + swap(in_half, "zl").astype(f32)
     in_other = swap(in_half, "core")
@@ -1068,10 +1084,17 @@
         grad_out, router_t, probs, prob_grad, attn_all, query, keys, value, log_total,
     )
     grad_query_lat = grad_query_lat.reshape(HEADS, TOK, KEYS)
-    normed_two_quarter = lax.dynamic_slice_in_dim(normed_two, column_start, QUARTER, 1)
-    router_part = nn(logit_grad, normed_two_quarter).reshape(EXP_DEV, N_CTX, QUARTER)
-    router_part = router_part.transpose(1, 0, 2)
-    gain_two_mine = pick(gain_two_part.reshape(N_CTX, 4, 16), ws, 1)
+
+    attn_parts, normed_one_part = call(
+        query_back_kernel,
+        [out((16, 2, 64, 1536), bf16), out((TOK, WIDTH), f32)],
+        "query_back",
+        2 * TOK * WIDTH * 2048 + 2 * TOK * RANK * 1536,
+        limit=48,
+    )(
+        core_is, after(grad_query_lat, outs_one), query_nope, normed_one, attn_all, cos, sin,
+        value.reshape(HEADS, TOK, RANK), head_grad, attn_grad, head_flat,
+    )
 
     keys_mine, keys_other = call(
         key_split_kernel,
@@ -1079,29 +1102,27 @@
         "key_split",
         1,
     )(jnp.concatenate([place_of, zl[None]]), after(keys_own, outs_one), swap(keys_send, "core"))
+    keys_arrived = swap(keys_other, "zl")
     (keys_sent,) = call(key_spread_kernel, [out((N_CTX, 64, KEYS), bf16)], "key_spread", 1)(
-        pairs, keys_mine, swap(keys_other, "zl")
+        pairs, keys_mine, after(keys_arrived, normed_one_part)
+    )
+    (outs_two,) = call(add_kernel, [buffer], "outputs_sum", 1)(
+        core_is, after(y_two, keys_sent), swap(y_two_send, "core")
     )
     keys_back = exchange_ctx(keys_sent, "key_grads")
-
-    attn_parts, normed_one_part = call(
-        query_back_kernel,
-        [out((16, 2, 64, 1536), bf16), out((TOK, WIDTH), f32)],
-        "query_back",
-        2 * TOK * WIDTH * 2048 + 2 * TOK * RANK * 1536,
-    )(
-        core_is, after(grad_query_lat, keys_other), query_nope, normed_one, attn_all, cos, sin,
-        value.reshape(HEADS, TOK, RANK), head_grad, attn_grad, head_flat,
-    )
 
     half_out = out((TOK, HALF), f32)
     (routed_half,) = call(outputs_kernel, [half_out], "outputs", 1)(
         core_is, after(outs_one, keys_sent), slot_by[:N_CTX], probs[:N_CTX],
         shared_own, swap(shared_send, "core"),
     )
-    (outs_two,) = call(add_kernel, [buffer], "outputs_sum", 1)(
-        core_is, after(y_two, keys_sent), swap(y_two_send, "core")
-    )
+    shared_pair = scatter_yx(
+        after(shared_grads, back_two).reshape(WIDTH, 3 * FF_SH), "shared_weight_grads"
+    )
+    attn_pair = scatter_yx(
+        after(attn_parts, (shared_pair, keys_sent)).reshape(WIDTH, 1536), "attn_weight_grads"
+    )
+    shared_sum = scatter_zh(shared_pair, "shared_weight_grads")
 
     filled = expert_grads(
         core_is, (one, one_other, two, two_other), (grad_own, grad_other),
@@ -1110,8 +1131,8 @@
     grad_expert_gate = filled[0].transpose(0, 2, 1)
     grad_expert_up = filled[1].transpose(0, 2, 1)
     grad_expert_down = filled[2]
-    keys_back = after(keys_back, (filled[0], normed_one_part, routed_half, outs_two))
-
+
+    keys_back = after(keys_back, (routed_half, shared_sum, filled[0], outs_two))
     compressed_grad, gain_kv_part = call(
         latent_back_kernel, [out((64, KEYS), bf16), out((1, RANK), f32)], "latent_back", 1
     )(
@@ -1119,61 +1140,47 @@
         lax.dynamic_slice_in_dim(cos, row_start, 64), lax.dynamic_slice_in_dim(sin, row_start, 64),
     )
     compressed_grad = gather_two(gather_two(compressed_grad, "core", 0), "zl", 0).reshape(TOK, KEYS)
-    input_own, input_send, gain_one_part, grad_down_part = call(
+    outs_two = exchange_ctx(after(outs_two, compressed_grad), "outputs_back")
+    input_own, input_send, small_parts = call(
         input_back_kernel,
         [
             out((TOK, HALF), f32),
             out((TOK, HALF), bf16),
-            out((1, WIDTH), f32),
-            out((KEYS, QUARTER), bf16),
+            out((N_CTX, 32, QUARTER), bf16),
         ],
         "input_back",
         4 * TOK * KEYS * QUARTER,
         [pltpu.VMEM((TOK, WIDTH), f32)],
     )(
         jnp.stack([core, zl]), compressed_grad, down_t, normed_one, normed_one_part, hidden_in,
-        root_one, gain_one.reshape(1, WIDTH),
-    )
-    grad_down_part = grad_down_part.reshape(N_CTX, 18, QUARTER)
+        root_one, gain_one.reshape(1, WIDTH), logit_grad, normed_two, gain_two_part, gain_kv_part,
+    )
     input_quarter = zl_quarter(input_own + swap(input_send, "core").astype(f32), zl)
     grad_in = lax.dynamic_slice_in_dim(after_grad, column_start, QUARTER, 1) + input_quarter
-    gain_parts = jnp.concatenate(
-        [gain_one_part.reshape(N_CTX, 2, 2, 16), gain_kv_part.reshape(N_CTX, 2, 2, 4)], axis=-1
-    )
-    gain_core = pick(gain_parts, core, 2) + swap(pick(gain_parts, 1 - core, 2), "core")
-    gain_mine = pick(gain_core, zl, 1) + swap(pick(gain_core, 1 - zl, 1), "zl")
-
-    shared_pair = scatter_yx(
-        after(shared_grads, back_two).reshape(WIDTH, 3 * FF_SH), "shared_weight_grads"
-    )
-    attn_pair = scatter_yx(
-        after(attn_parts, shared_pair).reshape(WIDTH, 1536), "attn_weight_grads"
-    )
-    shared_sum = scatter_zh(shared_pair, "shared_weight_grads")
+
     attn_sum = scatter_zh(attn_pair, "attn_weight_grads")
-    gain_rows = jnp.concatenate([gain_mine, gain_two_mine], axis=1)
-    gain_rows = jnp.pad(gain_rows, ((0, 0), (0, QUARTER - 36)))[:, None, :]
-    small_parts = jnp.concatenate(
-        [
-            grad_down_part,
-            router_part.astype(bf16),
-            gain_rows.astype(bf16),
-            jnp.zeros((N_CTX, 3, QUARTER), bf16),
-        ],
-        axis=1,
-    )
-    small_back = exchange_ctx(small_parts, "small_weight_grads", keys_back)
-    small_sum = jnp.sum(small_back.astype(f32), axis=0)
-    outs_two = exchange_ctx(outs_two, "outputs_back", small_back)
-    (routed_half,) = call(outputs_kernel, [half_out], "outputs", 1)(
-        core_is, outs_two, slot_by[N_CTX:], probs[N_CTX:], routed_half,
-        jnp.zeros((TOK, HALF), bf16),
+    (routed_half,) = call(outputs_two_kernel, [half_out], "outputs_two", 1)(
+        core_is, outs_two, slot_by[N_CTX:], probs[N_CTX:], routed_half
     )
     layer_out = (
         lax.dynamic_slice_in_dim(hidden_in, column_start, QUARTER, 1).astype(f32)
         + lax.dynamic_slice_in_dim(attn_half, zl * QUARTER, QUARTER, 1)
         + zl_quarter(routed_half, zl)
     ).astype(bf16)
+    small_back = exchange_ctx(small_parts, "small_weight_grads", outs_two)
+    small_back = after(small_back, (attn_sum, layer_out, grad_in))
+    small_sum = jnp.sum(small_back.astype(f32), axis=0)
+    lane = lax.rem(ctx, 8) * 64
+    gain_one_rows = lax.dynamic_slice(small_sum, (20 + ctx // 8, lane), (1, 64))
+    gain_two_rows = lax.dynamic_slice(small_sum, (24 + ctx // 8, lane), (1, 64))
+    gain_kv_rows = lax.dynamic_slice(small_sum, (28, ctx * 16), (1, 16))
+    gain_parts = jnp.concatenate(
+        [gain_one_rows.reshape(2, 2, 16), gain_kv_rows.reshape(2, 2, 4)], axis=-1
+    )
+    gain_core = pick(gain_parts, core, 1) + swap(pick(gain_parts, 1 - core, 1), "core")
+    gain_mine = pick(gain_core, zl, 0) + swap(pick(gain_core, 1 - zl, 0), "zl")
+    gain_two_mine = lax.dynamic_slice_in_dim(gain_two_rows[0], ws * 16, 16)
+
     up_sum = (
         attn_sum[:, 768 + QUARTER :]
         .reshape(HEADS, 16, NOPE + VDIM)
@@ -1183,9 +1190,9 @@
     return (
         layer_out,
         grad_in,
-        small_sum[20, :16],
-        small_sum[20, 16:20],
-        small_sum[20, 20:36],
+        gain_mine[:16],
+        gain_mine[16:],
+        gain_two_mine,
         attn_sum[:, :768],
         small_sum[:18].T,
         up_sum,

time: 729 us -> 676 us (0.927)
  waiting for transfers between devices: 299 us -> 251 us
  Pallas kernels: 206 us -> 172 us
  blocking collectives: 19.9 us -> 48.8 us
  local copies, waits for them, and re-layouts: 48.3 us -> 65.1 us
  starting transfers between devices: 97.1 us -> 89.1 us
  other arithmetic: 33.3 us -> 25.3 us
    pallas_call x16, Pallas kernels: 77.3 us -> 43 us  [run(): pl.pallas_call(body, in_specs=[pl.BlockSpec(memory_space=pltpu.SMEM)] + [...]
    all_to_all x10, waiting for transfers between devices: 142 us -> 109 us  [exchange_ctx(): return lax.all_to_all(value, CTX, 0, 0, tiled=True)]
    ppermute x37, waiting for transfers between devices: 147 us -> 117 us  [shift(): lax.ppermute(value, axis, [(i, (i + step) % size) for i in range(size)])]
    all_to_all x1, blocking collectives: 19.9 us -> 48.8 us  [exchange_ctx(): return lax.all_to_all(value, CTX, 0, 0, tiled=True)]
    unnamed x96 -> x166, local copies, waits for them, and re-layouts: 15.3 us -> 39.1 us
    reduce_scatter x2, waiting for transfers between devices: 10.4 us -> 23.9 us  [scatter_yx(): pair = lax.psum_scatter(value, ('y', 'x'), scatter_dimension=0, tiled=True)]
  transfers between devices with their start and end apart: 51 -> 51, of which waited for: 34 -> 31; matrix products, arithmetic and copies ran while one was open for 9% -> 7% of each run, Pallas kernels for 29% -> 26%
where the time goes in v3:
time: 676 us; the launch traced here: 667 us
  waiting for transfers between devices  251 us (37%)
  Pallas kernels  172 us (25%)
  starting transfers between devices  89.1 us (13%)
  local copies, waits for them, and re-layouts  65.1 us (10%)
  blocking collectives  48.8 us (7%)
  other arithmetic  25.3 us (4%)
  between operations  15.6 us (2%)
    ppermute x37, waiting for transfers between devices, shift(): lax.ppermute(value, axis, [(i, (i + step) % size) for i in range(size)])  117 us
    all_to_all x10, waiting for transfers between devices, exchange_ctx(): return lax.all_to_all(value, CTX, 0, 0, tiled=True)  109 us
    all_to_all x10, starting transfers between devices, exchange_ctx(): return lax.all_to_all(value, CTX, 0, 0, tiled=True)  65.4 us
    all_to_all x1, blocking collectives, exchange_ctx(): return lax.all_to_all(value, CTX, 0, 0, tiled=True)  48.8 us
    pallas_call x16, Pallas kernels, run(): pl.pallas_call(body, in_specs=[pl.BlockSpec(memory_space=pltpu.SMEM)] + [...  43 us
    pallas_call x2, Pallas kernels, expert(): pl.pallas_call(expert_kernel, grid=(total // step,), in_specs=[pl.BlockSp...  40.4 us
    unnamed x166, local copies, waits for them, and re-layouts  39.1 us
    pallas_call x1, Pallas kernels, attend_back(): pl.pallas_call(attend_back_kernel, grid_spec=pltpu.PrefetchScalarGridSpec...  26.8 us
  transfers between devices with their start and end apart: 51, of which 31 were waited for; matrix products, arithmetic and copies ran while one was open for 7% of the time, Pallas kernels for 26%

profile of v3, /device:TPU:0, one launch (start us, length us, event | category | flops | bytes accessed | tf_op | source)
XLA Modules:
  0.0 666.7 jit_solution(6048548324187202757)
XLA Ops:
  25.6 7.9 %all-to-all-start = ((bf16[32,24,512]{2,1,0:T(8,128)(2,1)}), bf16[32,24,512]{2,1,0:T(8,128)(2,1)S(1)}, u32[]{:S(2)}, u32[]{:S(2)}) async-start(bf16[32,24,512]{2,1,0:T(8,128)(2,1)} %broadcast_in_dim.37), calls=%async_computation | async-start | bytes 1572864 | tf_op jit(solution)/shard_map/small_weights/all_to_all | solution.py:127
  34.1 14.9 %all-to-all-done = bf16[32,24,512]{2,1,0:T(8,128)(2,1)S(1)} async-done(((bf16[32,24,512]{2,1,0:T(8,128)(2,1)}), bf16[32,24,512]{2,1,0:T(8,128)(2,1)S(1)}, u32[]{:S(2)}, u32[]{:S(2)}) %all-to-all-start) | async-done | bytes 786464 | tf_op jit(solution)/shard_map/small_weights/all_to_all | solution.py:127
  55.0 5.1 collective-permute-done.3
  63.6 8.5 %all-to-all-start.1 = ((bf16[32,64,576]{2,1,0:T(8,128)(2,1)}), bf16[32,64,576]{2,1,0:T(8,128)(2,1)}, u32[]{:S(2)}, u32[]{:S(2)}) async-start(bf16[32,64,576]{2,1,0:T(8,128)(2,1)} %broadcast_in_dim.42), calls=%async_computation.1 | async-start | bytes 5242880 | tf_op jit(solution)/shard_map/latents/all_to_all | solution.py:127
  77.8 35.6 %all-to-all-done.1 = bf16[32,64,576]{2,1,0:T(8,128)(2,1)} async-done(((bf16[32,64,576]{2,1,0:T(8,128)(2,1)}), bf16[32,64,576]{2,1,0:T(8,128)(2,1)}, u32[]{:S(2)}, u32[]{:S(2)}) %all-to-all-start.1) | async-done | bytes 2359328 | tf_op jit(solution)/shard_map/latents/all_to_all | solution.py:127
  116.7 21.3 %collective-permute-done.5.zl_ref = bf16[8,64,576]{2,1,0:T(8,128)(2,1)S(1)} collective-permute-done((bf16[8,64,576]{2,1,0:T(8,128)(2,1)S(1)}, bf16[8,64,576]{2,1,0:T(8,128)(2,1)S(1)}, u32[]{:S(2)}, u32[]{:S(2)}) %collective-permute-start.5) | collective-permute-done | bytes 589856 | tf_op jit(solution)/shard_map/ppermute | solution.py:87
  142.3 9.4 %all-to-all-start.2 = ((bf16[32,2,32,1024]{3,2,1,0:T(8,128)(2,1)}), bf16[32,2,32,1024]{3,2,1,0:T(8,128)(2,1)}, u32[]{:S(2)}, u32[]{:S(2)}) async-start(bf16[32,2,32,1024]{3,2,1,0:T(8,128)(2,1)} %copy-done.9), calls=%async_computation.2 | async-start | bytes 8388608 | tf_op jit(solution)/shard_map/cotangent_rows/all_to_all | solution.py:127
  167.3 18.8 %attend.1 = (f32[4,2,128,512]{3,2,1,0:T(8,128)}, f32[4,2,128,128]{3,2,1,0:T(8,128)}, bf16[256,512]{1,0:T(8,128)(2,1)}, f32[256,1024]{1,0:T(8,128)}, bf16[256,1024]{1,0:T(8,128)(2,1)}) custom-call(s32[3]{0:T(128)} %pad_add_fusion.place_ref, bf16[4,2,128,576]{3,2,1,0:T(8,128)(2,1)} %bitcast.132, bf16[2048,576]{1,0:T(8,128)(2,1)} %copy-done.10, ...), custom_call_target="tpu_custom_call" | custom-call | flops 2852126720 | bytes 16777216 | tf_op jit(solution)/shard_map/attend/pallas_call | solution.py:675
  190.0 26.3 %collective-permute-done.8 = bf16[256,1024]{1,0:T(8,128)(2,1)S(1)} collective-permute-done((bf16[256,1024]{1,0:T(8,128)(2,1)S(1)}, bf16[256,1024]{1,0:T(8,128)(2,1)S(1)}, u32[]{:S(2)}, u32[]{:S(2)}) %collective-permute-start.8) | collective-permute-done | bytes 524320 | tf_op jit(solution)/shard_map/ppermute | solution.py:87
  234.7 48.8 %all_to_all.55.own_ref.one_ref = bf16[32,32,1024]{2,1,0:T(8,128)(2,1)S(1)} all-to-all(bf16[32,32,1024]{2,1,0:T(8,128)(2,1)S(1)} %get-tuple-element.113), channel_id=1, replica_groups=mesh['zh'=2,'y'=4,'x'=4,'zl'=2,'core'=2] {'zh','y','x'}, dimensions={0} | all-to-all | bytes 4194304 | tf_op jit(solution)/shard_map/rows_to_experts/all_to_all | solution.py:127
  284.8 5.2 all-to-all-start.4
  290.1 20.2 %expert.2 = (bf16[32,32,1024]{2,1,0:T(8,128)(2,1)}, bf16[32,32,1024]{2,1,0:T(8,128)(2,1)}, bf16[32,32,1024]{2,1,0:T(8,128)(2,1)}, bf16[32,32,1024]{2,1,0:T(8,128...) custom-call(s32[2]{0:T(128)} %copy-done.42, ...), custom_call_target="tpu_custom_call" | custom-call | flops 8858370048 | bytes 25165824 | tf_op jit(solution)/shard_map/expert/pallas_call | solution.py:394
  310.3 9.1 %all-to-all-done.4.own_ref.two_ref = bf16[32,32,1024]{2,1,0:T(8,128)(2,1)} async-done(((bf16[32,32,1024]{2,1,0:T(8,128)(2,1)}), bf16[32,32,1024]{2,1,0:T(8,128)(2,1)}, u32[]{:S(2)}, u32[]{:S(2)}) %all-to-all-start.4) | async-done | bytes 2097184 | tf_op jit(solution)/shard_map/rows_to_experts/all_to_all | solution.py:127
  328.3 5.2 all-to-all-start.5
  333.5 20.2 %expert.3 = (bf16[32,32,1024]{2,1,0:T(8,128)(2,1)}, bf16[32,32,1024]{2,1,0:T(8,128)(2,1)}, bf16[32,32,1024]{2,1,0:T(8,128)(2,1)}, bf16[32,32,1024]{2,1,0:T(8,128...) custom-call(s32[2]{0:T(128)} %copy-done.42, ...), custom_call_target="tpu_custom_call" | custom-call | flops 8858370048 | bytes 25165824 | tf_op jit(solution)/shard_map/expert/pallas_call | solution.py:394
  353.7 9.6 %all-to-all-done.5.one_ref = bf16[32,32,1024]{2,1,0:T(8,128)(2,1)S(1)} async-done(((bf16[32,32,1024]{2,1,0:T(8,128)(2,1)}), bf16[32,32,1024]{2,1,0:T(8,128)(2,1)S(1)}, u32[]{:S(2)}, u32[]{:S(2)}) %all-to-all-start.5) | async-done | bytes 2097184 | tf_op jit(solution)/shard_map/row_grads_back/all_to_all | solution.py:127
  363.8 6.9 %collective-permute-done.18.dot_arrived_ref = f32[8,1024]{1,0:T(8,128)S(1)} collective-permute-done((f32[8,1024]{1,0:T(8,128)}, f32[8,1024]{1,0:T(8,128)S(1)}, u32[]{:S(2)}, u32[]{:S(2)}) %collective-permute-start.18) | collective-permute-done | bytes 32800 | tf_op jit(solution)/shard_map/ppermute | solution.py:87
  375.5 5.1 all-to-all-start.6
  385.6 20.0 %shared_experts.1 = (f32[256,1024]{1,0:T(8,128)}, bf16[256,1024]{1,0:T(8,128)(2,1)}, f32[256,1024]{1,0:T(8,128)}, bf16[256,1024]{1,0:T(8,128)(2,1)}, bf16[16,2,64,2112]{3,2,1,0:T(8,128)(2,1)}) custom-call(s32[2]{0:T(128)} %copy-done.42, bf16[256,2048]{1,0:T(8,128)(2,1)} %copy-done.28, bf16[256,2048]{1,0:T(8,128)(2,1)} %grad_ref.5, ...), custom_call_target="tpu_custom_call" | custom-call | flops 6643777536 | bytes 25165824 | tf_op jit(solution)/shard_map/shared_experts/pallas_call | solution.py:342
  417.3 13.6 %collective-permute-done.21 = bf16[256,1024]{1,0:T(8,128)(2,1)S(1)} collective-permute-done((bf16[256,1024]{1,0:T(8,128)(2,1)S(1)}, bf16[256,1024]{1,0:T(8,128)(2,1)S(1)}, u32[]{:S(2)}, u32[]{:S(2)}) %collective-permute-start.21) | collective-permute-done | bytes 524320 | tf_op jit(solution)/shard_map/ppermute | solution.py:87
  437.6 5.3 all-to-all-start.7
  443.0 26.8 %attend_back.1 = (f32[256,2048]{1,0:T(8,128)}, bf16[256,2048]{1,0:T(8,128)(2,1)}, bf16[64,256]{1,0:T(8,128)(2,1)}, f32[1,2048]{1,0:T(1,128)}, bf16[256,512]{1,0:...) custom-call(s32[3]{0:T(128)} %pad_add_fusion.place_ref, ...), custom_call_target="tpu_custom_call" | custom-call | flops 7549747200 | bytes 37748736 | tf_op jit(solution)/shard_map/attend_back/pallas_call | solution.py:861
  470.0 12.3 %all-to-all-done.7.back_ref = bf16[32,32,1024]{2,1,0:T(8,128)(2,1)S(1)} async-done(((bf16[32,32,1024]{2,1,0:T(8,128)(2,1)}), bf16[32,32,1024]{2,1,0:T(8,128)(2,1)S(1)}, u32[]{:S(2)}, u32[]{:S(2)}) %all-to-all-start.7) | async-done | bytes 2097184 | tf_op jit(solution)/shard_map/outputs_back/all_to_all | solution.py:127
  486.1 10.3 %query_back.1 = (bf16[16,2,64,1536]{3,2,1,0:T(8,128)(2,1)}, f32[256,2048]{1,0:T(8,128)S(1)}) custom-call(s32[2]{0:T(128)S(1)} %copy-done.45, f32[4,256,576]{2,1,0:T(8,128)} %bitcast.138, bf16[4,256,128]{2,1,0:T(8,128)(2,1)S(1)} %copy-done.36, bf16[256,2048]{1,0:T(8,128)(2,1)S(1)} %fusion.2.normed_ref, bf16[2,16,64,1536]{3,2,1,0:T(8,128)(2,1)} %bitcast.125, ...), custom_call_target="tpu_custom_call" | custom-call | flops 2550136832 | bytes 22151168 | tf_op jit(solution)/shard_map/query_back/pallas_call | solution.py:174
  503.9 8.6 %reduce-scatter.3.cloned.1.call-done = bf16[128,2112]{1,0:T(8,128)(2,1)} async-done(((bf16[2048,2112]{1,0:T(8,128)(2,1)}), bf16[128,2112]{1,0:T(8,128)(2,1)}) %reduce-scatter.3.cloned.1.call-update) | async-done | bytes 540688 | tf_op jit(solution)/shard_map/shared_weight_grads/reduce_scatter | solution.py:108
  514.5 8.0 %all-to-all-start.8 = ((bf16[32,64,576]{2,1,0:T(8,128)(2,1)}), bf16[32,64,576]{2,1,0:T(8,128)(2,1)}, u32[]{:S(2)}, u32[]{:S(2)}) async-start(bf16[32,64,576]{2,1,0:T(8,128)(2,1)} %copy-done.3), calls=%async_computation.8 | async-start | bytes 5242880 | tf_op jit(solution)/shard_map/key_grads/all_to_all | solution.py:127
  527.4 22.9 %expert_grads.1 = (f32[2,352,2048]{2,1,0:T(8,128)}, f32[2,352,2048]{2,1,0:T(8,128)}, f32[2,352,2048]{2,1,0:T(8,128)}) custom-call(s32[2]{0:T(128)} %copy-done.42, bf16[32,32,1024]{2,1,0:T(8,128)(2,1)} %copy-done.59, bf16[32,32,1024]{2,1,0:T(8,128)(2,1)} %collective-permute-done.12.other_ref.one_other_ref, ...), custom_call_target="tpu_custom_call" | custom-call | flops 8858370048 | bytes 37748736 | tf_op jit(solution)/shard_map/expert_grads/pallas_call | solution.py:547
  558.0 8.7 %all-to-all-done.8.back_ref = bf16[32,64,576]{2,1,0:T(8,128)(2,1)} async-done(((bf16[32,64,576]{2,1,0:T(8,128)(2,1)}), bf16[32,64,576]{2,1,0:T(8,128)(2,1)}, u32[]{:S(2)}, u32[]{:S(2)}) %all-to-all-start.8) | async-done | bytes 2359328 | tf_op jit(solution)/shard_map/key_grads/all_to_all | solution.py:127
  571.0 5.6 collective-permute-done.30
  599.7 14.7 %all-to-all-done.9.back_ref = bf16[32,32,1024]{2,1,0:T(8,128)(2,1)} async-done(((bf16[32,32,1024]{2,1,0:T(8,128)(2,1)}), bf16[32,32,1024]{2,1,0:T(8,128)(2,1)}, u32[]{:S(2)}, u32[]{:S(2)}) %all-to-all-start.9) | async-done | bytes 2097184 | tf_op jit(solution)/shard_map/outputs_back/all_to_all | solution.py:127
  620.5 6.0 all-to-all-start.10
  626.5 15.2 %reduce-scatter.5.cloned.1.call-done = bf16[128,1536]{1,0:T(8,128)(2,1)} async-done(((bf16[2048,1536]{1,0:T(8,128)(2,1)}), bf16[128,1536]{1,0:T(8,128)(2,1)}) %reduce-scatter.5.cloned.1.call-update) | async-done | bytes 393232 | tf_op jit(solution)/shard_map/attn_weight_grads/reduce_scatter | solution.py:108
  (382 shorter events, 195.0 us)
Async XLA Ops:
  7.2 152.3 %all-gather.5.cloned.1.call-start = ((), (), s32[]{:S(2)}) async-start(), calls=%async_computation.15 | async-start | bytes 6488064 | tf_op jit(solution)/shard_map/attn_weights/all_gather | solution.py:936
  11.7 40.0 %collective-permute-start.4 = (bf16[64,2112]{1,0:T(8,128)(2,1)S(1)}, bf16[64,2112]{1,0:T(8,128)(2,1)S(1)}, u32[]{:S(2)}, u32[]{:S(2)}) collective-permute-start(bf16[64,2112]{1,0:T(8,128)(2,1)S(1)} %concatenate.44), channel_id=1, source_target_pairs={{0,64},{64,0},{1,65},{65,1},{2,66},{66,2},{3,67},{67,3},{4,68},{68... | collective-permute-start | bytes 811016 | tf_op jit(solution)/shard_map/ppermute | solution.py:87
  25.6 23.3 %all-to-all-start = ((bf16[32,24,512]{2,1,0:T(8,128)(2,1)}), bf16[32,24,512]{2,1,0:T(8,128)(2,1)S(1)}, u32[]{:S(2)}, u32[]{:S(2)}) async-start(bf16[32,24,512]{2,1,0:T(8,128)(2,1)} %broadcast_in_dim.37), calls=%async_computation | async-start | bytes 1572864 | tf_op jit(solution)/shard_map/small_weights/all_to_all | solution.py:127
  63.6 49.8 %all-to-all-start.1 = ((bf16[32,64,576]{2,1,0:T(8,128)(2,1)}), bf16[32,64,576]{2,1,0:T(8,128)(2,1)}, u32[]{:S(2)}, u32[]{:S(2)}) async-start(bf16[32,64,576]{2,1,0:T(8,128)(2,1)} %broadcast_in_dim.42), calls=%async_computation.1 | async-start | bytes 5242880 | tf_op jit(solution)/shard_map/latents/all_to_all | solution.py:127
  115.8 22.1 %collective-permute-start.5 = (bf16[8,64,576]{2,1,0:T(8,128)(2,1)S(1)}, bf16[8,64,576]{2,1,0:T(8,128)(2,1)S(1)}, u32[]{:S(2)}, u32[]{:S(2)}) collective-permute-start(bf16[8,64,576]{2,1,0:T(8,128)(2,1)S(1)} %gather_fusion.1), channel_id=1, source_target_pairs={{0,2},{2,0},{1,3},{3,1},{4,6},{6,4},{5,7},{7,5},{8,10},{10,8},{9,1... | collective-permute-start | bytes 1769480 | tf_op jit(solution)/shard_map/ppermute | solution.py:87
  142.3 87.0 %all-to-all-start.2 = ((bf16[32,2,32,1024]{3,2,1,0:T(8,128)(2,1)}), bf16[32,2,32,1024]{3,2,1,0:T(8,128)(2,1)}, u32[]{:S(2)}, u32[]{:S(2)}) async-start(bf16[32,2,32,1024]{3,2,1,0:T(8,128)(2,1)} %copy-done.9), calls=%async_computation.2 | async-start | bytes 8388608 | tf_op jit(solution)/shard_map/cotangent_rows/all_to_all | solution.py:127
  151.8 233.8 %all-gather.7.cloned.1.call-start = ((), (), s32[]{:S(2)}) async-start(), calls=%async_computation.16 | async-start | bytes 9469952 | tf_op jit(solution)/shard_map/shared_weights/all_gather | solution.py:1060
  189.6 26.8 %collective-permute-start.8 = (bf16[256,1024]{1,0:T(8,128)(2,1)S(1)}, bf16[256,1024]{1,0:T(8,128)(2,1)S(1)}, u32[]{:S(2)}, u32[]{:S(2)}) collective-permute-start(bf16[256,1024]{1,0:T(8,128)(2,1)S(1)} %add_convert_fusion), channel_id=1, source_target_pairs={{0,2},{2,0},{1,3},{3,1},{4,6},{6,4},{5,7},{7,5},{8,10},{10,8},{9,1... | collective-permute-start | bytes 1572872 | tf_op jit(solution)/shard_map/ppermute | solution.py:87
  216.5 12.9 %collective-permute-start.9 = (f32[256,1024]{1,0:T(8,128)S(1)}, f32[256,1024]{1,0:T(8,128)}, u32[]{:S(2)}, u32[]{:S(2)}) collective-permute-start(f32[256,1024]{1,0:T(8,128)S(1)} %convert_add_fusion.2.own_ref.sum_own_ref), channel_id=1, source_target_pairs={{0,1},{1,0},{2,3},{3,2},{4,5},{5,4},{6,7},{7,6},{8,9},{9,8},{10,11... | collective-permute-start | bytes 3145736 | tf_op jit(solution)/shard_map/ppermute | solution.py:87
  229.3 60.7 %collective-permute-start.13 = (bf16[32,2,32,1024]{3,2,1,0:T(8,128)(2,1)}, bf16[32,2,32,1024]{3,2,1,0:T(8,128)(2,1)}, u32[]{:S(2)}, u32[]{:S(2)}) collective-permute-start(bf16[32,2,32,1024]{3,2,1,0:T(8,128)(2,1)} %all-to-all-done.2.grad_own_ref.ga_ref), channel_id=1, source_target_pairs={{0,1},{1,0},{2,3},{3,2},{4,5},{5,4},{6,7},{7,6},{8,9},{9,8},{10,11... | collective-permute-start | bytes 12582920 | tf_op jit(solution)/shard_map/ppermute | solution.py:87
  284.8 34.6 %all-to-all-start.4 = ((bf16[32,32,1024]{2,1,0:T(8,128)(2,1)}), bf16[32,32,1024]{2,1,0:T(8,128)(2,1)}, u32[]{:S(2)}, u32[]{:S(2)}) async-start(bf16[32,32,1024]{2,1,0:T(8,128)(2,1)} %copy-done.19), calls=%async_computation.4 | async-start | bytes 4194304 | tf_op jit(solution)/shard_map/rows_to_experts/all_to_all | solution.py:127
  310.2 13.3 %collective-permute-start.15 = (bf16[32,32,1024]{2,1,0:T(8,128)(2,1)}, bf16[32,32,1024]{2,1,0:T(8,128)(2,1)S(1)}, u32[]{:S(2)}, u32[]{:S(2)}) collective-permute-start(bf16[32,32,1024]{2,1,0:T(8,128)(2,1)} %get-tuple-element.120), channel_id=1, source_target_pairs={{0,1},{1,0},{2,3},{3,2},{4,5},{5,4},{6,7},{7,6},{8,9},{9,8},{10,11... | collective-permute-start | bytes 6291464 | tf_op jit(solution)/shard_map/ppermute | solution.py:87
  319.5 14.0 %collective-permute-start.14 = (bf16[32,32,1024]{2,1,0:T(8,128)(2,1)}, bf16[32,32,1024]{2,1,0:T(8,128)(2,1)}, u32[]{:S(2)}, u32[]{:S(2)}) collective-permute-start(bf16[32,32,1024]{2,1,0:T(8,128)(2,1)} %all-to-all-done.4.own_ref.two_ref), channel_id=1, source_target_pairs={{0,1},{1,0},{2,3},{3,2},{4,5},{5,4},{6,7},{7,6},{8,9},{9,8},{10,11... | collective-permute-start | bytes 6291464 | tf_op jit(solution)/shard_map/ppermute | solution.py:87
  328.3 35.0 %all-to-all-start.5 = ((bf16[32,32,1024]{2,1,0:T(8,128)(2,1)}), bf16[32,32,1024]{2,1,0:T(8,128)(2,1)S(1)}, u32[]{:S(2)}, u32[]{:S(2)}) async-start(bf16[32,32,1024]{2,1,0:T(8,128)(2,1)} %copy-done.6), calls=%async_computation.5 | async-start | bytes 4194304 | tf_op jit(solution)/shard_map/row_grads_back/all_to_all | solution.py:127
  363.3 7.4 %collective-permute-start.17 = (bf16[32,32,1024]{2,1,0:T(8,128)(2,1)}, bf16[32,32,1024]{2,1,0:T(8,128)(2,1)S(1)}, u32[]{:S(2)}, u32[]{:S(2)}) collective-permute-start(bf16[32,32,1024]{2,1,0:T(8,128)(2,1)} %get-tuple-element.124), channel_id=1, source_target_pairs={{0,1},{1,0},{2,3},{3,2},{4,5},{5,4},{6,7},{7,6},{8,9},{9,8},{10,11... | collective-permute-start | bytes 6291464 | tf_op jit(solution)/shard_map/ppermute | solution.py:87
  363.3 17.3 %collective-permute-start.19 = (bf16[32,32,1024]{2,1,0:T(8,128)(2,1)}, bf16[32,32,1024]{2,1,0:T(8,128)(2,1)}, u32[]{:S(2)}, u32[]{:S(2)}) collective-permute-start(bf16[32,32,1024]{2,1,0:T(8,128)(2,1)} %get-tuple-element.134), channel_id=1, source_target_pairs={{0,1},{1,0},{2,3},{3,2},{4,5},{5,4},{6,7},{7,6},{8,9},{9,8},{10,11... | collective-permute-start | bytes 6291464 | tf_op jit(solution)/shard_map/ppermute | solution.py:87
  375.5 34.6 %all-to-all-start.6 = ((bf16[32,32,1024]{2,1,0:T(8,128)(2,1)}), bf16[32,32,1024]{2,1,0:T(8,128)(2,1)}, u32[]{:S(2)}, u32[]{:S(2)}) async-start(bf16[32,32,1024]{2,1,0:T(8,128)(2,1)} %copy-done.5), calls=%async_computation.6 | async-start | bytes 4194304 | tf_op jit(solution)/shard_map/row_grads_back/all_to_all | solution.py:127
  380.6 132.0 %reduce-scatter.3.cloned.1.call-start = ((), (), s32[]{:S(2)}) async-start(), calls=%async_computation.13 | async-start | bytes 9469952 | tf_op jit(solution)/shard_map/shared_weight_grads/reduce_scatter | solution.py:108
  416.9 14.0 %collective-permute-start.21 = (bf16[256,1024]{1,0:T(8,128)(2,1)S(1)}, bf16[256,1024]{1,0:T(8,128)(2,1)S(1)}, u32[]{:S(2)}, u32[]{:S(2)}) collective-permute-start(bf16[256,1024]{1,0:T(8,128)(2,1)S(1)} %get-tuple-element.137), channel_id=1, source_target_pairs={{0,2},{2,0},{1,3},{3,1},{4,6},{6,4},{5,7},{7,5},{8,10},{10,8},{9,1... | collective-permute-start | bytes 1572872 | tf_op jit(solution)/shard_map/ppermute | solution.py:87
  437.6 44.7 %all-to-all-start.7 = ((bf16[32,32,1024]{2,1,0:T(8,128)(2,1)}), bf16[32,32,1024]{2,1,0:T(8,128)(2,1)S(1)}, u32[]{:S(2)}, u32[]{:S(2)}) async-start(bf16[32,32,1024]{2,1,0:T(8,128)(2,1)} %outputs_sum.2), calls=%async_computation.7 | async-start | bytes 4194304 | tf_op jit(solution)/shard_map/outputs_back/all_to_all | solution.py:127
  442.9 198.9 %reduce-scatter.5.cloned.1.call-start = ((), (), s32[]{:S(2)}) async-start(), calls=%async_computation.14 | async-start | bytes 6684672 | tf_op jit(solution)/shard_map/attn_weight_grads/reduce_scatter | solution.py:108
  469.8 12.5 %collective-permute-start.24 = (bf16[16,64,576]{2,1,0:T(8,128)(2,1)}, bf16[16,64,576]{2,1,0:T(8,128)(2,1)}, u32[]{:S(2)}, u32[]{:S(2)}) collective-permute-start(bf16[16,64,576]{2,1,0:T(8,128)(2,1)} %get-tuple-element.146), channel_id=1, source_target_pairs={{0,1},{1,0},{2,3},{3,2},{4,5},{5,4},{6,7},{7,6},{8,9},{9,8},{10,11... | collective-permute-start | bytes 3538952 | tf_op jit(solution)/shard_map/ppermute | solution.py:87
  485.5 15.9 %collective-permute-start.25 = (bf16[8,64,576]{2,1,0:T(8,128)(2,1)S(1)}, bf16[8,64,576]{2,1,0:T(8,128)(2,1)S(1)}, u32[]{:S(2)}, u32[]{:S(2)}) collective-permute-start(bf16[8,64,576]{2,1,0:T(8,128)(2,1)S(1)} %get-tuple-element.148), channel_id=1, source_target_pairs={{0,2},{2,0},{1,3},{3,1},{4,6},{6,4},{5,7},{7,5},{8,10},{10,8},{9,1... | collective-permute-start | bytes 1769480 | tf_op jit(solution)/shard_map/ppermute | solution.py:87
  512.6 37.7 %collective-permute-start.26 = (bf16[32,32,1024]{2,1,0:T(8,128)(2,1)}, bf16[32,32,1024]{2,1,0:T(8,128)(2,1)}, u32[]{:S(2)}, u32[]{:S(2)}) collective-permute-start(bf16[32,32,1024]{2,1,0:T(8,128)(2,1)} %get-tuple-element.158), channel_id=1, source_target_pairs={{0,1},{1,0},{2,3},{3,2},{4,5},{5,4},{6,7},{7,6},{8,9},{9,8},{10,11... | collective-permute-start | bytes 6291464 | tf_op jit(solution)/shard_map/ppermute | solution.py:87
  514.5 52.2 %all-to-all-start.8 = ((bf16[32,64,576]{2,1,0:T(8,128)(2,1)}), bf16[32,64,576]{2,1,0:T(8,128)(2,1)}, u32[]{:S(2)}, u32[]{:S(2)}) async-start(bf16[32,64,576]{2,1,0:T(8,128)(2,1)} %copy-done.3), calls=%async_computation.8 | async-start | bytes 5242880 | tf_op jit(solution)/shard_map/key_grads/all_to_all | solution.py:127
  522.7 31.1 %collective-permute-start.27 = (bf16[256,1024]{1,0:T(8,128)(2,1)}, bf16[256,1024]{1,0:T(8,128)(2,1)S(1)}, u32[]{:S(2)}, u32[]{:S(2)}) collective-permute-start(bf16[256,1024]{1,0:T(8,128)(2,1)} %get-tuple-element.161), channel_id=1, source_target_pairs={{0,1},{1,0},{2,3},{3,2},{4,5},{5,4},{6,7},{7,6},{8,9},{9,8},{10,11... | collective-permute-start | bytes 1572872 | tf_op jit(solution)/shard_map/ppermute | solution.py:87
  523.8 33.4 %collective-permute-start.28 = (bf16[64,2112]{1,0:T(8,128)(2,1)S(1)}, bf16[64,2112]{1,0:T(8,128)(2,1)S(1)}, u32[]{:S(2)}, u32[]{:S(2)}) collective-permute-start(bf16[64,2112]{1,0:T(8,128)(2,1)S(1)} %dynamic-slice_bitcast_fusion.1), channel_id=1, source_target_pairs={{0,64},{64,0},{1,65},{65,1},{2,66},{66,2},{3,67},{67,3},{4,68},{68... | collective-permute-start | bytes 811016 | tf_op jit(solution)/shard_map/shared_weight_grads/ppermute | solution.py:87
  576.8 37.6 %all-to-all-start.9 = ((bf16[32,32,1024]{2,1,0:T(8,128)(2,1)}), bf16[32,32,1024]{2,1,0:T(8,128)(2,1)}, u32[]{:S(2)}, u32[]{:S(2)}) async-start(bf16[32,32,1024]{2,1,0:T(8,128)(2,1)} %copy-done.4), calls=%async_computation.10 | async-start | bytes 4194304 | tf_op jit(solution)/shard_map/outputs_back/all_to_all | solution.py:127
  597.1 21.2 %collective-permute-start.33 = (bf16[256,512]{1,0:T(8,128)(2,1)}, bf16[256,512]{1,0:T(8,128)(2,1)}, u32[]{:S(2)}, u32[]{:S(2)}) collective-permute-start(bf16[256,512]{1,0:T(8,128)(2,1)} %dynamic-slice_convert_fusion), channel_id=1, source_target_pairs={{0,2},{2,0},{1,3},{3,1},{4,6},{6,4},{5,7},{7,5},{8,10},{10,8},{9,1... | collective-permute-start | bytes 786440 | tf_op jit(solution)/shard_map/ppermute | solution.py:87
  617.7 28.3 %collective-permute-start.31 = (bf16[256,512]{1,0:T(8,128)(2,1)}, bf16[256,512]{1,0:T(8,128)(2,1)S(1)}, u32[]{:S(2)}, u32[]{:S(2)}) collective-permute-start(bf16[256,512]{1,0:T(8,128)(2,1)} %dynamic-slice_convert_fusion.1), channel_id=1, source_target_pairs={{0,2},{2,0},{1,3},{3,1},{4,6},{6,4},{5,7},{7,5},{8,10},{10,8},{9,1... | collective-permute-start | bytes 786440 | tf_op jit(solution)/shard_map/ppermute | solution.py:87
  620.5 30.7 %all-to-all-start.10 = ((bf16[32,32,512]{2,1,0:T(8,128)(2,1)}), bf16[32,32,512]{2,1,0:T(8,128)(2,1)}, u32[]{:S(2)}, u32[]{:S(2)}) async-start(bf16[32,32,512]{2,1,0:T(8,128)(2,1)} %copy-done.26), calls=%async_computation.11 | async-start | bytes 2097152 | tf_op jit(solution)/shard_map/small_weight_grads/all_to_all | solution.py:127
  642.8 7.7 %collective-permute-start.34 = (bf16[64,1536]{1,0:T(8,128)(2,1)S(1)}, bf16[64,1536]{1,0:T(8,128)(2,1)S(1)}, u32[]{:S(2)}, u32[]{:S(2)}) collective-permute-start(bf16[64,1536]{1,0:T(8,128)(2,1)S(1)} %dynamic-slice_bitcast_fusion.2), channel_id=1, source_target_pairs={{0,64},{64,0},{1,65},{65,1},{2,66},{66,2},{3,67},{67,3},{4,68},{68... | collective-permute-start | bytes 589832 | tf_op jit(solution)/shard_map/attn_weight_grads/ppermute | solution.py:87
  (102 other events, 1024.9 us)
Sparse Core Ops, SparseCore 0:
  11.7 136.8 all-gather.4
  154.7 119.1 all-gather.6
  410.3 102.2 reduce-scatter.2
  516.2 125.5 reduce-scatter.4

commit v4 on v3

--- a/solution.py
+++ b/solution.py
@@ -30,6 +30,7 @@
 EPSILON = 1e-06
 ROPE_BASE = 10000.0
 SCALE = (NOPE + ROPE) ** (-0.5)
+SCALE_TWO = SCALE * 1.4426950408889634
 CTX = ("zh", "y", "x")
 MIB = 1 << 20
 
@@ -226,6 +227,16 @@
         sent_ref[:, e] = nn(hot, grad).astype(bf16).reshape(N_CTX, SLOTS, HALF)
 
 
+def router_kernel(core_ref, own_ref, zl_ref, core_two_ref, router_ref):
+    core, zl = core_ref[0], core_ref[1]
+    for e in range(EXP_DEV):
+        rows = slice(e * N_CTX, (e + 1) * N_CTX)
+        router_ref[rows, quarter_at(zl, core)] = own_ref[:, e, :]
+        router_ref[rows, quarter_at(1 - zl, core)] = zl_ref[:, e, :]
+        router_ref[rows, quarter_at(zl, 1 - core)] = core_two_ref[:, e, :]
+        router_ref[rows, quarter_at(1 - zl, 1 - core)] = core_two_ref[:, 2 + e, :]
+
+
 def middle_kernel(
     core_ref, own_ref, other_ref, input_ref, gain_ref, router_ref, slot_ref,
     normed_ref, root_ref, probs_ref, sent_one_ref, sent_two_ref,
@@ -333,7 +344,7 @@
             out((16, 2, 64, 3 * FF_SH), bf16),
         ],
         scratch_shapes=[pltpu.VMEM((TOK, 2 * FF_SH), f32), pltpu.VMEM((TOK, FF_SH), f32)],
-        compiler_params=pltpu.CompilerParams(vmem_limit_bytes=56 * MIB),
+        compiler_params=pltpu.CompilerParams(vmem_limit_bytes=40 * MIB),
         cost_estimate=pl.CostEstimate(
             flops=18 * TOK * WIDTH * FF_SH, bytes_accessed=24 * MIB, transcendentals=0
         ),
@@ -344,7 +355,7 @@
 
 def expert_kernel(
     core_ref, own_ref, other_ref, grad_own_ref, grad_other_ref, wg_ref, wu_ref, wd_ref,
-    back_own_ref, back_send_ref, y_own_ref, y_send_ref, dot_ref, scaled_ref, dg_ref, du_ref,
+    back_own_ref, back_send_ref, y_own_ref, y_send_ref, scaled_ref, dg_ref, du_ref,
 ):
     core = core_ref[0]
     groups = own_ref.shape[0]
@@ -367,7 +378,7 @@
     hidden = (act * up).astype(bf16)
     weight = column_of(own_ref[:, CAP, :], core_ref[1])
     scaled_ref[...] = (hidden.astype(f32) * weight).astype(bf16)
-    dot_ref[...] = nt(jnp.ones((8, 352), bf16), (hidden.astype(f32) * plain).astype(bf16))
+    dots = nt(jnp.ones((8, 352), bf16), (hidden.astype(f32) * plain).astype(bf16))[:1]
     back = plain * weight
     dg = (back * up * (sigmoid * (1.0 + gate * (1.0 - sigmoid)))).astype(bf16)
     du = (back * act).astype(bf16)
@@ -383,6 +394,9 @@
             back_ref[:, :, mine] = part.astype(bf16).reshape(groups, SLOTS, QUARTER)
             part = nn(hidden, wd_ref[0, :, place])
             y_ref[:, :, mine] = part.astype(bf16).reshape(groups, SLOTS, QUARTER)
+    lanes = pl.ds(pl.multiple_of(pl.program_id(0) * rows, rows), rows)
+    for back_ref in (back_own_ref, back_send_ref):
+        back_ref[:, CAP, lanes] = jnp.broadcast_to(dots.astype(bf16), (groups, rows))
 
 
 def expert(e, core, own, other, grad_own, grad_other, wg, wu, wd):
@@ -396,22 +410,14 @@
         grid=(total // step,),
         in_specs=[pl.BlockSpec(memory_space=pltpu.SMEM), rows, rows, grads, grads]
         + [weight] * 3,
-        out_specs=[rows] * 4 + [pl.BlockSpec((8, step), lambda i: (0, i))] + [units] * 3,
-        out_shape=[out((N_CTX, SLOTS, HALF), bf16)] * 4
-        + [out((8, total), f32)] + [out((total, 352), bf16)] * 3,
+        out_specs=[rows] * 4 + [units] * 3,
+        out_shape=[out((N_CTX, SLOTS, HALF), bf16)] * 4 + [out((total, 352), bf16)] * 3,
         compiler_params=pltpu.CompilerParams(vmem_limit_bytes=56 * MIB),
         cost_estimate=pl.CostEstimate(
             flops=12 * total * WIDTH * 352, bytes_accessed=24 * MIB, transcendentals=0
         ),
         name="expert",
     )(core, own, other, grad_own, grad_other, wg, wu, wd)
-
-
-def finish_rows_kernel(core_ref, own_ref, arrived_ref, dot_ref, dot_arrived_ref, sent_ref):
-    slot_row = lax.broadcasted_iota(jnp.int32, own_ref.shape, 1)
-    rows = own_ref[...].astype(f32) + arrived_ref[...].astype(f32)
-    dots = (dot_ref[:1] + dot_arrived_ref[:1]).reshape(1, 1, HALF)
-    sent_ref[...] = jnp.where(slot_row == CAP, dots, rows).astype(bf16)
 
 
 def add_kernel(core_ref, own_ref, arrived_ref, sum_ref):
@@ -587,11 +593,11 @@
 
 
 def weight_rows(attn_ref, z, group, first, last):
-    return attn_ref[z, group * 4 : group * 4 + 4, :, first:last].reshape(256, last - first)
+    return attn_ref[group * 4 : group * 4 + 4, z, :, first:last].reshape(256, last - first)
 
 
 def up_rows(attn_ref, z, head, first):
-    rows = attn_ref[z, :, head * 16 : head * 16 + 16, first : first + 128]
+    rows = attn_ref[:, z, head * 16 : head * 16 + 16, first : first + 128]
     return rows.reshape(256, 128)
 
 
@@ -632,28 +638,35 @@
         sum_ref[...] = jnp.zeros(sum_ref.shape, f32)
         acc_ref[...] = jnp.zeros(acc_ref.shape, f32)
 
-    @pl.when(chunk * (CHUNK // BLOCK) <= place)
-    def _():
-        q = q_ref[...].reshape(HEADS * BLOCK, KEYS)
+    def visit(masked):
         k = k_ref[pl.ds(chunk * CHUNK, CHUNK), :]
-        scores = nt(q, k) * SCALE
-        column = lax.broadcasted_iota(jnp.int32, scores.shape, 1) + chunk * CHUNK
-        scores = jnp.where(column < (place + 1) * BLOCK, scores, -1e30)
-        top_old = top_ref[...][:, :1]
-        top = jnp.maximum(top_old, jnp.max(scores, axis=1, keepdims=True))
-        weights = jnp.exp(scores - top)
-        fade = jnp.exp(top_old - top)
-        total = sum_ref[...][:, :1] * fade + jnp.sum(weights, axis=1, keepdims=True)
-        acc_ref[...] = acc_ref[...] * fade + nn(weights.astype(bf16), k[:, :RANK])
-        top_ref[...] = jnp.broadcast_to(top, top_ref.shape)
-        sum_ref[...] = jnp.broadcast_to(total, sum_ref.shape)
+        for group in range(2):
+            part = slice(group * 256, (group + 1) * 256)
+            q = q_ref[2 * group : 2 * group + 2].reshape(256, KEYS)
+            scores = nt(q, k) * SCALE_TWO
+            if masked:
+                column = lax.broadcasted_iota(jnp.int32, scores.shape, 1) + chunk * CHUNK
+                scores = jnp.where(column < (place + 1) * BLOCK, scores, -1e30)
+            top_old = top_ref[part, :1]
+            top = jnp.maximum(top_old, jnp.max(scores, axis=1, keepdims=True))
+            weights = jnp.exp2(scores - top)
+            fade = jnp.exp2(top_old - top)
+            total = sum_ref[part, :1] * fade + jnp.sum(weights, axis=1, keepdims=True)
+            acc_ref[part] = acc_ref[part] * fade + nn(weights.astype(bf16), k[:, :RANK])
+            top_ref[part] = jnp.broadcast_to(top, (256, 128))
+            sum_ref[part] = jnp.broadcast_to(total, (256, 128))
+
+    first = chunk * (CHUNK // BLOCK)
+    whole = place >= first + CHUNK // BLOCK - 1
+    pl.when(whole)(lambda: visit(False))
+    pl.when((place >= first) & jnp.logical_not(whole))(lambda: visit(True))
 
     @pl.when(chunk == pl.num_programs(1) - 1)
     def _():
         total = sum_ref[...][:, :1]
         value = acc_ref[...] / total
         out_ref[...] = value.reshape(out_ref.shape)
-        log_ref[...] = (top_ref[...] + jnp.log(sum_ref[...])).reshape(log_ref.shape)
+        log_ref[...] = (top_ref[...] + jnp.log2(sum_ref[...])).reshape(log_ref.shape)
         value = value.astype(bf16)
         for h in range(HEADS):
             rows = value[h * BLOCK : (h + 1) * BLOCK]
@@ -663,9 +676,9 @@
         flat = flat_ref[...]
         for z in range(2):
             mine = slice(z * QUARTER, (z + 1) * QUARTER)
-            weight = attn_ref[z, pl.ds(core * 8, 8), :, 768:1280].reshape(QUARTER, QUARTER)
+            weight = attn_ref[pl.ds(core * 8, 8), z, :, 768:1280].reshape(QUARTER, QUARTER)
             own_ref[:, mine] = nt(flat, weight)
-            weight = attn_ref[z, pl.ds(8 - core * 8, 8), :, 768:1280].reshape(QUARTER, QUARTER)
+            weight = attn_ref[pl.ds(8 - core * 8, 8), z, :, 768:1280].reshape(QUARTER, QUARTER)
             send_ref[:, mine] = nt(flat, weight).astype(bf16)
 
 
@@ -680,7 +693,7 @@
             in_specs=[
                 pl.BlockSpec((HEADS, 1, BLOCK, KEYS), lambda o, c, p: (0, o, 0, 0)),
                 pl.BlockSpec((SEQ_BLOCKS * BLOCK, KEYS), lambda o, c, p: (0, 0)),
-                pl.BlockSpec((2, 16, 64, 1536), lambda o, c, p: (0, 0, 0, 0)),
+                pl.BlockSpec((16, 2, 64, 1536), lambda o, c, p: (0, 0, 0, 0)),
             ],
             out_specs=[
                 pl.BlockSpec((HEADS, 1, BLOCK, RANK), lambda o, c, p: (0, o, 0, 0)),
@@ -702,7 +715,7 @@
             out((TOK, HALF), f32),
             out((TOK, HALF), bf16),
         ],
-        compiler_params=pltpu.CompilerParams(vmem_limit_bytes=56 * MIB),
+        compiler_params=pltpu.CompilerParams(vmem_limit_bytes=40 * MIB),
         cost_estimate=pl.CostEstimate(
             flops=2 * 2 * rows * 1280 * (KEYS + RANK), bytes_accessed=16 * MIB, transcendentals=0
         ),
@@ -809,21 +822,26 @@
         )
         inner_ref[...] = jnp.broadcast_to(inner, inner_ref.shape)
 
-    @pl.when(chunk * (CHUNK // BLOCK) <= place)
-    def _():
+    def visit(masked):
+        part = pl.ds(chunk * CHUNK, CHUNK)
+        k = k_ref[part, :]
         q = q_ref[...].reshape(rows, KEYS)
         grad = latent_ref[:, tokens, :].reshape(rows, RANK)
-        part = pl.ds(chunk * CHUNK, CHUNK)
-        k = k_ref[part, :]
-        scores = nt(q, k) * SCALE
-        column = lax.broadcasted_iota(jnp.int32, scores.shape, 1) + chunk * CHUNK
-        log_total = log_ref[...].reshape(rows, BLOCK)[:, :1]
-        probs = jnp.where(column < (place + 1) * BLOCK, jnp.exp(scores - log_total), 0.0)
+        scores = nt(q, k) * SCALE_TWO
+        probs = jnp.exp2(scores - log_ref[...].reshape(rows, BLOCK)[:, :1])
+        if masked:
+            column = lax.broadcasted_iota(jnp.int32, scores.shape, 1) + chunk * CHUNK
+            probs = jnp.where(column < (place + 1) * BLOCK, probs, 0.0)
         prob_back = nt(grad, k[:, :RANK])
-        score_grad = (probs * (prob_back - inner_ref[...][:, :1])).astype(bf16)
-        dq_ref[...] += (nn(score_grad, k) * SCALE).reshape(dq_ref.shape)
-        dk_ref[part, :] += tn(score_grad, q) * SCALE
+        score_grad = ((probs * SCALE) * (prob_back - inner_ref[...][:, :1])).astype(bf16)
+        dq_ref[...] += nn(score_grad, k).reshape(dq_ref.shape)
+        dk_ref[part, :] += tn(score_grad, q)
         dk_ref[part, :RANK] += tn(probs.astype(bf16), grad)
+
+    first = chunk * (CHUNK // BLOCK)
+    whole = place >= first + CHUNK // BLOCK - 1
+    pl.when(whole)(lambda: visit(False))
+    pl.when((place >= first) & jnp.logical_not(whole))(lambda: visit(True))
 
     @pl.when((owner == 1) & (chunk == pl.num_programs(1) - 1))
     def _():
@@ -927,13 +945,18 @@
     gain_two = gains_all[..., 20:].reshape(-1)
     router_mine = small_all[:, 18:20]
 
-    shared_pair_mine = gather_two(
-        jnp.concatenate([shared_gate, shared_up, shared_down.T], axis=1), "zh", 0
-    )
     up_mine = latent_up.reshape(16, HEADS, NOPE + VDIM).transpose(1, 0, 2).reshape(64, NOPE + VDIM)
-    with jax.named_scope("attn_weights"):
-        attn_mine = jnp.concatenate([query_weight, output_weight.T, up_mine], axis=1)
-        attn_all = lax.all_gather(attn_mine, CTX, tiled=False).reshape(2, 16, 64, 1536)
+    dense_mine = jnp.concatenate(
+        [query_weight, output_weight.T, up_mine, shared_gate, shared_up, shared_down.T], axis=1
+    )
+    dense_other = after(swap(dense_mine, "zh"), small)
+    first = lax.axis_index("zh") == 0
+    dense_mine = jnp.stack(
+        [jnp.where(first, dense_mine, dense_other), jnp.where(first, dense_other, dense_mine)]
+    )
+    with jax.named_scope("dense_weights"):
+        dense_all = lax.all_gather(dense_mine, ("y", "x"), tiled=False)
+    attn_all, shared_all = dense_all[..., :1536], dense_all[..., 1536:]
 
     core_is = jnp.stack([core, ctx])
     slot_by, grad_sent = call(
@@ -989,19 +1012,25 @@
         ],
         axis=1,
     )
-    latent_ctx = after(share_ctx(after(latent_rows, shared_pair_mine), "latents"), grad_sent)
-    latent_mine = latent_ctx[pairs]
-    latent_zl = swap(latent_mine, "zl")
-    latent_core = swap(jnp.stack([latent_mine, latent_zl]), "core")
-    (keys,) = call(keys_kernel, [out((SEQ_BLOCKS * BLOCK, KEYS), bf16)], "keys", 1)(
-        jnp.concatenate([slot_of, jnp.stack([zl, core])]), latent_mine, latent_zl, latent_core
-    )
-
     frequency = ROPE_BASE ** (-2.0 * jnp.arange(ROPE // 2, dtype=f32) / ROPE)
     angles = positions.astype(f32)[:, None] * frequency[None, :]
     cos = jnp.cos(angles)
     sin = jnp.sin(angles)
     cos, sin = jnp.concatenate([cos, cos], axis=1), jnp.concatenate([-sin, sin], axis=1)
+    key_slots = jnp.concatenate([slot_of, jnp.stack([zl, core])])
+    latent_ctx = after(share_ctx(latent_rows, "latents"), (grad_sent, cos, sin, key_slots))
+    latent_mine = latent_ctx[pairs]
+    latent_zl = swap(latent_mine, "zl")
+    latent_core = swap(jnp.stack([latent_mine, latent_zl]), "core")
+    router_zl = swap(router_mine, "zl")
+    router_core = swap(jnp.concatenate([router_mine, router_zl], axis=1), "core")
+    (router_t,) = call(router_kernel, [out((EXPERTS, WIDTH), bf16)], "router", 1)(
+        jnp.stack([core, zl]), router_mine, router_zl, router_core
+    )
+    (keys,) = call(keys_kernel, [out((SEQ_BLOCKS * BLOCK, KEYS), bf16)], "keys", 1)(
+        key_slots, latent_mine, latent_zl, latent_core
+    )
+
     query, query_nope = call(
         query_kernel,
         [out((HEADS, TOK, KEYS), bf16), out((HEADS, TOK, NOPE), bf16)],
@@ -1009,15 +1038,12 @@
         2 * TOK * 768 * (WIDTH + RANK),
     )(core_is, normed_one, attn_all, cos, sin)
     query = query.reshape(HEADS, 2, BLOCK, KEYS)
-    grad_own = exchange_ctx(grad_sent, "cotangent_rows", latent_core)
+    grad_own = exchange_ctx(grad_sent, "cotangent_rows", (latent_core, router_core))
     grad_other = swap(grad_own, "core")
     places_core = jnp.concatenate([places, core[None]])
-    value, log_total, head_flat, attn_own, attn_send = attend(places_core, query, keys, attn_all)
+    value, log_total, head_flat, attn_own, attn_send = attend(places_core, after(query, router_t), keys, attn_all)
     attn_half = zl_sum(attn_own + swap(attn_send, "core").astype(f32))
     attn_other = swap(attn_half, "core")
-
-    router_t = gather_two(gather_two(after(router_mine, keys), "zl", 0), "core", 1)
-    router_t = router_t.transpose(3, 2, 0, 1, 4).reshape(EXPERTS, WIDTH)
 
     gain_row = gain_two.reshape(1, WIDTH)
     buffer = out((N_CTX, SLOTS, HALF), bf16)
@@ -1037,34 +1063,32 @@
     weights = (expert_gate.transpose(0, 2, 1), expert_up.transpose(0, 2, 1), expert_down)
     one = exchange_ctx(sent_one, "rows_to_experts", grad_own)
     two = exchange_ctx(sent_two, "rows_to_experts", one)
+    shared_own, shared_send, in_own, in_send, shared_grads = shared(
+        core_is, normed_two, grad_out, shared_all
+    )
+    one = after(one, in_own)
     one_other = swap(one, "core")
-    back_own, back_send, y_one, y_one_send, dots, *units_one = expert(
+    back_own, back_send, y_one, y_one_send, *units_one = expert(
         0, core_is, one, one_other, grad_own, grad_other, *weights
     )
-    two = after(two, dots)
+    two = after(two, units_one[0])
     two_other = swap(two, "core")
-    (sent_one,) = call(finish_rows_kernel, [buffer], "finish_rows", 1, limit=20)(
-        core_is, after(back_own, two), swap(back_send, "core"), dots, swap(dots, "core")
+    (sent_one,) = call(add_kernel, [buffer], "finish_rows", 1, limit=20)(
+        core_is, after(back_own, two), swap(back_send, "core")
     )
     back_one = exchange_ctx(sent_one, "row_grads_back", two)
-    back_own, back_send, y_two, y_two_send, dots, *units_two = expert(
+    back_own, back_send, y_two, y_two_send, *units_two = expert(
         1, core_is, two, two_other, grad_own, grad_other, *weights
     )
-    (sent_two,) = call(finish_rows_kernel, [buffer], "finish_rows", 1, limit=20)(
-        core_is, back_own, swap(after(back_send, back_one), "core"), dots,
-        swap(after(dots, back_one), "core"),
+    (sent_two,) = call(add_kernel, [buffer], "finish_rows", 1, limit=20)(
+        core_is, back_own, swap(after(back_send, back_one), "core")
     )
     back_two = exchange_ctx(sent_two, "row_grads_back", back_one)
 
-    with jax.named_scope("shared_weights"):
-        shared_all = lax.all_gather(after(shared_pair_mine, latent_core), ("y", "x"), tiled=False)
-    shared_own, shared_send, in_own, in_send, shared_grads = shared(
-        core_is, after(normed_two, sent_two), grad_out, shared_all
-    )
     (outs_one,) = call(add_kernel, [buffer], "outputs_sum", 1)(
         core_is, after(y_one, sent_two), swap(y_one_send, "core")
     )
-    back_two = after(back_two, (in_own, outs_one))
+    back_two = after(back_two, outs_one)
 
     in_half, prob_grad = call(
         combine_kernel,
@@ -1117,7 +1141,7 @@
         shared_own, swap(shared_send, "core"),
     )
     shared_pair = scatter_yx(
-        after(shared_grads, back_two).reshape(WIDTH, 3 * FF_SH), "shared_weight_grads"
+        after(shared_grads, sent_two).reshape(WIDTH, 3 * FF_SH), "shared_weight_grads"
     )
     attn_pair = scatter_yx(
         after(attn_parts, (shared_pair, keys_sent)).reshape(WIDTH, 1536), "attn_weight_grads"

time: 676 us -> 672 us (level)
  blocking collectives: 48.8 us -> 0 us
  waiting for transfers between devices: 251 us -> 282 us
  local copies, waits for them, and re-layouts: 65.1 us -> 81.5 us
  starting transfers between devices: 89.1 us -> 98.5 us
  Pallas kernels: 172 us -> 164 us
    all_to_all x10 -> x11, waiting for transfers between devices: 109 us -> 160 us  [exchange_ctx(): return lax.all_to_all(value, CTX, 0, 0, tiled=True)]
    all_to_all x1 -> x0, blocking collectives: 48.8 us -> none  [exchange_ctx(): return lax.all_to_all(value, CTX, 0, 0, tiled=True)]
    slice x0 -> x2, local copies, waits for them, and re-layouts: none -> 11.6 us  [on_device(): attn_all, shared_all = (dense_all[..., :1536], dense_all[..., 1536:])]
    ppermute x37 -> x35, waiting for transfers between devices: 117 us -> 107 us  [shift(): lax.ppermute(value, axis, [(i, (i + step) % size) for i in range(size)])]
    all_to_all x10 -> x11, starting transfers between devices: 65.4 us -> 74.6 us  [exchange_ctx(): return lax.all_to_all(value, CTX, 0, 0, tiled=True)]
    reduce_scatter x2, waiting for transfers between devices: 23.9 us -> 15.4 us  [scatter_yx(): pair = lax.psum_scatter(value, ('y', 'x'), scatter_dimension=0, tiled=True)]
    unnamed x166 -> x198, local copies, waits for them, and re-layouts: 39.1 us -> 46.7 us
    pallas_call x16 -> x17, Pallas kernels: 43 us -> 45.4 us  [run(): pl.pallas_call(body, in_specs=[pl.BlockSpec(memory_space=pltpu.SMEM)] + [...]
  transfers between devices with their start and end apart: 51 -> 49, of which waited for: 31 -> 28; matrix products, arithmetic and copies ran while one was open for 7% -> 7% of each run, Pallas kernels for 26% -> 25%
where the time goes in v4:
time: 672 us; the launch traced here: 662 us
  waiting for transfers between devices  282 us (42%)
  Pallas kernels  164 us (24%)
  starting transfers between devices  98.5 us (15%)
  local copies, waits for them, and re-layouts  81.5 us (12%)
  other arithmetic  19.1 us (3%)
  between operations  15.7 us (2%)
    all_to_all x11, waiting for transfers between devices, exchange_ctx(): return lax.all_to_all(value, CTX, 0, 0, tiled=True)  160 us
    ppermute x35, waiting for transfers between devices, shift(): lax.ppermute(value, axis, [(i, (i + step) % size) for i in range(size)])  107 us
    all_to_all x11, starting transfers between devices, exchange_ctx(): return lax.all_to_all(value, CTX, 0, 0, tiled=True)  74.6 us
    unnamed x198, local copies, waits for them, and re-layouts  46.7 us
    pallas_call x17, Pallas kernels, run(): pl.pallas_call(body, in_specs=[pl.BlockSpec(memory_space=pltpu.SMEM)] + [...  45.4 us
    pallas_call x2, Pallas kernels, expert(): pl.pallas_call(expert_kernel, grid=(total // step,), in_specs=[pl.BlockSp...  40.6 us
    pallas_call x1, Pallas kernels, attend_back(): pl.pallas_call(attend_back_kernel, grid_spec=pltpu.PrefetchScalarGridSpec...  26.2 us
    ppermute x35, starting transfers between devices, shift(): lax.ppermute(value, axis, [(i, (i + step) % size) for i in range(size)])  23.5 us
  transfers between devices with their start and end apart: 49, of which 28 were waited for; matrix products, arithmetic and copies ran while one was open for 7% of the time, Pallas kernels for 25%

profile of v4, /device:TPU:0, one launch (start us, length us, event | category | flops | bytes accessed | tf_op | source)
XLA Modules:
  0.0 661.7 jit_solution(17739528211765334345)
XLA Ops:
  16.0 10.3 %collective-permute-done.1 = bf16[2,36]{1,0:T(2,128)(2,1)S(1)} collective-permute-done((bf16[2,36]{1,0:T(2,128)(2,1)S(1)}, bf16[2,36]{1,0:T(2,128)(2,1)S(1)}, u32[]{:S(2)}, u32[]{:S(2)}) %collective-permute-start.1) | collective-permute-done | bytes 176 | tf_op jit(solution)/shard_map/ppermute | solution.py:88
  29.3 8.3 %all-to-all-start = ((bf16[32,24,512]{2,1,0:T(8,128)(2,1)}), bf16[32,24,512]{2,1,0:T(8,128)(2,1)S(1)}, u32[]{:S(2)}, u32[]{:S(2)}) async-start(bf16[32,24,512]{2,1,0:T(8,128)(2,1)} %broadcast_in_dim.37), calls=%async_computation | async-start | bytes 1572864 | tf_op jit(solution)/shard_map/small_weights/all_to_all | solution.py:128
  38.0 22.2 %all-to-all-done = bf16[32,24,512]{2,1,0:T(8,128)(2,1)S(1)} async-done(((bf16[32,24,512]{2,1,0:T(8,128)(2,1)}), bf16[32,24,512]{2,1,0:T(8,128)(2,1)S(1)}, u32[]{:S(2)}, u32[]{:S(2)}) %all-to-all-start) | async-done | bytes 786464 | tf_op jit(solution)/shard_map/small_weights/all_to_all | solution.py:128
  74.7 4.9 all-to-all-start.1
  87.0 56.3 %all-to-all-done.1 = bf16[32,64,576]{2,1,0:T(8,128)(2,1)} async-done(((bf16[32,64,576]{2,1,0:T(8,128)(2,1)}), bf16[32,64,576]{2,1,0:T(8,128)(2,1)}, u32[]{:S(2)}, u32[]{:S(2)}) %all-to-all-start.1) | async-done | bytes 2359328 | tf_op jit(solution)/shard_map/latents/all_to_all | solution.py:128
  147.0 13.9 %collective-permute-done.7.zl_ref = bf16[8,64,576]{2,1,0:T(8,128)(2,1)S(1)} collective-permute-done((bf16[8,64,576]{2,1,0:T(8,128)(2,1)S(1)}, bf16[8,64,576]{2,1,0:T(8,128)(2,1)S(1)}, u32[]{:S(2)}, u32[]{:S(2)}) %collective-permute-start.7) | collective-permute-done | bytes 589856 | tf_op jit(solution)/shard_map/ppermute | solution.py:88
  170.1 5.1 all-to-all-start.2
  191.4 14.2 %attend.1 = (f32[4,2,128,512]{3,2,1,0:T(8,128)S(1)}, f32[4,2,128,128]{3,2,1,0:T(8,128)S(1)}, bf16[256,512]{1,0:T(8,128)(2,1)S(1)}, f32[256,1024]{1,0:T(8,128)S(1)}, bf16[256,1024]{1,0:T(8,128)(2,1)S(1)}) custom-call(s32[3]{0:T(128)S(1)} %pad_add_fusion.place_ref, bf16[4,2,128,576]{3,2,1,0:T(8,128)(2,1)S(1)} %bitcast.124, bf16[2048,576]{1,0:T(8,128)(2,1)S(1)} %copy-done.12, ...), custom_call_target="tpu_custom_call" | custom-call | flops 2852126720 | bytes 16777216 | tf_op jit(solution)/shard_map/attend/pallas_call | solution.py:688
  208.9 29.1 %collective-permute-done.10 = bf16[256,1024]{1,0:T(8,128)(2,1)S(1)} collective-permute-done((bf16[256,1024]{1,0:T(8,128)(2,1)S(1)}, bf16[256,1024]{1,0:T(8,128)(2,1)S(1)}, u32[]{:S(2)}, u32[]{:S(2)}) %collective-permute-start.10) | collective-permute-done | bytes 524320 | tf_op jit(solution)/shard_map/ppermute | solution.py:88
  242.1 5.6 middle.1
  251.2 9.3 %all-to-all-start.3 = ((bf16[32,32,1024]{2,1,0:T(8,128)(2,1)}), bf16[32,32,1024]{2,1,0:T(8,128)(2,1)}, u32[]{:S(2)}, u32[]{:S(2)}) async-start(bf16[32,32,1024]{2,1,0:T(8,128)(2,1)} %copy-done.21), calls=%async_computation.3 | async-start | bytes 4194304 | tf_op jit(solution)/shard_map/rows_to_experts/all_to_all | solution.py:128
  260.6 8.1 %slice.126.weight_ref = bf16[16,2,64,2112]{3,2,1,0:T(8,128)(2,1)} slice(bf16[16,2,64,3648]{3,2,1,0:T(8,128)(2,1)} %bitcast.127), slice={[0:16], [0:2], [0:64], [1536:3648]} | slice | bytes 17301504 | tf_op jit(solution)/shard_map/slice | solution.py:959
  268.7 14.9 %shared_experts.1 = (f32[256,1024]{1,0:T(8,128)S(1)}, bf16[256,1024]{1,0:T(8,128)(2,1)S(1)}, f32[256,1024]{1,0:T(8,128)S(1)}, bf16[256,1024]{1,0:T(8,128)(2,1)S(1)}, bf16[16,2,64,2112]{3,2,1,0:T(8,128)(2,1)S(1)}) custom-call(s32[2]{0:T(128)S(1)} %pad_add_fusion.1.core_ref, bf16[256,2048]{1,0:T(8,128)(2,1)S(1)} %copy-done.32, ...), custom_call_target="tpu_custom_call" | custom-call | flops 6643777536 | bytes 25165824 | tf_op jit(solution)/shard_map/shared_experts/pallas_call | solution.py:353
  290.6 10.1 %all-to-all-start.4 = ((bf16[32,32,1024]{2,1,0:T(8,128)(2,1)}), bf16[32,32,1024]{2,1,0:T(8,128)(2,1)}, u32[]{:S(2)}, u32[]{:S(2)}) async-start(bf16[32,32,1024]{2,1,0:T(8,128)(2,1)} %get-tuple-element.110), calls=%async_computation.4 | async-start | bytes 4194304 | tf_op jit(solution)/shard_map/rows_to_experts/all_to_all | solution.py:128
  302.0 20.2 %expert.2 = (bf16[32,32,1024]{2,1,0:T(8,128)(2,1)}, bf16[32,32,1024]{2,1,0:T(8,128)(2,1)}, bf16[32,32,1024]{2,1,0:T(8,128)(2,1)}, bf16[32,32,1024]{2,1,0:T(8,128...) custom-call(s32[2]{0:T(128)} %copy-done.55, ...), custom_call_target="tpu_custom_call" | custom-call | flops 8858370048 | bytes 25165824 | tf_op jit(solution)/shard_map/expert/pallas_call | solution.py:408
  322.6 8.0 %all-to-all-done.4.own_ref.two_ref = bf16[32,32,1024]{2,1,0:T(8,128)(2,1)} async-done(((bf16[32,32,1024]{2,1,0:T(8,128)(2,1)}), bf16[32,32,1024]{2,1,0:T(8,128)(2,1)}, u32[]{:S(2)}, u32[]{:S(2)}) %all-to-all-start.4) | async-done | bytes 2097184 | tf_op jit(solution)/shard_map/rows_to_experts/all_to_all | solution.py:128
  334.5 5.9 all-to-all-start.5
  340.7 20.4 %expert.3 = (bf16[32,32,1024]{2,1,0:T(8,128)(2,1)}, bf16[32,32,1024]{2,1,0:T(8,128)(2,1)}, bf16[32,32,1024]{2,1,0:T(8,128)(2,1)}, bf16[32,32,1024]{2,1,0:T(8,128...) custom-call(s32[2]{0:T(128)} %copy-done.55, ...), custom_call_target="tpu_custom_call" | custom-call | flops 8858370048 | bytes 25165824 | tf_op jit(solution)/shard_map/expert/pallas_call | solution.py:408
  361.0 9.0 %all-to-all-done.5.one_ref = bf16[32,32,1024]{2,1,0:T(8,128)(2,1)S(1)} async-done(((bf16[32,32,1024]{2,1,0:T(8,128)(2,1)}), bf16[32,32,1024]{2,1,0:T(8,128)(2,1)S(1)}, u32[]{:S(2)}, u32[]{:S(2)}) %all-to-all-start.5) | async-done | bytes 2097184 | tf_op jit(solution)/shard_map/row_grads_back/all_to_all | solution.py:128
  378.6 5.0 all-to-all-start.6
  389.0 35.5 %all-to-all-done.6.two_ref = bf16[32,32,1024]{2,1,0:T(8,128)(2,1)} async-done(((bf16[32,32,1024]{2,1,0:T(8,128)(2,1)}), bf16[32,32,1024]{2,1,0:T(8,128)(2,1)}, u32[]{:S(2)}, u32[]{:S(2)}) %all-to-all-start.6) | async-done | bytes 2097184 | tf_op jit(solution)/shard_map/row_grads_back/all_to_all | solution.py:128
  429.4 13.5 %collective-permute-done.19 = bf16[256,1024]{1,0:T(8,128)(2,1)S(1)} collective-permute-done((bf16[256,1024]{1,0:T(8,128)(2,1)S(1)}, bf16[256,1024]{1,0:T(8,128)(2,1)S(1)}, u32[]{:S(2)}, u32[]{:S(2)}) %collective-permute-start.19) | collective-permute-done | bytes 524320 | tf_op jit(solution)/shard_map/ppermute | solution.py:88
  453.3 26.2 %attend_back.1 = (f32[256,2048]{1,0:T(8,128)}, bf16[256,2048]{1,0:T(8,128)(2,1)}, bf16[64,256]{1,0:T(8,128)(2,1)}, f32[1,2048]{1,0:T(1,128)}, bf16[256,512]{1,0:...) custom-call(s32[3]{0:T(128)} %copy-done.70, ...), custom_call_target="tpu_custom_call" | custom-call | flops 7549747200 | bytes 37748736 | tf_op jit(solution)/shard_map/attend_back/pallas_call | solution.py:879
  479.7 5.7 all-to-all-done.7.back_ref
  488.8 10.2 %query_back.1 = (bf16[16,2,64,1536]{3,2,1,0:T(8,128)(2,1)}, f32[256,2048]{1,0:T(8,128)S(1)}) custom-call(s32[2]{0:T(128)S(1)} %copy-done.57, f32[4,256,576]{2,1,0:T(8,128)} %bitcast.131, bf16[4,256,128]{2,1,0:T(8,128)(2,1)S(1)} %copy-done.43, bf16[256,2048]{1,0:T(8,128)(2,1)S(1)} %fusion.2.normed_ref, bf16[16,2,64,1536]{3,2,1,0:T(8,128)(2,1)} %copy-done, ...), custom_call_target="tpu_custom_call" | custom-call | flops 2550136832 | bytes 22151168 | tf_op jit(solution)/shard_map/query_back/pallas_call | solution.py:175
  507.4 10.0 %all-to-all-start.8 = ((bf16[32,64,576]{2,1,0:T(8,128)(2,1)}), bf16[32,64,576]{2,1,0:T(8,128)(2,1)}, u32[]{:S(2)}, u32[]{:S(2)}) async-start(bf16[32,64,576]{2,1,0:T(8,128)(2,1)} %copy-done.3), calls=%async_computation.8 | async-start | bytes 5242880 | tf_op jit(solution)/shard_map/key_grads/all_to_all | solution.py:128
  522.3 22.9 %expert_grads.1 = (f32[2,352,2048]{2,1,0:T(8,128)}, f32[2,352,2048]{2,1,0:T(8,128)}, f32[2,352,2048]{2,1,0:T(8,128)}) custom-call(s32[2]{0:T(128)} %copy-done.55, bf16[32,32,1024]{2,1,0:T(8,128)(2,1)} %all-to-all-done.3.own_ref.one_ref, bf16[32,32,1024]{2,1,0:T(8,128)(2,1)} %copy-done.96, bf16[32,32,1024]{2,1,0:T(8,128)(2,1)} %all-to-all-done.4.own_ref.two_ref, ...), custom_call_target="tpu_custom_call" | custom-call | flops 8858370048 | bytes 37748736 | tf_op jit(solution)/shard_map/expert_grads/pallas_call | solution.py:553
  553.4 7.8 %all-to-all-done.8.back_ref = bf16[32,64,576]{2,1,0:T(8,128)(2,1)} async-done(((bf16[32,64,576]{2,1,0:T(8,128)(2,1)}), bf16[32,64,576]{2,1,0:T(8,128)(2,1)}, u32[]{:S(2)}, u32[]{:S(2)}) %all-to-all-start.8) | async-done | bytes 2359328 | tf_op jit(solution)/shard_map/key_grads/all_to_all | solution.py:128
  564.9 6.2 collective-permute-done.28
  593.8 15.1 %all-to-all-done.9.back_ref = bf16[32,32,1024]{2,1,0:T(8,128)(2,1)} async-done(((bf16[32,32,1024]{2,1,0:T(8,128)(2,1)}), bf16[32,32,1024]{2,1,0:T(8,128)(2,1)}, u32[]{:S(2)}, u32[]{:S(2)}) %all-to-all-start.9) | async-done | bytes 2097184 | tf_op jit(solution)/shard_map/outputs_back/all_to_all | solution.py:128
  615.5 6.3 all-to-all-start.10
  621.8 15.4 %reduce-scatter.5.cloned.1.call-done = bf16[128,1536]{1,0:T(8,128)(2,1)} async-done(((bf16[2048,1536]{1,0:T(8,128)(2,1)}), bf16[128,1536]{1,0:T(8,128)(2,1)}) %reduce-scatter.5.cloned.1.call-update) | async-done | bytes 393232 | tf_op jit(solution)/shard_map/attn_weight_grads/reduce_scatter | solution.py:109
  (404 shorter events, 190.2 us)
Async XLA Ops:
  7.2 177.0 %all-gather.3.cloned.1.call-start = ((), (), s32[]{:S(2)}) async-start(), calls=%async_computation.15 | async-start | bytes 16154624 | tf_op jit(solution)/shard_map/dense_weights/all_gather | solution.py:958
  10.0 17.2 %collective-permute-start.2 = (bf16[64,3648]{1,0:T(8,128)(2,1)S(1)}, bf16[64,3648]{1,0:T(8,128)(2,1)S(1)}, u32[]{:S(2)}, u32[]{:S(2)}) collective-permute-start(bf16[64,3648]{1,0:T(8,128)(2,1)S(1)} %concatenate.39), channel_id=1, source_target_pairs={{0,64},{64,0},{1,65},{65,1},{2,66},{66,2},{3,67},{67,3},{4,68},{68... | collective-permute-start | bytes 1400840 | tf_op jit(solution)/shard_map/ppermute | solution.py:88
  14.8 11.5 %collective-permute-start.1 = (bf16[2,36]{1,0:T(2,128)(2,1)S(1)}, bf16[2,36]{1,0:T(2,128)(2,1)S(1)}, u32[]{:S(2)}, u32[]{:S(2)}) collective-permute-start(bf16[2,36]{1,0:T(2,128)(2,1)S(1)} %pad_maximum_fusion.10), channel_id=1, source_target_pairs={{0,2},{2,0},{1,3},{3,1},{4,6},{6,4},{5,7},{7,5},{8,10},{10,8},{9,1... | collective-permute-start | bytes 440 | tf_op jit(solution)/shard_map/ppermute | solution.py:88
  29.3 30.9 %all-to-all-start = ((bf16[32,24,512]{2,1,0:T(8,128)(2,1)}), bf16[32,24,512]{2,1,0:T(8,128)(2,1)S(1)}, u32[]{:S(2)}, u32[]{:S(2)}) async-start(bf16[32,24,512]{2,1,0:T(8,128)(2,1)} %broadcast_in_dim.37), calls=%async_computation | async-start | bytes 1572864 | tf_op jit(solution)/shard_map/small_weights/all_to_all | solution.py:128
  74.7 68.6 %all-to-all-start.1 = ((bf16[32,64,576]{2,1,0:T(8,128)(2,1)}), bf16[32,64,576]{2,1,0:T(8,128)(2,1)}, u32[]{:S(2)}, u32[]{:S(2)}) async-start(bf16[32,64,576]{2,1,0:T(8,128)(2,1)} %broadcast_in_dim.42), calls=%async_computation.1 | async-start | bytes 5242880 | tf_op jit(solution)/shard_map/latents/all_to_all | solution.py:128
  145.6 15.3 %collective-permute-start.7 = (bf16[8,64,576]{2,1,0:T(8,128)(2,1)S(1)}, bf16[8,64,576]{2,1,0:T(8,128)(2,1)S(1)}, u32[]{:S(2)}, u32[]{:S(2)}) collective-permute-start(bf16[8,64,576]{2,1,0:T(8,128)(2,1)S(1)} %gather_fusion.1), channel_id=1, source_target_pairs={{0,2},{2,0},{1,3},{3,1},{4,6},{6,4},{5,7},{7,5},{8,10},{10,8},{9,1... | collective-permute-start | bytes 1769480 | tf_op jit(solution)/shard_map/ppermute | solution.py:88
  161.1 7.9 %collective-permute-start.8 = (bf16[2,8,64,576]{3,2,1,0:T(8,128)(2,1)S(1)}, bf16[2,8,64,576]{3,2,1,0:T(8,128)(2,1)S(1)}, u32[]{:S(2)}, u32[]{:S(2)}) collective-permute-start(bf16[2,8,64,576]{3,2,1,0:T(8,128)(2,1)S(1)} %pad_maximum_fusion), channel_id=1, source_target_pairs={{0,1},{1,0},{2,3},{3,2},{4,5},{5,4},{6,7},{7,6},{8,9},{9,8},{10,11... | collective-permute-start | bytes 3538952 | tf_op jit(solution)/shard_map/ppermute | solution.py:88
  170.1 68.4 %all-to-all-start.2 = ((bf16[32,2,32,1024]{3,2,1,0:T(8,128)(2,1)}), bf16[32,2,32,1024]{3,2,1,0:T(8,128)(2,1)}, u32[]{:S(2)}, u32[]{:S(2)}) async-start(bf16[32,2,32,1024]{3,2,1,0:T(8,128)(2,1)} %copy-done.10), calls=%async_computation.2 | async-start | bytes 8388608 | tf_op jit(solution)/shard_map/cotangent_rows/all_to_all | solution.py:128
  207.8 30.3 %collective-permute-start.10 = (bf16[256,1024]{1,0:T(8,128)(2,1)S(1)}, bf16[256,1024]{1,0:T(8,128)(2,1)S(1)}, u32[]{:S(2)}, u32[]{:S(2)}) collective-permute-start(bf16[256,1024]{1,0:T(8,128)(2,1)S(1)} %add_convert_fusion), channel_id=1, source_target_pairs={{0,2},{2,0},{1,3},{3,1},{4,6},{6,4},{5,7},{7,5},{8,10},{10,8},{9,1... | collective-permute-start | bytes 1572872 | tf_op jit(solution)/shard_map/ppermute | solution.py:88
  238.5 62.2 %collective-permute-start.13 = (bf16[32,2,32,1024]{3,2,1,0:T(8,128)(2,1)}, bf16[32,2,32,1024]{3,2,1,0:T(8,128)(2,1)}, u32[]{:S(2)}, u32[]{:S(2)}) collective-permute-start(bf16[32,2,32,1024]{3,2,1,0:T(8,128)(2,1)} %all-to-all-done.2.grad_own_ref.ga_ref), channel_id=1, source_target_pairs={{0,1},{1,0},{2,3},{3,2},{4,5},{5,4},{6,7},{7,6},{8,9},{9,8},{10,11... | collective-permute-start | bytes 12582920 | tf_op jit(solution)/shard_map/ppermute | solution.py:88
  251.2 39.4 %all-to-all-start.3 = ((bf16[32,32,1024]{2,1,0:T(8,128)(2,1)}), bf16[32,32,1024]{2,1,0:T(8,128)(2,1)}, u32[]{:S(2)}, u32[]{:S(2)}) async-start(bf16[32,32,1024]{2,1,0:T(8,128)(2,1)} %copy-done.21), calls=%async_computation.3 | async-start | bytes 4194304 | tf_op jit(solution)/shard_map/rows_to_experts/all_to_all | solution.py:128
  290.6 10.1 %collective-permute-start.12 = (bf16[32,32,1024]{2,1,0:T(8,128)(2,1)}, bf16[32,32,1024]{2,1,0:T(8,128)(2,1)S(1)}, u32[]{:S(2)}, u32[]{:S(2)}) collective-permute-start(bf16[32,32,1024]{2,1,0:T(8,128)(2,1)} %all-to-all-done.3.own_ref.one_ref), channel_id=1, source_target_pairs={{0,1},{1,0},{2,3},{3,2},{4,5},{5,4},{6,7},{7,6},{8,9},{9,8},{10,11... | collective-permute-start | bytes 6291464 | tf_op jit(solution)/shard_map/ppermute | solution.py:88
  290.6 40.0 %all-to-all-start.4 = ((bf16[32,32,1024]{2,1,0:T(8,128)(2,1)}), bf16[32,32,1024]{2,1,0:T(8,128)(2,1)}, u32[]{:S(2)}, u32[]{:S(2)}) async-start(bf16[32,32,1024]{2,1,0:T(8,128)(2,1)} %get-tuple-element.110), calls=%async_computation.4 | async-start | bytes 4194304 | tf_op jit(solution)/shard_map/rows_to_experts/all_to_all | solution.py:128
  322.3 8.3 %collective-permute-start.15 = (bf16[32,32,1024]{2,1,0:T(8,128)(2,1)}, bf16[32,32,1024]{2,1,0:T(8,128)(2,1)S(1)}, u32[]{:S(2)}, u32[]{:S(2)}) collective-permute-start(bf16[32,32,1024]{2,1,0:T(8,128)(2,1)} %get-tuple-element.119), channel_id=1, source_target_pairs={{0,1},{1,0},{2,3},{3,2},{4,5},{5,4},{6,7},{7,6},{8,9},{9,8},{10,11... | collective-permute-start | bytes 6291464 | tf_op jit(solution)/shard_map/ppermute | solution.py:88
  330.6 10.1 %collective-permute-start.14 = (bf16[32,32,1024]{2,1,0:T(8,128)(2,1)}, bf16[32,32,1024]{2,1,0:T(8,128)(2,1)}, u32[]{:S(2)}, u32[]{:S(2)}) collective-permute-start(bf16[32,32,1024]{2,1,0:T(8,128)(2,1)} %all-to-all-done.4.own_ref.two_ref), channel_id=1, source_target_pairs={{0,1},{1,0},{2,3},{3,2},{4,5},{5,4},{6,7},{7,6},{8,9},{9,8},{10,11... | collective-permute-start | bytes 6291464 | tf_op jit(solution)/shard_map/ppermute | solution.py:88
  334.5 35.5 %all-to-all-start.5 = ((bf16[32,32,1024]{2,1,0:T(8,128)(2,1)}), bf16[32,32,1024]{2,1,0:T(8,128)(2,1)S(1)}, u32[]{:S(2)}, u32[]{:S(2)}) async-start(bf16[32,32,1024]{2,1,0:T(8,128)(2,1)} %copy-done.7), calls=%async_computation.5 | async-start | bytes 4194304 | tf_op jit(solution)/shard_map/row_grads_back/all_to_all | solution.py:128
  340.4 165.1 %reduce-scatter.3.cloned.1.call-start = ((), (), s32[]{:S(2)}) async-start(), calls=%async_computation.13 | async-start | bytes 9469952 | tf_op jit(solution)/shard_map/shared_weight_grads/reduce_scatter | solution.py:109
  378.6 45.9 %all-to-all-start.6 = ((bf16[32,32,1024]{2,1,0:T(8,128)(2,1)}), bf16[32,32,1024]{2,1,0:T(8,128)(2,1)}, u32[]{:S(2)}, u32[]{:S(2)}) async-start(bf16[32,32,1024]{2,1,0:T(8,128)(2,1)} %copy-done.6), calls=%async_computation.6 | async-start | bytes 4194304 | tf_op jit(solution)/shard_map/row_grads_back/all_to_all | solution.py:128
  383.6 40.8 %collective-permute-start.18 = (bf16[256,1024]{1,0:T(8,128)(2,1)}, bf16[256,1024]{1,0:T(8,128)(2,1)}, u32[]{:S(2)}, u32[]{:S(2)}) collective-permute-start(bf16[256,1024]{1,0:T(8,128)(2,1)} %copy-done.69), channel_id=1, source_target_pairs={{0,1},{1,0},{2,3},{3,2},{4,5},{5,4},{6,7},{7,6},{8,9},{9,8},{10,11... | collective-permute-start | bytes 1572872 | tf_op jit(solution)/shard_map/ppermute | solution.py:88
  429.2 13.7 %collective-permute-start.19 = (bf16[256,1024]{1,0:T(8,128)(2,1)S(1)}, bf16[256,1024]{1,0:T(8,128)(2,1)S(1)}, u32[]{:S(2)}, u32[]{:S(2)}) collective-permute-start(bf16[256,1024]{1,0:T(8,128)(2,1)S(1)} %get-tuple-element.130), channel_id=1, source_target_pairs={{0,2},{2,0},{1,3},{3,1},{4,6},{6,4},{5,7},{7,5},{8,10},{10,8},{9,1... | collective-permute-start | bytes 1572872 | tf_op jit(solution)/shard_map/ppermute | solution.py:88
  448.4 37.0 %all-to-all-start.7 = ((bf16[32,32,1024]{2,1,0:T(8,128)(2,1)}), bf16[32,32,1024]{2,1,0:T(8,128)(2,1)S(1)}, u32[]{:S(2)}, u32[]{:S(2)}) async-start(bf16[32,32,1024]{2,1,0:T(8,128)(2,1)} %outputs_sum.2), calls=%async_computation.7 | async-start | bytes 4194304 | tf_op jit(solution)/shard_map/outputs_back/all_to_all | solution.py:128
  453.0 184.2 %reduce-scatter.5.cloned.1.call-start = ((), (), s32[]{:S(2)}) async-start(), calls=%async_computation.14 | async-start | bytes 6684672 | tf_op jit(solution)/shard_map/attn_weight_grads/reduce_scatter | solution.py:109
  488.7 14.4 %collective-permute-start.23 = (bf16[8,64,576]{2,1,0:T(8,128)(2,1)S(1)}, bf16[8,64,576]{2,1,0:T(8,128)(2,1)S(1)}, u32[]{:S(2)}, u32[]{:S(2)}) collective-permute-start(bf16[8,64,576]{2,1,0:T(8,128)(2,1)S(1)} %get-tuple-element.141), channel_id=1, source_target_pairs={{0,2},{2,0},{1,3},{3,1},{4,6},{6,4},{5,7},{7,5},{8,10},{10,8},{9,1... | collective-permute-start | bytes 1769480 | tf_op jit(solution)/shard_map/ppermute | solution.py:88
  505.5 39.8 %collective-permute-start.24 = (bf16[32,32,1024]{2,1,0:T(8,128)(2,1)}, bf16[32,32,1024]{2,1,0:T(8,128)(2,1)}, u32[]{:S(2)}, u32[]{:S(2)}) collective-permute-start(bf16[32,32,1024]{2,1,0:T(8,128)(2,1)} %get-tuple-element.151), channel_id=1, source_target_pairs={{0,1},{1,0},{2,3},{3,2},{4,5},{5,4},{6,7},{7,6},{8,9},{9,8},{10,11... | collective-permute-start | bytes 6291464 | tf_op jit(solution)/shard_map/ppermute | solution.py:88
  507.4 53.7 %all-to-all-start.8 = ((bf16[32,64,576]{2,1,0:T(8,128)(2,1)}), bf16[32,64,576]{2,1,0:T(8,128)(2,1)}, u32[]{:S(2)}, u32[]{:S(2)}) async-start(bf16[32,64,576]{2,1,0:T(8,128)(2,1)} %copy-done.3), calls=%async_computation.8 | async-start | bytes 5242880 | tf_op jit(solution)/shard_map/key_grads/all_to_all | solution.py:128
  517.7 31.1 %collective-permute-start.25 = (bf16[256,1024]{1,0:T(8,128)(2,1)}, bf16[256,1024]{1,0:T(8,128)(2,1)S(1)}, u32[]{:S(2)}, u32[]{:S(2)}) collective-permute-start(bf16[256,1024]{1,0:T(8,128)(2,1)} %copy-done.68), channel_id=1, source_target_pairs={{0,1},{1,0},{2,3},{3,2},{4,5},{5,4},{6,7},{7,6},{8,9},{9,8},{10,11... | collective-permute-start | bytes 1572872 | tf_op jit(solution)/shard_map/ppermute | solution.py:88
  518.8 33.6 %collective-permute-start.26 = (bf16[64,2112]{1,0:T(8,128)(2,1)S(1)}, bf16[64,2112]{1,0:T(8,128)(2,1)S(1)}, u32[]{:S(2)}, u32[]{:S(2)}) collective-permute-start(bf16[64,2112]{1,0:T(8,128)(2,1)S(1)} %dynamic-slice_bitcast_fusion.1), channel_id=1, source_target_pairs={{0,64},{64,0},{1,65},{65,1},{2,66},{66,2},{3,67},{67,3},{4,68},{68... | collective-permute-start | bytes 811016 | tf_op jit(solution)/shard_map/shared_weight_grads/ppermute | solution.py:88
  571.3 37.6 %all-to-all-start.9 = ((bf16[32,32,1024]{2,1,0:T(8,128)(2,1)}), bf16[32,32,1024]{2,1,0:T(8,128)(2,1)}, u32[]{:S(2)}, u32[]{:S(2)}) async-start(bf16[32,32,1024]{2,1,0:T(8,128)(2,1)} %copy-done.5), calls=%async_computation.10 | async-start | bytes 4194304 | tf_op jit(solution)/shard_map/outputs_back/all_to_all | solution.py:128
  591.6 21.8 %collective-permute-start.31 = (bf16[256,512]{1,0:T(8,128)(2,1)}, bf16[256,512]{1,0:T(8,128)(2,1)}, u32[]{:S(2)}, u32[]{:S(2)}) collective-permute-start(bf16[256,512]{1,0:T(8,128)(2,1)} %dynamic-slice_convert_fusion), channel_id=1, source_target_pairs={{0,2},{2,0},{1,3},{3,1},{4,6},{6,4},{5,7},{7,5},{8,10},{10,8},{9,1... | collective-permute-start | bytes 786440 | tf_op jit(solution)/shard_map/ppermute | solution.py:88
  612.1 29.4 %collective-permute-start.29 = (bf16[256,512]{1,0:T(8,128)(2,1)}, bf16[256,512]{1,0:T(8,128)(2,1)S(1)}, u32[]{:S(2)}, u32[]{:S(2)}) collective-permute-start(bf16[256,512]{1,0:T(8,128)(2,1)} %dynamic-slice_convert_fusion.1), channel_id=1, source_target_pairs={{0,2},{2,0},{1,3},{3,1},{4,6},{6,4},{5,7},{7,5},{8,10},{10,8},{9,1... | collective-permute-start | bytes 786440 | tf_op jit(solution)/shard_map/ppermute | solution.py:88
  615.5 30.7 %all-to-all-start.10 = ((bf16[32,32,512]{2,1,0:T(8,128)(2,1)}), bf16[32,32,512]{2,1,0:T(8,128)(2,1)}, u32[]{:S(2)}, u32[]{:S(2)}) async-start(bf16[32,32,512]{2,1,0:T(8,128)(2,1)} %copy-done.29), calls=%async_computation.11 | async-start | bytes 2097152 | tf_op jit(solution)/shard_map/small_weight_grads/all_to_all | solution.py:128
  638.3 7.3 %collective-permute-start.32 = (bf16[64,1536]{1,0:T(8,128)(2,1)S(1)}, bf16[64,1536]{1,0:T(8,128)(2,1)S(1)}, u32[]{:S(2)}, u32[]{:S(2)}) collective-permute-start(bf16[64,1536]{1,0:T(8,128)(2,1)S(1)} %dynamic-slice_bitcast_fusion.2), channel_id=1, source_target_pairs={{0,64},{64,0},{1,65},{65,1},{2,66},{66,2},{3,67},{67,3},{4,68},{68... | collective-permute-start | bytes 589832 | tf_op jit(solution)/shard_map/attn_weight_grads/ppermute | solution.py:88
  (116 other events, 1119.9 us)
Sparse Core Ops, SparseCore 0:
  28.5 136.9 all-gather.2
  378.5 114.0 reduce-scatter.2
  505.7 131.5 reduce-scatter.4
